TPU v7x, 32 devices: a whole 2x2x4 slice. The times are simulated.
32 devices in a mesh: lat: 4 (over x, core), lon: 8 (over z, y).
Axes of the slice: x: 2, y: 2, z: 4, core: 2. Of those that a mesh axis runs over, the one named last changes fastest.
Arguments:
- features: bfloat16 [128, 128, 768], P('lat', 'lon'), may hold values from -6 to 6
- cotangent: bfloat16 [128, 128, 768], P('lat', 'lon'), may hold values from -6 to 6
- weight_first: bfloat16 [2, 8, 96, 96], replicated, may hold values from -1 to 1
- weight_second: bfloat16 [2, 8, 96, 96], replicated, may hold values from -1 to 1
Outputs:
- mixed_field: bfloat16 [128, 128, 768], P('lat', 'lon')
- feature_grad: bfloat16 [128, 128, 768], P('lat', 'lon')
- grad_first: float32 [2, 8, 96, 96], replicated
- grad_second: float32 [2, 8, 96, 96], replicated
All inputs are finite; a program needn't handle non-finite values.
Results may differ from a plain program's by a relative error of at most 0.012.
The roundings to bfloat16 on the way count: a program that leaves them out, or rounds other values in their place, can miss the bound.
Values may be sent and summed in bfloat16 or wider, within the bound.
No kernel may reach another device: no remote copies, remote signals or barrier semaphores. Data moves between devices by JAX's collectives and lax.ppermute only.
A program may use at most 64 MiB of HBM per device.

v0:
```python
import functools
import math

import jax
import jax.numpy as jnp
import ml_dtypes
import numpy as np
from jax import lax
from jax.experimental import pallas as pl
from jax.experimental.pallas import tpu as pltpu
from jax.sharding import PartitionSpec as P

NB = 8
BS = 96
KWD = 1
RQ = 4
PACK = RQ * BS
WIDE = 2 * BS
STATE = -(-WIDE // 128) * 128
MIB = 1024 * 1024

shrink_level = 0.01
gelu_coeff = 0.7978845608028654


def wave_table(first, second, length):
    product = (first[:, None] * second[None, :]) % length
    angle = np.float32(2.0 * math.pi / length) * product.astype(np.float32)
    scale = np.float32(math.sqrt(length))
    rounded = ml_dtypes.bfloat16
    cos = (np.cos(angle) / scale).astype(rounded).astype(np.float32)
    sin = (np.sin(angle) / scale).astype(rounded).astype(np.float32)
    return cos, sin


def lon_tables(kept, cols, lon_count, rows):
    cos, sin = wave_table(np.arange(kept), np.arange(cols), cols)
    parts = np.stack([cos, -sin], axis=1).reshape(kept, 2, lon_count, cols // lon_count)
    eye = np.eye(rows, dtype=np.float32)
    forward = np.einsum("kpgw,rs->kprgsw", parts, eye).reshape(2 * kept * rows, -1)
    return forward, forward.T


def lat_table(rows, lat_count, subs, rows_sub, rows_cut, pack_modes):
    cos, sin = wave_table(np.arange(rows), np.arange(rows), rows)
    forward = np.stack([np.stack([cos, sin], axis=1), np.stack([-sin, cos], axis=1)])
    split = forward.reshape(2, rows, 2, lat_count, RQ, subs, rows_sub // rows_cut, rows_cut)
    eye = np.eye(pack_modes, dtype=np.float32)
    return np.einsum("aqplgshr,jk->jaqglskhpr", split, eye).reshape(2 * pack_modes * rows, -1)


def constant(table):
    return jnp.asarray(table.astype(ml_dtypes.bfloat16))


def kernel_call(body, out_shape, scalars, arrays, scratch=(), anchors=(), far=(), limit=8 * MIB):
    specs = {
        space: pl.BlockSpec(memory_space=space)
        for space in (pltpu.VMEM, pltpu.SMEM, pltpu.HBM, pl.ANY)
    }
    far = [pltpu.with_memory_space_constraint(value, pltpu.HBM) for value in far]
    in_specs = [specs[pltpu.SMEM]] * len(scalars) + [specs[pltpu.VMEM]] * len(arrays)
    in_specs += [specs[pltpu.HBM]] * len(far) + [specs[pl.ANY]] * len(anchors)
    is_far = [getattr(shape, "memory_space", None) is pltpu.HBM for shape in out_shape]
    return pl.pallas_call(
        body,
        out_shape=out_shape,
        in_specs=in_specs,
        out_specs=[specs[pltpu.HBM if distant else pltpu.VMEM] for distant in is_far],
        scratch_shapes=list(scratch),
        compiler_params=pltpu.CompilerParams(vmem_limit_bytes=limit),
    )(*[value.reshape(1).astype(jnp.int32) for value in scalars], *arrays, *far, *anchors)


def gate(source, anchors):
    anywhere = pl.BlockSpec(memory_space=pl.ANY)
    return pl.pallas_call(
        lambda *refs: None,
        out_shape=jax.ShapeDtypeStruct(source.shape, source.dtype),
        in_specs=[anywhere] * (1 + len(anchors)),
        out_specs=anywhere,
        input_output_aliases={0: 0},
    )(source, *anchors)


def pack_body(rows_sub, subs, own, source, *rest):
    sent, slots = rest[:-1], rest[-1]
    cols = source.shape[1]
    for sub in range(subs):
        for block in range(NB):
            pieces = []
            for group in range(RQ):
                row = (group * subs + sub) * rows_sub
                piece = source[row : row + rows_sub, :, block * BS : (block + 1) * BS]
                pieces.append(piece.reshape(rows_sub * cols, BS))
            slots[sub * NB + block] = jnp.concatenate(pieces, axis=1)
    deal(sent, slots, own[0])


def unpack_body(rows_sub, subs, own, base, *rest):
    received, (result, slots) = rest[:-2], rest[-2:]
    cols = base.shape[1]
    place(slots, received, own[0])
    for sub in range(subs):
        for group in range(RQ):
            row = (group * subs + sub) * rows_sub
            pieces = [
                slots[sub * NB + block, :, group * BS : (group + 1) * BS] for block in range(NB)
            ]
            update = jnp.concatenate(pieces, axis=1).reshape(rows_sub, cols, NB * BS)
            old = base[row : row + rows_sub]
            result[row : row + rows_sub] = (
                old.astype(jnp.float32) + update.astype(jnp.float32)
            ).astype(jnp.bfloat16)


def product(left, right):
    return jnp.dot(left, right, preferred_element_type=jnp.float32)


def product_back(left, right):
    return lax.dot_general(
        left, right, (((1,), (1,)), ((), ())), preferred_element_type=jnp.float32
    )


def product_outer(left, right):
    return lax.dot_general(
        left, right, (((0,), (0,)), ((), ())), preferred_element_type=jnp.float32
    )


def place(slots, pieces, own):
    if len(pieces) == 1:
        slots[...] = pieces[0][...]
        return
    for offset, piece in enumerate(pieces):
        slots[jnp.bitwise_xor(own, offset)] = piece[...]


def deal(pieces, slots, own):
    if len(pieces) == 1:
        pieces[0][...] = slots[...]
        return
    for offset, piece in enumerate(pieces):
        piece[...] = slots[jnp.bitwise_xor(own, offset)]


def spectra_body(count, extra, cuts, kept, own_in, own_out, table, *rest):
    received, (sent, slots_in, slots_out) = rest[:count], (rest[count + extra : -2], *rest[-2:])
    place(slots_in, received, own_in[0])
    each = slots_in.shape[1] // cuts
    parts = []
    for cut in range(cuts):
        flat = slots_in[:, cut * each : (cut + 1) * each].reshape(-1, PACK)
        parts.append(product(table[...], flat).reshape(slots_out.shape[0] * kept, -1, PACK))
    joined = jnp.stack(parts, axis=1) if cuts > 1 else parts[0]
    slots_out[...] = joined.reshape(slots_out.shape).astype(jnp.bfloat16)
    deal(sent, slots_out, own_out[0])


def columns_body(count, extra, cuts, kept, own_in, table, *rest):
    received, (result, slots_in, slots_out, sems) = rest[:count], rest[count + extra :]
    place(slots_in, received, own_in[0])
    each = slots_out.shape[1] // cuts
    modes = slots_in.shape[0] * kept
    split = slots_in[...].astype(jnp.float32).reshape(modes, cuts, -1, PACK)
    flats = [split[:, cut].reshape(-1, PACK).astype(jnp.bfloat16) for cut in range(cuts)]
    copies = []
    for cut, flat in enumerate(flats):
        part = product(table[...], flat).astype(jnp.bfloat16)
        rows = pl.ds(cut * each, each)
        slots_out[:, rows] = part.reshape(slots_out.shape[0], each, PACK)
        copies.append(
            pltpu.make_async_copy(slots_out.at[:, rows], result.at[:, rows], sems.at[cut])
        )
        copies[-1].start()
    finish(copies)


def finish(copies):
    for copy in copies:
        copy.wait()


def load_weights(block, weights, real_imag, sems):
    copies = [
        pltpu.make_async_copy(source.at[part, block], real_imag.at[slot, part], sems.at[slot, part])
        for slot, source in enumerate(weights)
        for part in range(2)
    ]
    for copy in copies:
        copy.start()
    return copies


def complex_weights(real_imag, full):
    for slot in range(full.shape[0]):
        real, imag = real_imag[slot, 0], real_imag[slot, 1]
        full[slot, :BS] = jnp.concatenate([real, imag], axis=1)
        full[slot, BS:] = jnp.concatenate([-imag, real], axis=1)


def lat_forward(table, slots, tile, deep, rows):
    slab = slots[:, tile * deep : (tile + 1) * deep]
    flat = slab.reshape(slab.shape[0] * deep, PACK)
    stacked = jnp.concatenate(
        [flat[:, group * BS : (group + 1) * BS] for group in range(RQ)], axis=0
    )
    spectrum = product(table, stacked).astype(jnp.bfloat16)
    return [
        jnp.concatenate([spectrum[at : at + rows], spectrum[at + rows : at + 2 * rows]], axis=1)
        for at in range(0, spectrum.shape[0], 2 * rows)
    ]


def lat_inverse(table, values, slots, tile, deep):
    stacked = jnp.concatenate(
        [part for value in values for part in (value[:, :BS], value[:, BS:])], axis=0
    )
    rows = product(table, stacked).astype(jnp.bfloat16)
    each = rows.shape[0] // RQ
    packed = jnp.concatenate([rows[at : at + each] for at in range(0, RQ * each, each)], axis=1)
    slots[:, tile * deep : (tile + 1) * deep] = packed.reshape(slots.shape[0], deep, PACK)


def mode_weight(first_mode, index):
    return jnp.where(first_mode + index == 0, 1.0, 2.0).astype(jnp.float32)


def gelu(pre):
    squared = pre * pre
    tangent = jnp.tanh(gelu_coeff * (pre + 0.044715 * squared * pre))
    act = (0.5 * pre * (1.0 + tangent)).astype(jnp.bfloat16)
    return act, squared, tangent


def forward_body(members, pack_modes, member, first_mode, block, table, *rest):
    received, weights, sent = rest[:members], rest[members : members + 2], rest[members + 2 :]
    sent, rest = sent[:members], sent[members:]
    saved, anchor, slots, spec, real_imag, full, weight_sems, save_sems = rest
    anchor[...] = jnp.zeros_like(anchor)
    loads = load_weights(block[0], weights, real_imag, weight_sems)
    own = member[0]
    kept, rows, _ = spec.shape
    deep = slots.shape[1] * pack_modes // kept
    place(slots, received, own)
    lat = table[...]
    inverse = lat.T
    copies = []
    for tile in range(kept // pack_modes):
        for inner, values in enumerate(lat_forward(lat, slots, tile, deep, rows)):
            index = tile * pack_modes + inner
            spec[index, :, :WIDE] = values
            copies.append(
                pltpu.make_async_copy(spec.at[index], saved.at[index], save_sems.at[index])
            )
            copies[-1].start()
    finish(loads)
    complex_weights(real_imag, full)
    for tile in range(kept // pack_modes):
        outs = []
        for index in range(tile * pack_modes, (tile + 1) * pack_modes):
            act, _, _ = gelu(product(spec[index, :, :WIDE], full[0]))
            post = product(act, full[1])
            weight = mode_weight(first_mode[0], index)
            shrunk = post - shrink_level * jnp.tanh(post / shrink_level)
            outs.append((weight * shrunk).astype(jnp.bfloat16))
        lat_inverse(inverse, outs, slots, tile, deep)
    deal(sent, slots, own)
    finish(copies)


def backward_body(
    members, shares, pack_modes, factor, member, first_mode, lat_own, block, table, *rest
):
    received, rest = rest[:members], rest[members:]
    weights, saved, result, combined, rest = rest[:2], rest[2], rest[3], rest[4], rest[5:]
    parts, (slots, grads, cots, spec, real_imag, full, weight_sems, load_sems) = (
        rest[:shares],
        rest[shares:],
    )
    loads = load_weights(block[0], weights, real_imag, weight_sems)
    kept, rows, _ = spec.shape
    deep = slots.shape[1] * pack_modes // kept
    spec_loads = [
        pltpu.make_async_copy(saved.at[index], spec.at[index], load_sems.at[index])
        for index in range(kept)
    ]
    for copy in spec_loads:
        copy.start()
    place(slots, received, member[0])
    lat = table[...]
    for tile in range(kept // pack_modes):
        for inner, cot in enumerate(lat_forward(lat, slots, tile, deep, rows)):
            cots[tile * pack_modes + inner] = cot
    finish(loads)
    complex_weights(real_imag, full)
    combined[...] = full[0]
    total_first = jnp.zeros((WIDE, WIDE), jnp.float32)
    total_second = jnp.zeros((WIDE, WIDE), jnp.float32)
    for index in range(kept):
        spec_loads[index].wait()
        values = spec[index, :, :WIDE]
        pre = product(values, full[0])
        act, squared, tangent = gelu(pre)
        slope = 0.5 * (1.0 + tangent) + 0.5 * pre * (1.0 - tangent * tangent) * gelu_coeff * (
            1.0 + 3.0 * 0.044715 * squared
        )
        ratio = jnp.tanh(product(act, full[1]) / shrink_level)
        weight = mode_weight(first_mode[0], index)
        cot = cots[index].astype(jnp.float32)
        grad_post = (weight * cot * (ratio * ratio)).astype(jnp.bfloat16)
        grad_pre = (product_back(grad_post, full[1]) * slope).astype(jnp.bfloat16)
        result[index] = grad_pre
        total_second += product_outer(act, grad_post)
        total_first += product_outer(values, grad_pre)
    share = grads.shape[1]
    for slot, total in enumerate((total_first, total_second)):
        real = (total[:BS, :BS] + total[BS:, BS:]) * factor
        imag = (total[:BS, BS:] - total[BS:, :BS]) * factor
        for part, value in enumerate((real, imag)):
            for at in range(0, BS, share):
                piece = ((2 * slot + part) * BS + at) // share
                grads[piece] = value[at : at + share].astype(jnp.bfloat16)
    deal(parts, grads, lat_own[0])


def input_grad_body(pack_modes, extra, member, table, grad_pre, combined, *rest):
    sent, slots = rest[extra:-1], rest[-1]
    kept = grad_pre.shape[0]
    deep = slots.shape[1] * pack_modes // kept
    inverse = table[...].T
    for tile in range(kept // pack_modes):
        backs = [
            product_back(grad_pre[index], combined[...]).astype(jnp.bfloat16)
            for index in range(tile * pack_modes, (tile + 1) * pack_modes)
        ]
        lat_inverse(inverse, backs, slots, tile, deep)
    deal(sent, slots, member[0])


def sum_body(*refs):
    refs[-1][...] = sum(value[...].astype(jnp.float32) for value in refs[:-1]).astype(jnp.bfloat16)


def stack_body(*refs):
    for slot, piece in enumerate(refs[:-1]):
        refs[-1][slot] = piece[...]


def blocks_body(own, near, other, blocks):
    for slot in range(near.shape[0]):
        blocks[jnp.bitwise_xor(own[0], 2 * slot)] = near[slot]
        blocks[jnp.bitwise_xor(own[0], 2 * slot + 1)] = other[slot]


def assemble_body(lat_count, subs, lat_own, *rest):
    gathered, (first, second, slots) = rest[:lat_count], rest[lat_count:]
    rows = gathered[0].shape[1]
    for offset, pieces in enumerate(gathered):
        start = jnp.bitwise_xor(lat_own[0], offset) * rows
        matrix, row = start // BS, pl.multiple_of(start % BS, 16)
        for block in range(NB):
            total = None
            for sub in range(subs):
                value = pieces[sub * NB + block].astype(jnp.float32)
                total = value if total is None else total + value
            slots[matrix, block, pl.ds(row, rows)] = total
    first[...] = slots[:2]
    second[...] = slots[2:]


def exchange(source):
    return lax.all_to_all(source, "lon", split_axis=0, concat_axis=0, tiled=True)


def swap(pieces, axes, partners):
    return [pieces[0]] + [
        lax.ppermute(piece, axes, partners(offset))
        for offset, piece in enumerate(pieces)
        if offset
    ]


def shards(features, cotangent, weight_first, weight_second):
    lat_count = lax.axis_size("lat")
    lon_count = lax.axis_size("lon")
    band_rows, band_cols, channels = features.shape
    rows_total = band_rows * lat_count
    cols_total = band_cols * lon_count
    kept_total = KWD * lat_count * lon_count
    subs = lon_count // NB
    members = lat_count * subs
    rows_sub = band_rows // (RQ * subs)
    rows_cut = min(rows_sub, 4)
    cuts = rows_sub // rows_cut
    kept = kept_total // members
    deep = 2 * rows_sub
    pack_modes = max(1, 16 // deep)
    lat_index = lax.axis_index("lat")
    lon_index = lax.axis_index("lon")
    block = lon_index % NB
    member = lat_index * subs + lon_index // NB
    bf16, f32 = jnp.bfloat16, jnp.float32
    array = jax.ShapeDtypeStruct

    def member_pairs(offset):
        pairs = []
        for lat in range(lat_count):
            for lon in range(lon_count):
                other = (lat * subs + lon // NB) ^ offset
                lon_other = other % subs * NB + lon % NB
                pairs.append((lat * lon_count + lon, other // subs * lon_count + lon_other))
        return pairs

    def line_pairs(count):
        return lambda offset: [(place, place ^ offset) for place in range(count)]

    lon_fwd, lon_inv = map(constant, lon_tables(kept_total, cols_total, lon_count, rows_cut))
    lat_both = constant(lat_table(rows_total, lat_count, subs, rows_sub, rows_cut, pack_modes))
    lon_piece = array((rows_sub * band_cols, PACK), bf16)
    lon_whole = array((lon_count, rows_sub * band_cols, PACK), bf16)
    mid_piece = array((kept * deep, PACK), bf16)
    lon_slots = pltpu.VMEM(lon_whole.shape, bf16)
    mid_slots = pltpu.VMEM((members, kept * deep, PACK), bf16)
    mid_limit = 14 * MIB + 5 * lat_both.size
    share = 4 * BS // lat_count

    def mid_swap(pieces):
        return swap(pieces, ("lat", "lon"), member_pairs)

    def pack(source, sent):
        body = functools.partial(pack_body, rows_sub, subs)
        return kernel_call(body, sent, [lon_index], [source], [lon_slots])

    def unpack(source, base):
        body = functools.partial(unpack_body, rows_sub, subs)
        result = array(base.shape, bf16)
        return kernel_call(body, [result], [lon_index], [base, source], [lon_slots])[0]

    def to_spectra(pieces, anchors=()):
        return kernel_call(
            functools.partial(spectra_body, len(pieces), len(anchors), cuts, kept),
            [mid_piece] * members,
            [lon_index, member],
            [lon_fwd, *pieces],
            [lon_slots, mid_slots],
            anchors,
        )

    def to_columns(pieces, anchors=()):
        return kernel_call(
            functools.partial(columns_body, members, len(anchors), cuts, kept),
            [pltpu.HBM(lon_whole.shape, bf16)],
            [member],
            [lon_inv, *pieces],
            [mid_slots, lon_slots, pltpu.SemaphoreType.DMA((cuts,))],
            anchors,
        )[0]

    modes = (kept, rows_total, STATE)
    weights = [weight_first, weight_second]
    mid_scratch = [
        pltpu.VMEM(modes, bf16),
        pltpu.VMEM((2, 2, BS, BS), bf16),
        pltpu.VMEM((2, WIDE, WIDE), bf16),
        pltpu.SemaphoreType.DMA((2, 2)),
        pltpu.SemaphoreType.DMA((kept,)),
    ]

    field = swap(pack(features, [lon_piece] * lon_count), "lon", line_pairs(lon_count))
    field_cot = exchange(gate(pack(cotangent, [lon_whole])[0], field))
    results = kernel_call(
        functools.partial(forward_body, members, pack_modes),
        [mid_piece] * members + [pltpu.HBM(modes, bf16), array((8, 128), f32)],
        [member, member * kept, block],
        [lat_both, *mid_swap(to_spectra(field))],
        [mid_slots, *mid_scratch],
        far=weights,
        limit=mid_limit,
    )
    saved, anchor = results[members:]
    spectra_cot = to_spectra([field_cot], [anchor])
    filtered = exchange(to_columns(mid_swap(results[:members]), spectra_cot[:1]))
    wide = (kept, rows_total, WIDE)
    grad_pre, combined, *parts = kernel_call(
        functools.partial(
            backward_body, members, lat_count, pack_modes, 1.0 / math.sqrt(rows_total * kept_total)
        ),
        [array(wide, bf16), array((WIDE, WIDE), bf16)] + [array((share, BS), bf16)] * lat_count,
        [member, member * kept, lat_index, block],
        [lat_both, *mid_swap(spectra_cot)],
        [
            mid_slots,
            pltpu.VMEM((lat_count, share, BS), bf16),
            pltpu.VMEM(wide, bf16),
            *mid_scratch,
        ],
        far=weights + [saved],
        limit=mid_limit,
    )
    own_share = kernel_call(
        sum_body, [array((share, BS), bf16)], [], swap(parts, "lat", line_pairs(lat_count))
    )[0]
    back = kernel_call(
        functools.partial(input_grad_body, pack_modes, 1),
        [mid_piece] * members,
        [member],
        [lat_both, grad_pre, combined],
        [mid_slots],
        [own_share],
        limit=mid_limit,
    )
    lon_pairs = line_pairs(lon_count)
    near = kernel_call(
        stack_body,
        [array((lon_count // 2, share, BS), bf16)],
        [],
        [own_share]
        + [lax.ppermute(own_share, "lon", lon_pairs(far)) for far in range(2, lon_count, 2)],
    )[0]
    returned = exchange(to_columns(mid_swap(back), [near]))
    blocks = kernel_call(
        blocks_body,
        [array((lon_count, share, BS), bf16)],
        [lon_index],
        [near, lax.ppermute(near, "lon", lon_pairs(1))],
    )[0]

    gathered = {0: blocks}
    step = lat_count // 2
    while step:
        for offset in sorted(gathered):
            moved = lax.ppermute(gathered[offset], "lat", line_pairs(lat_count)(step))
            gathered[offset | step] = moved
        step //= 2
    gathered = [gathered[offset] for offset in range(lat_count)]
    full = array((2, NB, BS, BS), f32)
    grad_first, grad_second = kernel_call(
        functools.partial(assemble_body, lat_count, subs),
        [full, full],
        [lat_index],
        gathered,
        [pltpu.VMEM((4, NB, BS, BS), f32)],
    )
    return (unpack(filtered, features), unpack(returned, cotangent), grad_first, grad_second)


def solution(mesh):
    in_specs = (P("lat", "lon", None), P("lat", "lon", None), P(), P())
    out_specs = (P("lat", "lon", None), P("lat", "lon", None), P(), P())
    return jax.shard_map(shards, mesh=mesh, in_specs=in_specs, out_specs=out_specs, check_vma=False)
```

profile of v0, /device:TPU:0, one launch (start us, length us, event | category | flops | bytes accessed | tf_op | source)
XLA Modules:
  0.0 116.7 jit_solution(16886737296880328813)
XLA Ops:
  2.9 3.0 %collective-permute-start = (bf16[128,384]{1,0:T(8,128)(2,1)S(1)}, bf16[128,384]{1,0:T(8,128)(2,1)S(1)}, u32[]{:S(2)}, u32[]{:S(2)}) collective-permute-start(bf16[128,384]{1,0:T(8,128)(2,1)S(1)} %get-tuple-element.39), channel_id=1, source_target_pairs={{0,1},{1,0},{2,3},{3,2},{4,5},{5,4},{6,7},{7,6},{8,9},{9,8},{10,11... | collective-permute-start | bytes 294920 | tf_op jit(solution)/shard_map/ppermute | solution.py:380
  5.9 1.6 %collective-permute-start.1 = (bf16[128,384]{1,0:T(8,128)(2,1)S(1)}, bf16[128,384]{1,0:T(8,128)(2,1)S(1)}, u32[]{:S(2)}, u32[]{:S(2)}) collective-permute-start(bf16[128,384]{1,0:T(8,128)(2,1)S(1)} %get-tuple-element.40), channel_id=1, source_target_pairs={{0,2},{1,3},{2,0},{3,1},{4,6},{5,7},{6,4},{7,5},{8,10},{9,11},{10,... | collective-permute-start | bytes 294920 | tf_op jit(solution)/shard_map/ppermute | solution.py:380
  7.5 3.0 %collective-permute-start.3 = (bf16[128,384]{1,0:T(8,128)(2,1)S(1)}, bf16[128,384]{1,0:T(8,128)(2,1)S(1)}, u32[]{:S(2)}, u32[]{:S(2)}) collective-permute-start(bf16[128,384]{1,0:T(8,128)(2,1)S(1)} %get-tuple-element.42), channel_id=1, source_target_pairs={{0,4},{1,5},{2,6},{3,7},{4,0},{5,1},{6,2},{7,3},{8,12},{9,13},{10,... | collective-permute-start | bytes 294920 | tf_op jit(solution)/shard_map/ppermute | solution.py:380
  10.5 1.3 %collective-permute-start.4 = (bf16[128,384]{1,0:T(8,128)(2,1)S(1)}, bf16[128,384]{1,0:T(8,128)(2,1)S(1)}, u32[]{:S(2)}, u32[]{:S(2)}) collective-permute-start(bf16[128,384]{1,0:T(8,128)(2,1)S(1)} %get-tuple-element.43), channel_id=1, source_target_pairs={{0,5},{1,4},{2,7},{3,6},{4,1},{5,0},{6,3},{7,2},{8,13},{9,12},{10,... | collective-permute-start | bytes 294920 | tf_op jit(solution)/shard_map/ppermute | solution.py:380
  11.8 3.6 %collective-permute-start.5 = (bf16[128,384]{1,0:T(8,128)(2,1)S(1)}, bf16[128,384]{1,0:T(8,128)(2,1)S(1)}, u32[]{:S(2)}, u32[]{:S(2)}) collective-permute-start(bf16[128,384]{1,0:T(8,128)(2,1)S(1)} %get-tuple-element.44), channel_id=1, source_target_pairs={{0,6},{1,7},{2,4},{3,5},{4,2},{5,3},{6,0},{7,1},{8,14},{9,15},{10,... | collective-permute-start | bytes 294920 | tf_op jit(solution)/shard_map/ppermute | solution.py:380
  16.9 8.8 %collective-permute-done.4.rest_5_.refs_6_ = bf16[128,384]{1,0:T(8,128)(2,1)S(1)} collective-permute-done((bf16[128,384]{1,0:T(8,128)(2,1)S(1)}, bf16[128,384]{1,0:T(8,128)(2,1)S(1)}, u32[]{:S(2)}, u32[]{:S(2)}) %collective-permute-start.4) | collective-permute-done | bytes 98336 | tf_op jit(solution)/shard_map/ppermute | solution.py:380
  26.5 6.5 %all-to-all-start = ((bf16[8,128,384]{2,1,0:T(8,128)(2,1)}), bf16[8,128,384]{2,1,0:T(8,128)(2,1)S(1)}, u32[]{:S(2)}, u32[]{:S(2)}) async-start(bf16[8,128,384]{2,1,0:T(8,128)(2,1)} %shard_map.106), calls=%async_computation | async-start | bytes 1572864 | tf_op jit(solution)/shard_map/all_to_all | solution.py:375
  33.7 1.6 %collective-permute-start.8 = (bf16[128,384]{1,0:T(8,128)(2,1)S(1)}, bf16[128,384]{1,0:T(8,128)(2,1)S(1)}, u32[]{:S(2)}, u32[]{:S(2)}) collective-permute-start(bf16[128,384]{1,0:T(8,128)(2,1)S(1)} %get-tuple-element.48), channel_id=1, source_target_pairs={{0,16},{1,17},{2,18},{3,19},{4,20},{5,21},{6,22},{7,23},{8,24},{9,... | collective-permute-start | bytes 294920 | tf_op jit(solution)/shard_map/ppermute | solution.py:380
  35.6 3.8 %collective-permute-done.8.rest_2_ = bf16[128,384]{1,0:T(8,128)(2,1)S(1)} collective-permute-done((bf16[128,384]{1,0:T(8,128)(2,1)S(1)}, bf16[128,384]{1,0:T(8,128)(2,1)S(1)}, u32[]{:S(2)}, u32[]{:S(2)}) %collective-permute-start.8) | collective-permute-done | bytes 98336 | tf_op jit(solution)/shard_map/ppermute | solution.py:380
  40.6 3.5 %shard_map.104 = (bf16[128,384]{1,0:T(8,128)(2,1)S(1)}, bf16[128,384]{1,0:T(8,128)(2,1)S(1)}, bf16[128,384]{1,0:T(8,128)(2,1)S(1)}, bf16[128,384]{1,0:T(8,128)(2...) custom-call(s32[1]{0:T(128)} %bitcast.1.own_out.member.own_in, s32[1]{0:T(128)} %bitcast.2.first_mode, ...), custom_call_target="tpu_custom_call" | custom-call | tf_op jit(solution)/shard_map/pallas_call | solution.py:65
  44.7 1.5 %collective-permute-start.11 = (bf16[128,384]{1,0:T(8,128)(2,1)S(1)}, bf16[128,384]{1,0:T(8,128)(2,1)S(1)}, u32[]{:S(2)}, u32[]{:S(2)}) collective-permute-start(bf16[128,384]{1,0:T(8,128)(2,1)S(1)} %get-tuple-element.52), channel_id=1, source_target_pairs={{0,16},{1,17},{2,18},{3,19},{4,20},{5,21},{6,22},{7,23},{8,24},{9,... | collective-permute-start | bytes 294920 | tf_op jit(solution)/shard_map/ppermute | solution.py:380
  46.2 6.4 %all-to-all-done.rest_0_ = bf16[8,128,384]{2,1,0:T(8,128)(2,1)S(1)} async-done(((bf16[8,128,384]{2,1,0:T(8,128)(2,1)}), bf16[8,128,384]{2,1,0:T(8,128)(2,1)S(1)}, u32[]{:S(2)}, u32[]{:S(2)}) %all-to-all-start) | async-done | bytes 786464 | tf_op jit(solution)/shard_map/all_to_all | solution.py:375
  53.5 1.2 %shard_map.108 = bf16[8,128,384]{2,1,0:T(8,128)(2,1)} custom-call(s32[1]{0:T(128)} %bitcast.1.own_out.member.own_in, bf16[512,256]{1,0:T(8,128)(2,1)S(1)} %copy-done.6, bf16[128,384]{1,0:T(8,128)(2,1)S(1)} %get-tuple-element.50.rest_0_, bf16[128,384]{1,0:T(8,128)(2,1)S(1)} %collective-permute-done.10.rest_1_, ...), custom_call_target="tpu_custom_call" | custom-call | tf_op jit(solution)/shard_map/pallas_call | solution.py:65
  54.8 3.8 %all-to-all-start.1 = ((bf16[8,128,384]{2,1,0:T(8,128)(2,1)}), bf16[8,128,384]{2,1,0:T(8,128)(2,1)S(1)}, u32[]{:S(2)}, u32[]{:S(2)}) async-start(bf16[8,128,384]{2,1,0:T(8,128)(2,1)} %shard_map.108), calls=%async_computation.1 | async-start | bytes 1572864 | tf_op jit(solution)/shard_map/all_to_all | solution.py:375
  58.5 1.4 %collective-permute-start.14 = (bf16[128,384]{1,0:T(8,128)(2,1)S(1)}, bf16[128,384]{1,0:T(8,128)(2,1)S(1)}, u32[]{:S(2)}, u32[]{:S(2)}) collective-permute-start(bf16[128,384]{1,0:T(8,128)(2,1)S(1)} %get-tuple-element.57), channel_id=1, source_target_pairs={{0,16},{1,17},{2,18},{3,19},{4,20},{5,21},{6,22},{7,23},{8,24},{9,... | collective-permute-start | bytes 294920 | tf_op jit(solution)/shard_map/ppermute | solution.py:380
  60.4 3.8 %collective-permute-done.14.rest_2_ = bf16[128,384]{1,0:T(8,128)(2,1)S(1)} collective-permute-done((bf16[128,384]{1,0:T(8,128)(2,1)S(1)}, bf16[128,384]{1,0:T(8,128)(2,1)S(1)}, u32[]{:S(2)}, u32[]{:S(2)}) %collective-permute-start.14) | collective-permute-done | bytes 98336 | tf_op jit(solution)/shard_map/ppermute | solution.py:380
  65.4 5.8 %shard_map.110 = (bf16[8,128,192]{2,1,0:T(8,128)(2,1)S(1)}, bf16[192,192]{1,0:T(8,128)(2,1)S(1)}, bf16[96,96]{1,0:T(8,128)(2,1)S(1)}, bf16[96,96]{1,0:T(8,128)(2...) custom-call(s32[1]{0:T(128)} %bitcast.1.own_out.member.own_in, s32[1]{0:T(128)} %bitcast.2.first_mode, ...), custom_call_target="tpu_custom_call" | custom-call | tf_op jit(solution)/shard_map/pallas_call | solution.py:65
  71.9 1.4 %collective-permute-start.17 = (bf16[96,96]{1,0:T(8,128)(2,1)S(1)}, bf16[96,96]{1,0:T(8,128)(2,1)S(1)}, u32[]{:S(2)}, u32[]{:S(2)}) collective-permute-start(bf16[96,96]{1,0:T(8,128)(2,1)S(1)} %get-tuple-element.64), channel_id=1, source_target_pairs={{0,16},{8,24},{16,0},{24,8},{1,17},{9,25},{17,1},{25,9},{2,18},{10... | collective-permute-start | bytes 55304 | tf_op jit(solution)/shard_map/ppermute | solution.py:380
  73.3 2.4 %collective-permute-done.17.refs_2_ = bf16[96,96]{1,0:T(8,128)(2,1)S(1)} collective-permute-done((bf16[96,96]{1,0:T(8,128)(2,1)S(1)}, bf16[96,96]{1,0:T(8,128)(2,1)S(1)}, u32[]{:S(2)}, u32[]{:S(2)}) %collective-permute-start.17) | collective-permute-done | bytes 18464 | tf_op jit(solution)/shard_map/ppermute | solution.py:380
  76.8 1.6 %shard_map.112 = (bf16[128,384]{1,0:T(8,128)(2,1)S(1)}, bf16[128,384]{1,0:T(8,128)(2,1)S(1)}, bf16[128,384]{1,0:T(8,128)(2,1)S(1)}, bf16[128,384]{1,0:T(8,128)(2,1)S(1)}) custom-call(s32[1]{0:T(128)} %bitcast.1.own_out.member.own_in, bf16[256,256]{1,0:T(8,128)(2,1)S(1)} %copy-done.4, bf16[8,128,192]{2,1,0:T(8,128)(2,1)S(1)} %get-tuple-element.60.grad_pre, ...), custom_call_target="tpu_custom_call" | custom-call | tf_op jit(solution)/shard_map/pallas_call | solution.py:65
  80.3 3.7 %collective-permute-start.24 = (bf16[96,96]{1,0:T(8,128)(2,1)S(1)}, bf16[96,96]{1,0:T(8,128)(2,1)S(1)}, u32[]{:S(2)}, u32[]{:S(2)}) collective-permute-start(bf16[96,96]{1,0:T(8,128)(2,1)S(1)} %shard_map.111.rest_0_.refs_0_), channel_id=1, source_target_pairs={{0,6},{1,7},{2,4},{3,5},{4,2},{5,3},{6,0},{7,1},{8,14},{9,15},{10,... | collective-permute-start | bytes 55304 | tf_op jit(solution)/shard_map/ppermute | solution.py:521
  84.0 1.9 %collective-permute-done.24.refs_3_ = bf16[96,96]{1,0:T(8,128)(2,1)S(1)} collective-permute-done((bf16[96,96]{1,0:T(8,128)(2,1)S(1)}, bf16[96,96]{1,0:T(8,128)(2,1)S(1)}, u32[]{:S(2)}, u32[]{:S(2)}) %collective-permute-start.24) | collective-permute-done | bytes 18464 | tf_op jit(solution)/shard_map/ppermute | solution.py:521
  86.6 2.2 %collective-permute-done.23.refs_2_ = bf16[96,96]{1,0:T(8,128)(2,1)S(1)} collective-permute-done((bf16[96,96]{1,0:T(8,128)(2,1)S(1)}, bf16[96,96]{1,0:T(8,128)(2,1)S(1)}, u32[]{:S(2)}, u32[]{:S(2)}) %collective-permute-start.23) | collective-permute-done | bytes 18464 | tf_op jit(solution)/shard_map/ppermute | solution.py:521
  89.8 1.2 %shard_map.114 = bf16[8,128,384]{2,1,0:T(8,128)(2,1)} custom-call(s32[1]{0:T(128)} %bitcast.1.own_out.member.own_in, bf16[512,256]{1,0:T(8,128)(2,1)S(1)} %copy-done.6, bf16[128,384]{1,0:T(8,128)(2,1)S(1)} %get-tuple-element.66.rest_0_, bf16[128,384]{1,0:T(8,128)(2,1)S(1)} %collective-permute-done.19.rest_1_, ...), custom_call_target="tpu_custom_call" | custom-call | tf_op jit(solution)/shard_map/pallas_call | solution.py:65
  91.1 5.9 %all-to-all-start.2 = ((bf16[8,128,384]{2,1,0:T(8,128)(2,1)}), bf16[8,128,384]{2,1,0:T(8,128)(2,1)S(1)}, u32[]{:S(2)}, u32[]{:S(2)}) async-start(bf16[8,128,384]{2,1,0:T(8,128)(2,1)} %shard_map.114), calls=%async_computation.2 | async-start | bytes 1572864 | tf_op jit(solution)/shard_map/all_to_all | solution.py:375
  97.0 2.0 %collective-permute-start.25 = (bf16[4,96,96]{2,1,0:T(8,128)(2,1)S(1)}, bf16[4,96,96]{2,1,0:T(8,128)(2,1)S(1)}, u32[]{:S(2)}, u32[]{:S(2)}) collective-permute-start(bf16[4,96,96]{2,1,0:T(8,128)(2,1)S(1)} %shard_map.113.rest_4_.near), channel_id=1, source_target_pairs={{0,1},{1,0},{2,3},{3,2},{4,5},{5,4},{6,7},{7,6},{8,9},{9,8},{10,11... | collective-permute-start | bytes 221192 | tf_op jit(solution)/shard_map/ppermute | solution.py:528
  99.0 6.3 %collective-permute-done.25.other = bf16[4,96,96]{2,1,0:T(8,128)(2,1)S(1)} collective-permute-done((bf16[4,96,96]{2,1,0:T(8,128)(2,1)S(1)}, bf16[4,96,96]{2,1,0:T(8,128)(2,1)S(1)}, u32[]{:S(2)}, u32[]{:S(2)}) %collective-permute-start.25) | collective-permute-done | bytes 73760 | tf_op jit(solution)/shard_map/ppermute | solution.py:528
  106.3 4.8 %collective-permute-done.27.rest_2_ = bf16[8,96,96]{2,1,0:T(8,128)(2,1)S(1)} collective-permute-done((bf16[8,96,96]{2,1,0:T(8,128)(2,1)S(1)}, bf16[8,96,96]{2,1,0:T(8,128)(2,1)S(1)}, u32[]{:S(2)}, u32[]{:S(2)}) %collective-permute-start.27) | collective-permute-done | bytes 147488 | tf_op jit(solution)/shard_map/ppermute | solution.py:535
  111.1 1.4 %collective-permute-done.28.rest_3_ = bf16[8,96,96]{2,1,0:T(8,128)(2,1)S(1)} collective-permute-done((bf16[8,96,96]{2,1,0:T(8,128)(2,1)S(1)}, bf16[8,96,96]{2,1,0:T(8,128)(2,1)S(1)}, u32[]{:S(2)}, u32[]{:S(2)}) %collective-permute-start.28) | collective-permute-done | bytes 147488 | tf_op jit(solution)/shard_map/ppermute | solution.py:535
  112.5 1.3 %shard_map.117 = (f32[2,8,96,96]{3,2,1,0:T(8,128)}, f32[2,8,96,96]{3,2,1,0:T(8,128)}) custom-call(s32[1]{0:T(128)} %bitcast.4.lat_own, bf16[8,96,96]{2,1,0:T(8,128)(2,1)S(1)} %shard_map.116.rest_0_, bf16[8,96,96]{2,1,0:T(8,128)(2,1)S(1)} %collective-permute-done.26.rest_1_, bf16[8,96,96]{2,1,0:T(8,128)(2,1)S(1)} %collective-permute-done.27.rest_2_, ...), custom_call_target="tpu_custom_call" | custom-call | tf_op jit(solution)/shard_map/pallas_call | solution.py:65
  113.8 1.3 %shard_map.109 = bf16[32,16,768]{2,1,0:T(8,128)(2,1)} custom-call(s32[1]{0:T(128)} %bitcast.own.own_in, bf16[32,16,768]{2,1,0:T(8,128)(2,1)S(1)} %copy-done.3, bf16[8,128,384]{2,1,0:T(8,128)(2,1)S(1)} %all-to-all-done.1.rest_0_), custom_call_target="tpu_custom_call" | custom-call | tf_op jit(solution)/shard_map/pallas_call | solution.py:65
  115.4 1.3 %shard_map.115 = bf16[32,16,768]{2,1,0:T(8,128)(2,1)} custom-call(s32[1]{0:T(128)} %bitcast.own.own_in, bf16[32,16,768]{2,1,0:T(8,128)(2,1)S(1)} %copy-done.1, bf16[8,128,384]{2,1,0:T(8,128)(2,1)S(1)} %all-to-all-done.2.rest_0_), custom_call_target="tpu_custom_call" | custom-call | tf_op jit(solution)/shard_map/pallas_call | solution.py:65
  (94 shorter events, 16.5 us)
Async XLA Ops:
  2.9 8.8 %collective-permute-start = (bf16[128,384]{1,0:T(8,128)(2,1)S(1)}, bf16[128,384]{1,0:T(8,128)(2,1)S(1)}, u32[]{:S(2)}, u32[]{:S(2)}) collective-permute-start(bf16[128,384]{1,0:T(8,128)(2,1)S(1)} %get-tuple-element.39), channel_id=1, source_target_pairs={{0,1},{1,0},{2,3},{3,2},{4,5},{5,4},{6,7},{7,6},{8,9},{9,8},{10,11... | collective-permute-start | bytes 294920 | tf_op jit(solution)/shard_map/ppermute | solution.py:380
  5.9 9.5 %collective-permute-start.1 = (bf16[128,384]{1,0:T(8,128)(2,1)S(1)}, bf16[128,384]{1,0:T(8,128)(2,1)S(1)}, u32[]{:S(2)}, u32[]{:S(2)}) collective-permute-start(bf16[128,384]{1,0:T(8,128)(2,1)S(1)} %get-tuple-element.40), channel_id=1, source_target_pairs={{0,2},{1,3},{2,0},{3,1},{4,6},{5,7},{6,4},{7,5},{8,10},{9,11},{10,... | collective-permute-start | bytes 294920 | tf_op jit(solution)/shard_map/ppermute | solution.py:380
  7.5 9.4 %collective-permute-start.2 = (bf16[128,384]{1,0:T(8,128)(2,1)S(1)}, bf16[128,384]{1,0:T(8,128)(2,1)S(1)}, u32[]{:S(2)}, u32[]{:S(2)}) collective-permute-start(bf16[128,384]{1,0:T(8,128)(2,1)S(1)} %get-tuple-element.41), channel_id=1, source_target_pairs={{0,3},{1,2},{2,1},{3,0},{4,7},{5,6},{6,5},{7,4},{8,11},{9,10},{10,... | collective-permute-start | bytes 294920 | tf_op jit(solution)/shard_map/ppermute | solution.py:380
  7.5 9.4 %collective-permute-start.3 = (bf16[128,384]{1,0:T(8,128)(2,1)S(1)}, bf16[128,384]{1,0:T(8,128)(2,1)S(1)}, u32[]{:S(2)}, u32[]{:S(2)}) collective-permute-start(bf16[128,384]{1,0:T(8,128)(2,1)S(1)} %get-tuple-element.42), channel_id=1, source_target_pairs={{0,4},{1,5},{2,6},{3,7},{4,0},{5,1},{6,2},{7,3},{8,12},{9,13},{10,... | collective-permute-start | bytes 294920 | tf_op jit(solution)/shard_map/ppermute | solution.py:380
  10.5 15.2 %collective-permute-start.4 = (bf16[128,384]{1,0:T(8,128)(2,1)S(1)}, bf16[128,384]{1,0:T(8,128)(2,1)S(1)}, u32[]{:S(2)}, u32[]{:S(2)}) collective-permute-start(bf16[128,384]{1,0:T(8,128)(2,1)S(1)} %get-tuple-element.43), channel_id=1, source_target_pairs={{0,5},{1,4},{2,7},{3,6},{4,1},{5,0},{6,3},{7,2},{8,13},{9,12},{10,... | collective-permute-start | bytes 294920 | tf_op jit(solution)/shard_map/ppermute | solution.py:380
  11.8 13.9 %collective-permute-start.5 = (bf16[128,384]{1,0:T(8,128)(2,1)S(1)}, bf16[128,384]{1,0:T(8,128)(2,1)S(1)}, u32[]{:S(2)}, u32[]{:S(2)}) collective-permute-start(bf16[128,384]{1,0:T(8,128)(2,1)S(1)} %get-tuple-element.44), channel_id=1, source_target_pairs={{0,6},{1,7},{2,4},{3,5},{4,2},{5,3},{6,0},{7,1},{8,14},{9,15},{10,... | collective-permute-start | bytes 294920 | tf_op jit(solution)/shard_map/ppermute | solution.py:380
  15.4 10.3 %collective-permute-start.6 = (bf16[128,384]{1,0:T(8,128)(2,1)S(1)}, bf16[128,384]{1,0:T(8,128)(2,1)S(1)}, u32[]{:S(2)}, u32[]{:S(2)}) collective-permute-start(bf16[128,384]{1,0:T(8,128)(2,1)S(1)} %get-tuple-element.45), channel_id=1, source_target_pairs={{0,7},{1,6},{2,5},{3,4},{4,3},{5,2},{6,1},{7,0},{8,15},{9,14},{10,... | collective-permute-start | bytes 294920 | tf_op jit(solution)/shard_map/ppermute | solution.py:380
  26.5 26.1 %all-to-all-start = ((bf16[8,128,384]{2,1,0:T(8,128)(2,1)}), bf16[8,128,384]{2,1,0:T(8,128)(2,1)S(1)}, u32[]{:S(2)}, u32[]{:S(2)}) async-start(bf16[8,128,384]{2,1,0:T(8,128)(2,1)} %shard_map.106), calls=%async_computation | async-start | bytes 1572864 | tf_op jit(solution)/shard_map/all_to_all | solution.py:375
  33.6 1.9 %collective-permute-start.7 = (bf16[128,384]{1,0:T(8,128)(2,1)S(1)}, bf16[128,384]{1,0:T(8,128)(2,1)S(1)}, u32[]{:S(2)}, u32[]{:S(2)}) collective-permute-start(bf16[128,384]{1,0:T(8,128)(2,1)S(1)} %get-tuple-element.47), channel_id=1, source_target_pairs={{0,8},{1,9},{2,10},{3,11},{4,12},{5,13},{6,14},{7,15},{8,0},{9,1},... | collective-permute-start | bytes 294920 | tf_op jit(solution)/shard_map/ppermute | solution.py:380
  33.7 5.7 %collective-permute-start.8 = (bf16[128,384]{1,0:T(8,128)(2,1)S(1)}, bf16[128,384]{1,0:T(8,128)(2,1)S(1)}, u32[]{:S(2)}, u32[]{:S(2)}) collective-permute-start(bf16[128,384]{1,0:T(8,128)(2,1)S(1)} %get-tuple-element.48), channel_id=1, source_target_pairs={{0,16},{1,17},{2,18},{3,19},{4,20},{5,21},{6,22},{7,23},{8,24},{9,... | collective-permute-start | bytes 294920 | tf_op jit(solution)/shard_map/ppermute | solution.py:380
  35.3 5.3 %collective-permute-start.9 = (bf16[128,384]{1,0:T(8,128)(2,1)S(1)}, bf16[128,384]{1,0:T(8,128)(2,1)S(1)}, u32[]{:S(2)}, u32[]{:S(2)}) collective-permute-start(bf16[128,384]{1,0:T(8,128)(2,1)S(1)} %get-tuple-element.49), channel_id=1, source_target_pairs={{0,24},{1,25},{2,26},{3,27},{4,28},{5,29},{6,30},{7,31},{8,16},{9,... | collective-permute-start | bytes 294920 | tf_op jit(solution)/shard_map/ppermute | solution.py:380
  44.1 9.0 %collective-permute-start.10 = (bf16[128,384]{1,0:T(8,128)(2,1)S(1)}, bf16[128,384]{1,0:T(8,128)(2,1)S(1)}, u32[]{:S(2)}, u32[]{:S(2)}) collective-permute-start(bf16[128,384]{1,0:T(8,128)(2,1)S(1)} %get-tuple-element.51), channel_id=1, source_target_pairs={{0,8},{1,9},{2,10},{3,11},{4,12},{5,13},{6,14},{7,15},{8,0},{9,1},... | collective-permute-start | bytes 294920 | tf_op jit(solution)/shard_map/ppermute | solution.py:380
  44.7 8.4 %collective-permute-start.11 = (bf16[128,384]{1,0:T(8,128)(2,1)S(1)}, bf16[128,384]{1,0:T(8,128)(2,1)S(1)}, u32[]{:S(2)}, u32[]{:S(2)}) collective-permute-start(bf16[128,384]{1,0:T(8,128)(2,1)S(1)} %get-tuple-element.52), channel_id=1, source_target_pairs={{0,16},{1,17},{2,18},{3,19},{4,20},{5,21},{6,22},{7,23},{8,24},{9,... | collective-permute-start | bytes 294920 | tf_op jit(solution)/shard_map/ppermute | solution.py:380
  46.2 6.9 %collective-permute-start.12 = (bf16[128,384]{1,0:T(8,128)(2,1)S(1)}, bf16[128,384]{1,0:T(8,128)(2,1)S(1)}, u32[]{:S(2)}, u32[]{:S(2)}) collective-permute-start(bf16[128,384]{1,0:T(8,128)(2,1)S(1)} %get-tuple-element.53), channel_id=1, source_target_pairs={{0,24},{1,25},{2,26},{3,27},{4,28},{5,29},{6,30},{7,31},{8,16},{9,... | collective-permute-start | bytes 294920 | tf_op jit(solution)/shard_map/ppermute | solution.py:380
  54.8 36.3 %all-to-all-start.1 = ((bf16[8,128,384]{2,1,0:T(8,128)(2,1)}), bf16[8,128,384]{2,1,0:T(8,128)(2,1)S(1)}, u32[]{:S(2)}, u32[]{:S(2)}) async-start(bf16[8,128,384]{2,1,0:T(8,128)(2,1)} %shard_map.108), calls=%async_computation.1 | async-start | bytes 1572864 | tf_op jit(solution)/shard_map/all_to_all | solution.py:375
  58.5 1.9 %collective-permute-start.13 = (bf16[128,384]{1,0:T(8,128)(2,1)S(1)}, bf16[128,384]{1,0:T(8,128)(2,1)S(1)}, u32[]{:S(2)}, u32[]{:S(2)}) collective-permute-start(bf16[128,384]{1,0:T(8,128)(2,1)S(1)} %get-tuple-element.56), channel_id=1, source_target_pairs={{0,8},{1,9},{2,10},{3,11},{4,12},{5,13},{6,14},{7,15},{8,0},{9,1},... | collective-permute-start | bytes 294920 | tf_op jit(solution)/shard_map/ppermute | solution.py:380
  58.5 5.7 %collective-permute-start.14 = (bf16[128,384]{1,0:T(8,128)(2,1)S(1)}, bf16[128,384]{1,0:T(8,128)(2,1)S(1)}, u32[]{:S(2)}, u32[]{:S(2)}) collective-permute-start(bf16[128,384]{1,0:T(8,128)(2,1)S(1)} %get-tuple-element.57), channel_id=1, source_target_pairs={{0,16},{1,17},{2,18},{3,19},{4,20},{5,21},{6,22},{7,23},{8,24},{9,... | collective-permute-start | bytes 294920 | tf_op jit(solution)/shard_map/ppermute | solution.py:380
  60.0 5.4 %collective-permute-start.15 = (bf16[128,384]{1,0:T(8,128)(2,1)S(1)}, bf16[128,384]{1,0:T(8,128)(2,1)S(1)}, u32[]{:S(2)}, u32[]{:S(2)}) collective-permute-start(bf16[128,384]{1,0:T(8,128)(2,1)S(1)} %get-tuple-element.58), channel_id=1, source_target_pairs={{0,24},{1,25},{2,26},{3,27},{4,28},{5,29},{6,30},{7,31},{8,16},{9,... | collective-permute-start | bytes 294920 | tf_op jit(solution)/shard_map/ppermute | solution.py:380
  71.2 2.1 %collective-permute-start.16 = (bf16[96,96]{1,0:T(8,128)(2,1)S(1)}, bf16[96,96]{1,0:T(8,128)(2,1)S(1)}, u32[]{:S(2)}, u32[]{:S(2)}) collective-permute-start(bf16[96,96]{1,0:T(8,128)(2,1)S(1)} %get-tuple-element.63), channel_id=1, source_target_pairs={{0,8},{8,0},{16,24},{24,16},{1,9},{9,1},{17,25},{25,17},{2,10},{10... | collective-permute-start | bytes 55304 | tf_op jit(solution)/shard_map/ppermute | solution.py:380
  71.9 3.8 %collective-permute-start.17 = (bf16[96,96]{1,0:T(8,128)(2,1)S(1)}, bf16[96,96]{1,0:T(8,128)(2,1)S(1)}, u32[]{:S(2)}, u32[]{:S(2)}) collective-permute-start(bf16[96,96]{1,0:T(8,128)(2,1)S(1)} %get-tuple-element.64), channel_id=1, source_target_pairs={{0,16},{8,24},{16,0},{24,8},{1,17},{9,25},{17,1},{25,9},{2,18},{10... | collective-permute-start | bytes 55304 | tf_op jit(solution)/shard_map/ppermute | solution.py:380
  73.3 3.5 %collective-permute-start.18 = (bf16[96,96]{1,0:T(8,128)(2,1)S(1)}, bf16[96,96]{1,0:T(8,128)(2,1)S(1)}, u32[]{:S(2)}, u32[]{:S(2)}) collective-permute-start(bf16[96,96]{1,0:T(8,128)(2,1)S(1)} %get-tuple-element.65), channel_id=1, source_target_pairs={{0,24},{8,16},{16,8},{24,0},{1,25},{9,17},{17,9},{25,1},{2,26},{10... | collective-permute-start | bytes 55304 | tf_op jit(solution)/shard_map/ppermute | solution.py:380
  78.4 11.4 %collective-permute-start.19 = (bf16[128,384]{1,0:T(8,128)(2,1)S(1)}, bf16[128,384]{1,0:T(8,128)(2,1)S(1)}, u32[]{:S(2)}, u32[]{:S(2)}) collective-permute-start(bf16[128,384]{1,0:T(8,128)(2,1)S(1)} %get-tuple-element.67), channel_id=1, source_target_pairs={{0,8},{1,9},{2,10},{3,11},{4,12},{5,13},{6,14},{7,15},{8,0},{9,1},... | collective-permute-start | bytes 294920 | tf_op jit(solution)/shard_map/ppermute | solution.py:380
  78.5 11.3 %collective-permute-start.20 = (bf16[128,384]{1,0:T(8,128)(2,1)S(1)}, bf16[128,384]{1,0:T(8,128)(2,1)S(1)}, u32[]{:S(2)}, u32[]{:S(2)}) collective-permute-start(bf16[128,384]{1,0:T(8,128)(2,1)S(1)} %get-tuple-element.68), channel_id=1, source_target_pairs={{0,16},{1,17},{2,18},{3,19},{4,20},{5,21},{6,22},{7,23},{8,24},{9,... | collective-permute-start | bytes 294920 | tf_op jit(solution)/shard_map/ppermute | solution.py:380
  79.2 10.6 %collective-permute-start.21 = (bf16[128,384]{1,0:T(8,128)(2,1)S(1)}, bf16[128,384]{1,0:T(8,128)(2,1)S(1)}, u32[]{:S(2)}, u32[]{:S(2)}) collective-permute-start(bf16[128,384]{1,0:T(8,128)(2,1)S(1)} %get-tuple-element.69), channel_id=1, source_target_pairs={{0,24},{1,25},{2,26},{3,27},{4,28},{5,29},{6,30},{7,31},{8,16},{9,... | collective-permute-start | bytes 294920 | tf_op jit(solution)/shard_map/ppermute | solution.py:380
  80.3 5.7 %collective-permute-start.24 = (bf16[96,96]{1,0:T(8,128)(2,1)S(1)}, bf16[96,96]{1,0:T(8,128)(2,1)S(1)}, u32[]{:S(2)}, u32[]{:S(2)}) collective-permute-start(bf16[96,96]{1,0:T(8,128)(2,1)S(1)} %shard_map.111.rest_0_.refs_0_), channel_id=1, source_target_pairs={{0,6},{1,7},{2,4},{3,5},{4,2},{5,3},{6,0},{7,1},{8,14},{9,15},{10,... | collective-permute-start | bytes 55304 | tf_op jit(solution)/shard_map/ppermute | solution.py:521
  84.0 4.7 %collective-permute-start.23 = (bf16[96,96]{1,0:T(8,128)(2,1)S(1)}, bf16[96,96]{1,0:T(8,128)(2,1)S(1)}, u32[]{:S(2)}, u32[]{:S(2)}) collective-permute-start(bf16[96,96]{1,0:T(8,128)(2,1)S(1)} %shard_map.111.rest_0_.refs_0_), channel_id=1, source_target_pairs={{0,4},{1,5},{2,6},{3,7},{4,0},{5,1},{6,2},{7,3},{8,12},{9,13},{10,... | collective-permute-start | bytes 55304 | tf_op jit(solution)/shard_map/ppermute | solution.py:521
  86.0 3.8 %collective-permute-start.22 = (bf16[96,96]{1,0:T(8,128)(2,1)S(1)}, bf16[96,96]{1,0:T(8,128)(2,1)S(1)}, u32[]{:S(2)}, u32[]{:S(2)}) collective-permute-start(bf16[96,96]{1,0:T(8,128)(2,1)S(1)} %shard_map.111.rest_0_.refs_0_), channel_id=1, source_target_pairs={{0,2},{1,3},{2,0},{3,1},{4,6},{5,7},{6,4},{7,5},{8,10},{9,11},{10,... | collective-permute-start | bytes 55304 | tf_op jit(solution)/shard_map/ppermute | solution.py:521
  91.1 24.4 %all-to-all-start.2 = ((bf16[8,128,384]{2,1,0:T(8,128)(2,1)}), bf16[8,128,384]{2,1,0:T(8,128)(2,1)S(1)}, u32[]{:S(2)}, u32[]{:S(2)}) async-start(bf16[8,128,384]{2,1,0:T(8,128)(2,1)} %shard_map.114), calls=%async_computation.2 | async-start | bytes 1572864 | tf_op jit(solution)/shard_map/all_to_all | solution.py:375
  97.0 8.3 %collective-permute-start.25 = (bf16[4,96,96]{2,1,0:T(8,128)(2,1)S(1)}, bf16[4,96,96]{2,1,0:T(8,128)(2,1)S(1)}, u32[]{:S(2)}, u32[]{:S(2)}) collective-permute-start(bf16[4,96,96]{2,1,0:T(8,128)(2,1)S(1)} %shard_map.113.rest_4_.near), channel_id=1, source_target_pairs={{0,1},{1,0},{2,3},{3,2},{4,5},{5,4},{6,7},{7,6},{8,9},{9,8},{10,11... | collective-permute-start | bytes 221192 | tf_op jit(solution)/shard_map/ppermute | solution.py:528
  105.3 5.7 %collective-permute-start.27 = (bf16[8,96,96]{2,1,0:T(8,128)(2,1)S(1)}, bf16[8,96,96]{2,1,0:T(8,128)(2,1)S(1)}, u32[]{:S(2)}, u32[]{:S(2)}) collective-permute-start(bf16[8,96,96]{2,1,0:T(8,128)(2,1)S(1)} %shard_map.116.rest_0_), channel_id=1, source_target_pairs={{0,16},{8,24},{16,0},{24,8},{1,17},{9,25},{17,1},{25,9},{2,18},{10... | collective-permute-start | bytes 442376 | tf_op jit(solution)/shard_map/ppermute | solution.py:535
  106.3 4.8 %collective-permute-start.26 = (bf16[8,96,96]{2,1,0:T(8,128)(2,1)S(1)}, bf16[8,96,96]{2,1,0:T(8,128)(2,1)S(1)}, u32[]{:S(2)}, u32[]{:S(2)}) collective-permute-start(bf16[8,96,96]{2,1,0:T(8,128)(2,1)S(1)} %shard_map.116.rest_0_), channel_id=1, source_target_pairs={{0,8},{8,0},{16,24},{24,16},{1,9},{9,1},{17,25},{25,17},{2,10},{10... | collective-permute-start | bytes 442376 | tf_op jit(solution)/shard_map/ppermute | solution.py:535
  111.1 1.4 %collective-permute-start.28 = (bf16[8,96,96]{2,1,0:T(8,128)(2,1)S(1)}, bf16[8,96,96]{2,1,0:T(8,128)(2,1)S(1)}, u32[]{:S(2)}, u32[]{:S(2)}) collective-permute-start(bf16[8,96,96]{2,1,0:T(8,128)(2,1)S(1)} %collective-permute-done.27.rest_2_), channel_id=1, source_target_pairs={{0,8},{8,0},{16,24},{24,16},{1,9},{9,1},{17,25},{25,17},{2,10},{10... | collective-permute-start | bytes 442376 | tf_op jit(solution)/shard_map/ppermute | solution.py:535
  (23 other events, 126.6 us)
where the time goes:
time: 117 us
  waiting for transfers between devices  46.5 us (40%)
  starting transfers between devices  45.9 us (39%)
  Pallas kernels  19.2 us (16%)
  local copies, waits for them, and re-layouts  4.08 us (3%)
    ppermute x22, starting transfers between devices, swap(): lax.ppermute(piece, axes, partners(offset))  22.4 us
    ppermute x22, waiting for transfers between devices, swap(): lax.ppermute(piece, axes, partners(offset))  22.2 us
    pallas_call x15, Pallas kernels, kernel_call(): pl.pallas_call(body, out_shape=out_shape, in_specs=in_specs, out_specs=[s...  19.2 us
    all_to_all x3, starting transfers between devices, exchange(): lax.all_to_all(source, 'lon', split_axis=0, concat_axis=0, tiled=True)  16.2 us
    all_to_all x3, waiting for transfers between devices, exchange(): lax.all_to_all(source, 'lon', split_axis=0, concat_axis=0, tiled=True)  6.7 us
    ppermute x1, waiting for transfers between devices, shards(): lax.ppermute(near, 'lon', lon_pairs(1))  6.29 us
    ppermute x3, waiting for transfers between devices, shards(): moved = lax.ppermute(gathered[offset], 'lat', line_pairs(lat_count)(step))  6.2 us
    ppermute x3, waiting for transfers between devices, shards(): lax.ppermute(own_share, 'lon', lon_pairs(far))  5.12 us
  transfers between devices with their start and end apart: 32, of which 15 were waited for; matrix products, arithmetic and copies ran while one was open for 0% of the time, Pallas kernels for 14%

commit v1 on v0

--- a/solution.py
+++ b/solution.py
@@ -83,9 +83,23 @@
     )(source, *anchors)
 
 
-def pack_body(rows_sub, subs, own, source, *rest):
-    sent, slots = rest[:-1], rest[-1]
+def group_copies(source, target, sems):
+    rows = target.shape[0] // RQ
+    return [
+        pltpu.make_async_copy(
+            source.at[pl.ds(group * rows, rows)], target.at[pl.ds(group * rows, rows)], sems.at[group]
+        )
+        for group in range(RQ)
+    ]
+
+
+def pack_body(rows_sub, subs, own, field, *rest):
+    sent, (slots, source, sems) = rest[:-3], rest[-3:]
     cols = source.shape[1]
+    loads = group_copies(field, source, sems)
+    for copy in loads:
+        copy.start()
+    finish(loads)
     for sub in range(subs):
         for block in range(NB):
             pieces = []
@@ -97,21 +111,27 @@
     deal(sent, slots, own[0])
 
 
-def unpack_body(rows_sub, subs, own, base, *rest):
-    received, (result, slots) = rest[:-2], rest[-2:]
+def unpack_body(rows_sub, subs, own, packed, field, result, slots, base, mixed, load_sems, save_sems):
     cols = base.shape[1]
-    place(slots, received, own[0])
-    for sub in range(subs):
-        for group in range(RQ):
+    loads = group_copies(field, base, load_sems)
+    saves = group_copies(mixed, result, save_sems)
+    for copy in loads:
+        copy.start()
+    place(slots, [packed], own[0])
+    for group in range(RQ):
+        loads[group].wait()
+        for sub in range(subs):
             row = (group * subs + sub) * rows_sub
             pieces = [
                 slots[sub * NB + block, :, group * BS : (group + 1) * BS] for block in range(NB)
             ]
             update = jnp.concatenate(pieces, axis=1).reshape(rows_sub, cols, NB * BS)
             old = base[row : row + rows_sub]
-            result[row : row + rows_sub] = (
+            mixed[row : row + rows_sub] = (
                 old.astype(jnp.float32) + update.astype(jnp.float32)
             ).astype(jnp.bfloat16)
+        saves[group].start()
+    finish(saves)
 
 
 def product(left, right):
@@ -258,15 +278,21 @@
             copies[-1].start()
     finish(loads)
     complex_weights(real_imag, full)
-    for tile in range(kept // pack_modes):
-        outs = []
-        for index in range(tile * pack_modes, (tile + 1) * pack_modes):
-            act, _, _ = gelu(product(spec[index, :, :WIDE], full[0]))
-            post = product(act, full[1])
-            weight = mode_weight(first_mode[0], index)
-            shrunk = post - shrink_level * jnp.tanh(post / shrink_level)
-            outs.append((weight * shrunk).astype(jnp.bfloat16))
-        lat_inverse(inverse, outs, slots, tile, deep)
+    count = max(pack_modes, 2)
+    for start in range(0, kept, count):
+        values = spec[start : start + count].reshape(count * rows, -1)[:, :WIDE]
+        act, _, _ = gelu(product(values, full[0]))
+        post = product(act, full[1])
+        shrunk = post - shrink_level * jnp.tanh(post / shrink_level)
+        outs = [
+            (mode_weight(first_mode[0], start + at) * shrunk[at * rows : (at + 1) * rows]).astype(
+                jnp.bfloat16
+            )
+            for at in range(count)
+        ]
+        for at in range(0, count, pack_modes):
+            tile = (start + at) // pack_modes
+            lat_inverse(inverse, outs[at : at + pack_modes], slots, tile, deep)
     deal(sent, slots, own)
     finish(copies)
 
@@ -276,7 +302,7 @@
 ):
     received, rest = rest[:members], rest[members:]
     weights, saved, result, combined, rest = rest[:2], rest[2], rest[3], rest[4], rest[5:]
-    parts, (slots, grads, cots, spec, real_imag, full, weight_sems, load_sems) = (
+    parts, (slots, grads, cots, hidden, spec, real_imag, full, weight_sems, load_sems) = (
         rest[:shares],
         rest[shares:],
     )
@@ -293,28 +319,35 @@
     lat = table[...]
     for tile in range(kept // pack_modes):
         for inner, cot in enumerate(lat_forward(lat, slots, tile, deep, rows)):
-            cots[tile * pack_modes + inner] = cot
+            index = tile * pack_modes + inner
+            weight = mode_weight(first_mode[0], index)
+            cots[index] = (weight * cot.astype(jnp.float32)).astype(jnp.bfloat16)
     finish(loads)
     complex_weights(real_imag, full)
     combined[...] = full[0]
-    total_first = jnp.zeros((WIDE, WIDE), jnp.float32)
-    total_second = jnp.zeros((WIDE, WIDE), jnp.float32)
-    for index in range(kept):
-        spec_loads[index].wait()
-        values = spec[index, :, :WIDE]
+    count = max(pack_modes, 2)
+    for start in range(0, kept, count):
+        group = pl.ds(start, count)
+        finish(spec_loads[start : start + count])
+        values = spec[group].reshape(count * rows, -1)[:, :WIDE]
         pre = product(values, full[0])
         act, squared, tangent = gelu(pre)
         slope = 0.5 * (1.0 + tangent) + 0.5 * pre * (1.0 - tangent * tangent) * gelu_coeff * (
             1.0 + 3.0 * 0.044715 * squared
         )
         ratio = jnp.tanh(product(act, full[1]) / shrink_level)
-        weight = mode_weight(first_mode[0], index)
-        cot = cots[index].astype(jnp.float32)
-        grad_post = (weight * cot * (ratio * ratio)).astype(jnp.bfloat16)
+        cot = cots[group].reshape(count * rows, WIDE).astype(jnp.float32)
+        grad_post = (cot * (ratio * ratio)).astype(jnp.bfloat16)
         grad_pre = (product_back(grad_post, full[1]) * slope).astype(jnp.bfloat16)
-        result[index] = grad_pre
-        total_second += product_outer(act, grad_post)
-        total_first += product_outer(values, grad_pre)
+        result[group] = grad_pre.reshape(count, rows, WIDE)
+        hidden[group] = act.reshape(count, rows, WIDE)
+        cots[group] = grad_post.reshape(count, rows, WIDE)
+    modes = kept * rows
+    grads_pre = result[...].reshape(modes, WIDE)
+    total_first = product_outer(spec[...].reshape(modes, -1)[:, :WIDE], grads_pre)
+    total_second = product_outer(
+        hidden[...].reshape(modes, WIDE), cots[...].reshape(modes, WIDE)
+    )
     share = grads.shape[1]
     for slot, total in enumerate((total_first, total_second)):
         real = (total[:BS, :BS] + total[BS:, BS:]) * factor
@@ -432,12 +465,15 @@
 
     def pack(source, sent):
         body = functools.partial(pack_body, rows_sub, subs)
-        return kernel_call(body, sent, [lon_index], [source], [lon_slots])
+        scratch = [lon_slots, pltpu.VMEM(source.shape, bf16), pltpu.SemaphoreType.DMA((RQ,))]
+        return kernel_call(body, sent, [lon_index], [], scratch, far=[source])
 
     def unpack(source, base):
         body = functools.partial(unpack_body, rows_sub, subs)
-        result = array(base.shape, bf16)
-        return kernel_call(body, [result], [lon_index], [base, source], [lon_slots])[0]
+        scratch = [lon_slots] + [pltpu.VMEM(base.shape, bf16)] * 2
+        scratch += [pltpu.SemaphoreType.DMA((RQ,))] * 2
+        result = pltpu.HBM(base.shape, bf16)
+        return kernel_call(body, [result], [lon_index], [source], scratch, far=[base])[0]
 
     def to_spectra(pieces, anchors=()):
         return kernel_call(
@@ -470,7 +506,7 @@
     ]
 
     field = swap(pack(features, [lon_piece] * lon_count), "lon", line_pairs(lon_count))
-    field_cot = exchange(gate(pack(cotangent, [lon_whole])[0], field))
+    field_cot = exchange(gate(pack(cotangent, [lon_whole])[0], field[1:]))
     results = kernel_call(
         functools.partial(forward_body, members, pack_modes),
         [mid_piece] * members + [pltpu.HBM(modes, bf16), array((8, 128), f32)],
@@ -495,6 +531,7 @@
             mid_slots,
             pltpu.VMEM((lat_count, share, BS), bf16),
             pltpu.VMEM(wide, bf16),
+            pltpu.VMEM(wide, bf16),
             *mid_scratch,
         ],
         far=weights + [saved],

time: 117 us -> 117 us (level)
  Pallas kernels: 19.2 us -> 22.1 us
  waiting for transfers between devices: 46.5 us -> 44.6 us
  local copies, waits for them, and re-layouts: 4.08 us -> 2.65 us
    pallas_call x15, Pallas kernels: 19.2 us -> 22.1 us  [kernel_call(): pl.pallas_call(body, out_shape=out_shape, in_specs=in_specs, out_specs=[s...]
    unnamed x46 -> x36, local copies, waits for them, and re-layouts: 4.08 us -> 2.65 us
    ppermute x22, waiting for transfers between devices: 22.2 us -> 20.9 us  [swap(): lax.ppermute(piece, axes, partners(offset))]
  transfers between devices with their start and end apart: 32 -> 32, of which waited for: 15 -> 14; matrix products, arithmetic and copies ran while one was open for 0% -> 0% of each run, Pallas kernels for 14% -> 15%
where the time goes in v1:
time: 117 us; the launch traced here: 116 us
  starting transfers between devices  45.7 us (39%)
  waiting for transfers between devices  44.6 us (38%)
  Pallas kernels  22.1 us (19%)
  local copies, waits for them, and re-layouts  2.65 us (2%)
    ppermute x22, starting transfers between devices, swap(): lax.ppermute(piece, axes, partners(offset))  22.4 us
    pallas_call x15, Pallas kernels, kernel_call(): pl.pallas_call(body, out_shape=out_shape, in_specs=in_specs, out_specs=[s...  22.1 us
    ppermute x22, waiting for transfers between devices, swap(): lax.ppermute(piece, axes, partners(offset))  20.9 us
    all_to_all x3, starting transfers between devices, exchange(): lax.all_to_all(source, 'lon', split_axis=0, concat_axis=0, tiled=True)  15.8 us
    ppermute x1, waiting for transfers between devices, shards(): lax.ppermute(near, 'lon', lon_pairs(1))  6.29 us
    all_to_all x3, waiting for transfers between devices, exchange(): lax.all_to_all(source, 'lon', split_axis=0, concat_axis=0, tiled=True)  6.18 us
    ppermute x3, waiting for transfers between devices, shards(): moved = lax.ppermute(gathered[offset], 'lat', line_pairs(lat_count)(step))  6.14 us
    ppermute x3, waiting for transfers between devices, shards(): lax.ppermute(own_share, 'lon', lon_pairs(far))  5.06 us
  transfers between devices with their start and end apart: 32, of which 14 were waited for; matrix products, arithmetic and copies ran while one was open for 0% of the time, Pallas kernels for 15%

profile of v1, /device:TPU:0, one launch (start us, length us, event | category | flops | bytes accessed | tf_op | source)
XLA Modules:
  0.0 116.1 jit_solution(2870470368890481172)
XLA Ops:
  0.6 1.7 %shard_map.102 = (bf16[128,384]{1,0:T(8,128)(2,1)S(1)}, bf16[128,384]{1,0:T(8,128)(2,1)S(1)}, bf16[128,384]{1,0:T(8,128)(2,1)S(1)}, bf16[128,384]{1,0:T(8,128)(2...) custom-call(s32[1]{0:T(128)} %bitcast.own.own_in, ...), custom_call_target="tpu_custom_call" | custom-call | tf_op jit(solution)/shard_map/pallas_call | solution.py:65
  2.3 3.0 %collective-permute-start = (bf16[128,384]{1,0:T(8,128)(2,1)S(1)}, bf16[128,384]{1,0:T(8,128)(2,1)S(1)}, u32[]{:S(2)}, u32[]{:S(2)}) collective-permute-start(bf16[128,384]{1,0:T(8,128)(2,1)S(1)} %get-tuple-element.39), channel_id=1, source_target_pairs={{0,1},{1,0},{2,3},{3,2},{4,5},{5,4},{6,7},{7,6},{8,9},{9,8},{10,11... | collective-permute-start | bytes 294920 | tf_op jit(solution)/shard_map/ppermute | solution.py:413
  5.4 1.6 %collective-permute-start.1 = (bf16[128,384]{1,0:T(8,128)(2,1)S(1)}, bf16[128,384]{1,0:T(8,128)(2,1)S(1)}, u32[]{:S(2)}, u32[]{:S(2)}) collective-permute-start(bf16[128,384]{1,0:T(8,128)(2,1)S(1)} %get-tuple-element.40), channel_id=1, source_target_pairs={{0,2},{1,3},{2,0},{3,1},{4,6},{5,7},{6,4},{7,5},{8,10},{9,11},{10,... | collective-permute-start | bytes 294920 | tf_op jit(solution)/shard_map/ppermute | solution.py:413
  7.0 3.0 %collective-permute-start.3 = (bf16[128,384]{1,0:T(8,128)(2,1)S(1)}, bf16[128,384]{1,0:T(8,128)(2,1)S(1)}, u32[]{:S(2)}, u32[]{:S(2)}) collective-permute-start(bf16[128,384]{1,0:T(8,128)(2,1)S(1)} %get-tuple-element.42), channel_id=1, source_target_pairs={{0,4},{1,5},{2,6},{3,7},{4,0},{5,1},{6,2},{7,3},{8,12},{9,13},{10,... | collective-permute-start | bytes 294920 | tf_op jit(solution)/shard_map/ppermute | solution.py:413
  9.9 1.3 %collective-permute-start.4 = (bf16[128,384]{1,0:T(8,128)(2,1)S(1)}, bf16[128,384]{1,0:T(8,128)(2,1)S(1)}, u32[]{:S(2)}, u32[]{:S(2)}) collective-permute-start(bf16[128,384]{1,0:T(8,128)(2,1)S(1)} %get-tuple-element.43), channel_id=1, source_target_pairs={{0,5},{1,4},{2,7},{3,6},{4,1},{5,0},{6,3},{7,2},{8,13},{9,12},{10,... | collective-permute-start | bytes 294920 | tf_op jit(solution)/shard_map/ppermute | solution.py:413
  11.2 3.6 %collective-permute-start.5 = (bf16[128,384]{1,0:T(8,128)(2,1)S(1)}, bf16[128,384]{1,0:T(8,128)(2,1)S(1)}, u32[]{:S(2)}, u32[]{:S(2)}) collective-permute-start(bf16[128,384]{1,0:T(8,128)(2,1)S(1)} %get-tuple-element.44), channel_id=1, source_target_pairs={{0,6},{1,7},{2,4},{3,5},{4,2},{5,3},{6,0},{7,1},{8,14},{9,15},{10,... | collective-permute-start | bytes 294920 | tf_op jit(solution)/shard_map/ppermute | solution.py:413
  14.9 1.7 %shard_map.105.refs_0_ = bf16[8,128,384]{2,1,0:T(8,128)(2,1)S(1)} custom-call(s32[1]{0:T(128)} %bitcast.own.own_in, bf16[32,16,768]{2,1,0:T(8,128)(2,1)} %field.7), custom_call_target="tpu_custom_call" | custom-call | tf_op jit(solution)/shard_map/pallas_call | solution.py:65
  17.5 7.6 %collective-permute-done.4.rest_5_.refs_5_ = bf16[128,384]{1,0:T(8,128)(2,1)S(1)} collective-permute-done((bf16[128,384]{1,0:T(8,128)(2,1)S(1)}, bf16[128,384]{1,0:T(8,128)(2,1)S(1)}, u32[]{:S(2)}, u32[]{:S(2)}) %collective-permute-start.4) | collective-permute-done | bytes 98336 | tf_op jit(solution)/shard_map/ppermute | solution.py:413
  26.5 5.9 %all-to-all-start = ((bf16[8,128,384]{2,1,0:T(8,128)(2,1)}), bf16[8,128,384]{2,1,0:T(8,128)(2,1)S(1)}, u32[]{:S(2)}, u32[]{:S(2)}) async-start(bf16[8,128,384]{2,1,0:T(8,128)(2,1)} %shard_map.106), calls=%async_computation | async-start | bytes 1572864 | tf_op jit(solution)/shard_map/all_to_all | solution.py:408
  33.2 1.6 %collective-permute-start.8 = (bf16[128,384]{1,0:T(8,128)(2,1)S(1)}, bf16[128,384]{1,0:T(8,128)(2,1)S(1)}, u32[]{:S(2)}, u32[]{:S(2)}) collective-permute-start(bf16[128,384]{1,0:T(8,128)(2,1)S(1)} %get-tuple-element.48), channel_id=1, source_target_pairs={{0,16},{1,17},{2,18},{3,19},{4,20},{5,21},{6,22},{7,23},{8,24},{9,... | collective-permute-start | bytes 294920 | tf_op jit(solution)/shard_map/ppermute | solution.py:413
  35.0 3.8 %collective-permute-done.8.rest_2_ = bf16[128,384]{1,0:T(8,128)(2,1)S(1)} collective-permute-done((bf16[128,384]{1,0:T(8,128)(2,1)S(1)}, bf16[128,384]{1,0:T(8,128)(2,1)S(1)}, u32[]{:S(2)}, u32[]{:S(2)}) %collective-permute-start.8) | collective-permute-done | bytes 98336 | tf_op jit(solution)/shard_map/ppermute | solution.py:413
  40.0 3.7 %shard_map.104 = (bf16[128,384]{1,0:T(8,128)(2,1)S(1)}, bf16[128,384]{1,0:T(8,128)(2,1)S(1)}, bf16[128,384]{1,0:T(8,128)(2,1)S(1)}, bf16[128,384]{1,0:T(8,128)(2...) custom-call(s32[1]{0:T(128)} %bitcast.1.own_out.member.own_in, s32[1]{0:T(128)} %bitcast.2.first_mode, ...), custom_call_target="tpu_custom_call" | custom-call | tf_op jit(solution)/shard_map/pallas_call | solution.py:65
  44.4 1.5 %collective-permute-start.11 = (bf16[128,384]{1,0:T(8,128)(2,1)S(1)}, bf16[128,384]{1,0:T(8,128)(2,1)S(1)}, u32[]{:S(2)}, u32[]{:S(2)}) collective-permute-start(bf16[128,384]{1,0:T(8,128)(2,1)S(1)} %get-tuple-element.52), channel_id=1, source_target_pairs={{0,16},{1,17},{2,18},{3,19},{4,20},{5,21},{6,22},{7,23},{8,24},{9,... | collective-permute-start | bytes 294920 | tf_op jit(solution)/shard_map/ppermute | solution.py:413
  45.9 6.2 %all-to-all-done.rest_0_ = bf16[8,128,384]{2,1,0:T(8,128)(2,1)S(1)} async-done(((bf16[8,128,384]{2,1,0:T(8,128)(2,1)}), bf16[8,128,384]{2,1,0:T(8,128)(2,1)S(1)}, u32[]{:S(2)}, u32[]{:S(2)}) %all-to-all-start) | async-done | bytes 786464 | tf_op jit(solution)/shard_map/all_to_all | solution.py:408
  54.2 4.0 %all-to-all-start.1 = ((bf16[8,128,384]{2,1,0:T(8,128)(2,1)}), bf16[8,128,384]{2,1,0:T(8,128)(2,1)S(1)}, u32[]{:S(2)}, u32[]{:S(2)}) async-start(bf16[8,128,384]{2,1,0:T(8,128)(2,1)} %shard_map.108), calls=%async_computation.1 | async-start | bytes 1572864 | tf_op jit(solution)/shard_map/all_to_all | solution.py:408
  58.2 1.3 %collective-permute-start.14 = (bf16[128,384]{1,0:T(8,128)(2,1)S(1)}, bf16[128,384]{1,0:T(8,128)(2,1)S(1)}, u32[]{:S(2)}, u32[]{:S(2)}) collective-permute-start(bf16[128,384]{1,0:T(8,128)(2,1)S(1)} %get-tuple-element.57), channel_id=1, source_target_pairs={{0,16},{1,17},{2,18},{3,19},{4,20},{5,21},{6,22},{7,23},{8,24},{9,... | collective-permute-start | bytes 294920 | tf_op jit(solution)/shard_map/ppermute | solution.py:413
  60.1 3.8 %collective-permute-done.14.rest_2_ = bf16[128,384]{1,0:T(8,128)(2,1)S(1)} collective-permute-done((bf16[128,384]{1,0:T(8,128)(2,1)S(1)}, bf16[128,384]{1,0:T(8,128)(2,1)S(1)}, u32[]{:S(2)}, u32[]{:S(2)}) %collective-permute-start.14) | collective-permute-done | bytes 98336 | tf_op jit(solution)/shard_map/ppermute | solution.py:413
  65.0 4.1 %shard_map.110 = (bf16[8,128,192]{2,1,0:T(8,128)(2,1)S(1)}, bf16[192,192]{1,0:T(8,128)(2,1)S(1)}, bf16[96,96]{1,0:T(8,128)(2,1)S(1)}, bf16[96,96]{1,0:T(8,128)(2...) custom-call(s32[1]{0:T(128)} %bitcast.1.own_out.member.own_in, s32[1]{0:T(128)} %bitcast.2.first_mode, ...), custom_call_target="tpu_custom_call" | custom-call | tf_op jit(solution)/shard_map/pallas_call | solution.py:65
  71.2 2.4 %collective-permute-done.17.refs_2_ = bf16[96,96]{1,0:T(8,128)(2,1)S(1)} collective-permute-done((bf16[96,96]{1,0:T(8,128)(2,1)S(1)}, bf16[96,96]{1,0:T(8,128)(2,1)S(1)}, u32[]{:S(2)}, u32[]{:S(2)}) %collective-permute-start.17) | collective-permute-done | bytes 18464 | tf_op jit(solution)/shard_map/ppermute | solution.py:413
  74.4 1.6 %shard_map.112 = (bf16[128,384]{1,0:T(8,128)(2,1)S(1)}, bf16[128,384]{1,0:T(8,128)(2,1)S(1)}, bf16[128,384]{1,0:T(8,128)(2,1)S(1)}, bf16[128,384]{1,0:T(8,128)(2,1)S(1)}) custom-call(s32[1]{0:T(128)} %bitcast.1.own_out.member.own_in, bf16[256,256]{1,0:T(8,128)(2,1)S(1)} %copy-done.1, bf16[8,128,192]{2,1,0:T(8,128)(2,1)S(1)} %get-tuple-element.60.grad_pre, ...), custom_call_target="tpu_custom_call" | custom-call | tf_op jit(solution)/shard_map/pallas_call | solution.py:65
  78.0 3.8 %collective-permute-start.24 = (bf16[96,96]{1,0:T(8,128)(2,1)S(1)}, bf16[96,96]{1,0:T(8,128)(2,1)S(1)}, u32[]{:S(2)}, u32[]{:S(2)}) collective-permute-start(bf16[96,96]{1,0:T(8,128)(2,1)S(1)} %shard_map.111.rest_0_.refs_0_), channel_id=1, source_target_pairs={{0,6},{1,7},{2,4},{3,5},{4,2},{5,3},{6,0},{7,1},{8,14},{9,15},{10,... | collective-permute-start | bytes 55304 | tf_op jit(solution)/shard_map/ppermute | solution.py:558
  81.7 1.9 %collective-permute-done.24.refs_3_ = bf16[96,96]{1,0:T(8,128)(2,1)S(1)} collective-permute-done((bf16[96,96]{1,0:T(8,128)(2,1)S(1)}, bf16[96,96]{1,0:T(8,128)(2,1)S(1)}, u32[]{:S(2)}, u32[]{:S(2)}) %collective-permute-start.24) | collective-permute-done | bytes 18464 | tf_op jit(solution)/shard_map/ppermute | solution.py:558
  84.3 2.2 %collective-permute-done.23.refs_2_ = bf16[96,96]{1,0:T(8,128)(2,1)S(1)} collective-permute-done((bf16[96,96]{1,0:T(8,128)(2,1)S(1)}, bf16[96,96]{1,0:T(8,128)(2,1)S(1)}, u32[]{:S(2)}, u32[]{:S(2)}) %collective-permute-start.23) | collective-permute-done | bytes 18464 | tf_op jit(solution)/shard_map/ppermute | solution.py:558
  87.5 1.2 %shard_map.114 = bf16[8,128,384]{2,1,0:T(8,128)(2,1)} custom-call(s32[1]{0:T(128)} %bitcast.1.own_out.member.own_in, bf16[512,256]{1,0:T(8,128)(2,1)S(1)} %copy-done.3, bf16[128,384]{1,0:T(8,128)(2,1)S(1)} %get-tuple-element.66.rest_0_, bf16[128,384]{1,0:T(8,128)(2,1)S(1)} %collective-permute-done.19.rest_1_, ...), custom_call_target="tpu_custom_call" | custom-call | tf_op jit(solution)/shard_map/pallas_call | solution.py:65
  88.8 5.9 %all-to-all-start.2 = ((bf16[8,128,384]{2,1,0:T(8,128)(2,1)}), bf16[8,128,384]{2,1,0:T(8,128)(2,1)S(1)}, u32[]{:S(2)}, u32[]{:S(2)}) async-start(bf16[8,128,384]{2,1,0:T(8,128)(2,1)} %shard_map.114), calls=%async_computation.2 | async-start | bytes 1572864 | tf_op jit(solution)/shard_map/all_to_all | solution.py:408
  94.7 2.0 %collective-permute-start.25 = (bf16[4,96,96]{2,1,0:T(8,128)(2,1)S(1)}, bf16[4,96,96]{2,1,0:T(8,128)(2,1)S(1)}, u32[]{:S(2)}, u32[]{:S(2)}) collective-permute-start(bf16[4,96,96]{2,1,0:T(8,128)(2,1)S(1)} %shard_map.113.rest_4_.near), channel_id=1, source_target_pairs={{0,1},{1,0},{2,3},{3,2},{4,5},{5,4},{6,7},{7,6},{8,9},{9,8},{10,11... | collective-permute-start | bytes 221192 | tf_op jit(solution)/shard_map/ppermute | solution.py:565
  96.7 6.3 %collective-permute-done.25.other = bf16[4,96,96]{2,1,0:T(8,128)(2,1)S(1)} collective-permute-done((bf16[4,96,96]{2,1,0:T(8,128)(2,1)S(1)}, bf16[4,96,96]{2,1,0:T(8,128)(2,1)S(1)}, u32[]{:S(2)}, u32[]{:S(2)}) %collective-permute-start.25) | collective-permute-done | bytes 73760 | tf_op jit(solution)/shard_map/ppermute | solution.py:565
  104.1 4.7 %collective-permute-done.27.rest_2_ = bf16[8,96,96]{2,1,0:T(8,128)(2,1)S(1)} collective-permute-done((bf16[8,96,96]{2,1,0:T(8,128)(2,1)S(1)}, bf16[8,96,96]{2,1,0:T(8,128)(2,1)S(1)}, u32[]{:S(2)}, u32[]{:S(2)}) %collective-permute-start.27) | collective-permute-done | bytes 147488 | tf_op jit(solution)/shard_map/ppermute | solution.py:572
  108.8 1.4 %collective-permute-done.28.rest_3_ = bf16[8,96,96]{2,1,0:T(8,128)(2,1)S(1)} collective-permute-done((bf16[8,96,96]{2,1,0:T(8,128)(2,1)S(1)}, bf16[8,96,96]{2,1,0:T(8,128)(2,1)S(1)}, u32[]{:S(2)}, u32[]{:S(2)}) %collective-permute-start.28) | collective-permute-done | bytes 147488 | tf_op jit(solution)/shard_map/ppermute | solution.py:572
  110.2 1.3 %shard_map.117 = (f32[2,8,96,96]{3,2,1,0:T(8,128)}, f32[2,8,96,96]{3,2,1,0:T(8,128)}) custom-call(s32[1]{0:T(128)} %bitcast.4.lat_own, bf16[8,96,96]{2,1,0:T(8,128)(2,1)S(1)} %shard_map.116.rest_0_, bf16[8,96,96]{2,1,0:T(8,128)(2,1)S(1)} %collective-permute-done.26.rest_1_, bf16[8,96,96]{2,1,0:T(8,128)(2,1)S(1)} %collective-permute-done.27.rest_2_, ...), custom_call_target="tpu_custom_call" | custom-call | tf_op jit(solution)/shard_map/pallas_call | solution.py:65
  111.5 2.3 %shard_map.109 = bf16[32,16,768]{2,1,0:T(8,128)(2,1)} custom-call(s32[1]{0:T(128)} %bitcast.own.own_in, bf16[8,128,384]{2,1,0:T(8,128)(2,1)S(1)} %all-to-all-done.1.packed, bf16[32,16,768]{2,1,0:T(8,128)(2,1)} %field.6), custom_call_target="tpu_custom_call" | custom-call | tf_op jit(solution)/shard_map/pallas_call | solution.py:65
  113.8 2.3 %shard_map.115 = bf16[32,16,768]{2,1,0:T(8,128)(2,1)} custom-call(s32[1]{0:T(128)} %bitcast.own.own_in, bf16[8,128,384]{2,1,0:T(8,128)(2,1)S(1)} %all-to-all-done.2.packed, bf16[32,16,768]{2,1,0:T(8,128)(2,1)} %field.7), custom_call_target="tpu_custom_call" | custom-call | tf_op jit(solution)/shard_map/pallas_call | solution.py:65
  (84 shorter events, 16.5 us)
Async XLA Ops:
  2.3 8.9 %collective-permute-start = (bf16[128,384]{1,0:T(8,128)(2,1)S(1)}, bf16[128,384]{1,0:T(8,128)(2,1)S(1)}, u32[]{:S(2)}, u32[]{:S(2)}) collective-permute-start(bf16[128,384]{1,0:T(8,128)(2,1)S(1)} %get-tuple-element.39), channel_id=1, source_target_pairs={{0,1},{1,0},{2,3},{3,2},{4,5},{5,4},{6,7},{7,6},{8,9},{9,8},{10,11... | collective-permute-start | bytes 294920 | tf_op jit(solution)/shard_map/ppermute | solution.py:413
  5.4 9.5 %collective-permute-start.1 = (bf16[128,384]{1,0:T(8,128)(2,1)S(1)}, bf16[128,384]{1,0:T(8,128)(2,1)S(1)}, u32[]{:S(2)}, u32[]{:S(2)}) collective-permute-start(bf16[128,384]{1,0:T(8,128)(2,1)S(1)} %get-tuple-element.40), channel_id=1, source_target_pairs={{0,2},{1,3},{2,0},{3,1},{4,6},{5,7},{6,4},{7,5},{8,10},{9,11},{10,... | collective-permute-start | bytes 294920 | tf_op jit(solution)/shard_map/ppermute | solution.py:413
  7.0 10.5 %collective-permute-start.2 = (bf16[128,384]{1,0:T(8,128)(2,1)S(1)}, bf16[128,384]{1,0:T(8,128)(2,1)S(1)}, u32[]{:S(2)}, u32[]{:S(2)}) collective-permute-start(bf16[128,384]{1,0:T(8,128)(2,1)S(1)} %get-tuple-element.41), channel_id=1, source_target_pairs={{0,3},{1,2},{2,1},{3,0},{4,7},{5,6},{6,5},{7,4},{8,11},{9,10},{10,... | collective-permute-start | bytes 294920 | tf_op jit(solution)/shard_map/ppermute | solution.py:413
  7.0 10.5 %collective-permute-start.3 = (bf16[128,384]{1,0:T(8,128)(2,1)S(1)}, bf16[128,384]{1,0:T(8,128)(2,1)S(1)}, u32[]{:S(2)}, u32[]{:S(2)}) collective-permute-start(bf16[128,384]{1,0:T(8,128)(2,1)S(1)} %get-tuple-element.42), channel_id=1, source_target_pairs={{0,4},{1,5},{2,6},{3,7},{4,0},{5,1},{6,2},{7,3},{8,12},{9,13},{10,... | collective-permute-start | bytes 294920 | tf_op jit(solution)/shard_map/ppermute | solution.py:413
  9.9 15.2 %collective-permute-start.4 = (bf16[128,384]{1,0:T(8,128)(2,1)S(1)}, bf16[128,384]{1,0:T(8,128)(2,1)S(1)}, u32[]{:S(2)}, u32[]{:S(2)}) collective-permute-start(bf16[128,384]{1,0:T(8,128)(2,1)S(1)} %get-tuple-element.43), channel_id=1, source_target_pairs={{0,5},{1,4},{2,7},{3,6},{4,1},{5,0},{6,3},{7,2},{8,13},{9,12},{10,... | collective-permute-start | bytes 294920 | tf_op jit(solution)/shard_map/ppermute | solution.py:413
  11.2 13.9 %collective-permute-start.5 = (bf16[128,384]{1,0:T(8,128)(2,1)S(1)}, bf16[128,384]{1,0:T(8,128)(2,1)S(1)}, u32[]{:S(2)}, u32[]{:S(2)}) collective-permute-start(bf16[128,384]{1,0:T(8,128)(2,1)S(1)} %get-tuple-element.44), channel_id=1, source_target_pairs={{0,6},{1,7},{2,4},{3,5},{4,2},{5,3},{6,0},{7,1},{8,14},{9,15},{10,... | collective-permute-start | bytes 294920 | tf_op jit(solution)/shard_map/ppermute | solution.py:413
  14.8 10.3 %collective-permute-start.6 = (bf16[128,384]{1,0:T(8,128)(2,1)S(1)}, bf16[128,384]{1,0:T(8,128)(2,1)S(1)}, u32[]{:S(2)}, u32[]{:S(2)}) collective-permute-start(bf16[128,384]{1,0:T(8,128)(2,1)S(1)} %get-tuple-element.45), channel_id=1, source_target_pairs={{0,7},{1,6},{2,5},{3,4},{4,3},{5,2},{6,1},{7,0},{8,15},{9,14},{10,... | collective-permute-start | bytes 294920 | tf_op jit(solution)/shard_map/ppermute | solution.py:413
  26.5 25.5 %all-to-all-start = ((bf16[8,128,384]{2,1,0:T(8,128)(2,1)}), bf16[8,128,384]{2,1,0:T(8,128)(2,1)S(1)}, u32[]{:S(2)}, u32[]{:S(2)}) async-start(bf16[8,128,384]{2,1,0:T(8,128)(2,1)} %shard_map.106), calls=%async_computation | async-start | bytes 1572864 | tf_op jit(solution)/shard_map/all_to_all | solution.py:408
  33.1 1.9 %collective-permute-start.7 = (bf16[128,384]{1,0:T(8,128)(2,1)S(1)}, bf16[128,384]{1,0:T(8,128)(2,1)S(1)}, u32[]{:S(2)}, u32[]{:S(2)}) collective-permute-start(bf16[128,384]{1,0:T(8,128)(2,1)S(1)} %get-tuple-element.47), channel_id=1, source_target_pairs={{0,8},{1,9},{2,10},{3,11},{4,12},{5,13},{6,14},{7,15},{8,0},{9,1},... | collective-permute-start | bytes 294920 | tf_op jit(solution)/shard_map/ppermute | solution.py:413
  33.2 5.7 %collective-permute-start.8 = (bf16[128,384]{1,0:T(8,128)(2,1)S(1)}, bf16[128,384]{1,0:T(8,128)(2,1)S(1)}, u32[]{:S(2)}, u32[]{:S(2)}) collective-permute-start(bf16[128,384]{1,0:T(8,128)(2,1)S(1)} %get-tuple-element.48), channel_id=1, source_target_pairs={{0,16},{1,17},{2,18},{3,19},{4,20},{5,21},{6,22},{7,23},{8,24},{9,... | collective-permute-start | bytes 294920 | tf_op jit(solution)/shard_map/ppermute | solution.py:413
  34.7 5.3 %collective-permute-start.9 = (bf16[128,384]{1,0:T(8,128)(2,1)S(1)}, bf16[128,384]{1,0:T(8,128)(2,1)S(1)}, u32[]{:S(2)}, u32[]{:S(2)}) collective-permute-start(bf16[128,384]{1,0:T(8,128)(2,1)S(1)} %get-tuple-element.49), channel_id=1, source_target_pairs={{0,24},{1,25},{2,26},{3,27},{4,28},{5,29},{6,30},{7,31},{8,16},{9,... | collective-permute-start | bytes 294920 | tf_op jit(solution)/shard_map/ppermute | solution.py:413
  43.7 8.8 %collective-permute-start.10 = (bf16[128,384]{1,0:T(8,128)(2,1)S(1)}, bf16[128,384]{1,0:T(8,128)(2,1)S(1)}, u32[]{:S(2)}, u32[]{:S(2)}) collective-permute-start(bf16[128,384]{1,0:T(8,128)(2,1)S(1)} %get-tuple-element.51), channel_id=1, source_target_pairs={{0,8},{1,9},{2,10},{3,11},{4,12},{5,13},{6,14},{7,15},{8,0},{9,1},... | collective-permute-start | bytes 294920 | tf_op jit(solution)/shard_map/ppermute | solution.py:413
  44.4 8.2 %collective-permute-start.11 = (bf16[128,384]{1,0:T(8,128)(2,1)S(1)}, bf16[128,384]{1,0:T(8,128)(2,1)S(1)}, u32[]{:S(2)}, u32[]{:S(2)}) collective-permute-start(bf16[128,384]{1,0:T(8,128)(2,1)S(1)} %get-tuple-element.52), channel_id=1, source_target_pairs={{0,16},{1,17},{2,18},{3,19},{4,20},{5,21},{6,22},{7,23},{8,24},{9,... | collective-permute-start | bytes 294920 | tf_op jit(solution)/shard_map/ppermute | solution.py:413
  45.9 6.7 %collective-permute-start.12 = (bf16[128,384]{1,0:T(8,128)(2,1)S(1)}, bf16[128,384]{1,0:T(8,128)(2,1)S(1)}, u32[]{:S(2)}, u32[]{:S(2)}) collective-permute-start(bf16[128,384]{1,0:T(8,128)(2,1)S(1)} %get-tuple-element.53), channel_id=1, source_target_pairs={{0,24},{1,25},{2,26},{3,27},{4,28},{5,29},{6,30},{7,31},{8,16},{9,... | collective-permute-start | bytes 294920 | tf_op jit(solution)/shard_map/ppermute | solution.py:413
  54.2 34.5 %all-to-all-start.1 = ((bf16[8,128,384]{2,1,0:T(8,128)(2,1)}), bf16[8,128,384]{2,1,0:T(8,128)(2,1)S(1)}, u32[]{:S(2)}, u32[]{:S(2)}) async-start(bf16[8,128,384]{2,1,0:T(8,128)(2,1)} %shard_map.108), calls=%async_computation.1 | async-start | bytes 1572864 | tf_op jit(solution)/shard_map/all_to_all | solution.py:408
  58.2 1.9 %collective-permute-start.13 = (bf16[128,384]{1,0:T(8,128)(2,1)S(1)}, bf16[128,384]{1,0:T(8,128)(2,1)S(1)}, u32[]{:S(2)}, u32[]{:S(2)}) collective-permute-start(bf16[128,384]{1,0:T(8,128)(2,1)S(1)} %get-tuple-element.56), channel_id=1, source_target_pairs={{0,8},{1,9},{2,10},{3,11},{4,12},{5,13},{6,14},{7,15},{8,0},{9,1},... | collective-permute-start | bytes 294920 | tf_op jit(solution)/shard_map/ppermute | solution.py:413
  58.2 5.7 %collective-permute-start.14 = (bf16[128,384]{1,0:T(8,128)(2,1)S(1)}, bf16[128,384]{1,0:T(8,128)(2,1)S(1)}, u32[]{:S(2)}, u32[]{:S(2)}) collective-permute-start(bf16[128,384]{1,0:T(8,128)(2,1)S(1)} %get-tuple-element.57), channel_id=1, source_target_pairs={{0,16},{1,17},{2,18},{3,19},{4,20},{5,21},{6,22},{7,23},{8,24},{9,... | collective-permute-start | bytes 294920 | tf_op jit(solution)/shard_map/ppermute | solution.py:413
  59.5 5.5 %collective-permute-start.15 = (bf16[128,384]{1,0:T(8,128)(2,1)S(1)}, bf16[128,384]{1,0:T(8,128)(2,1)S(1)}, u32[]{:S(2)}, u32[]{:S(2)}) collective-permute-start(bf16[128,384]{1,0:T(8,128)(2,1)S(1)} %get-tuple-element.58), channel_id=1, source_target_pairs={{0,24},{1,25},{2,26},{3,27},{4,28},{5,29},{6,30},{7,31},{8,16},{9,... | collective-permute-start | bytes 294920 | tf_op jit(solution)/shard_map/ppermute | solution.py:413
  69.1 2.1 %collective-permute-start.16 = (bf16[96,96]{1,0:T(8,128)(2,1)S(1)}, bf16[96,96]{1,0:T(8,128)(2,1)S(1)}, u32[]{:S(2)}, u32[]{:S(2)}) collective-permute-start(bf16[96,96]{1,0:T(8,128)(2,1)S(1)} %get-tuple-element.63), channel_id=1, source_target_pairs={{0,8},{8,0},{16,24},{24,16},{1,9},{9,1},{17,25},{25,17},{2,10},{10... | collective-permute-start | bytes 55304 | tf_op jit(solution)/shard_map/ppermute | solution.py:413
  69.8 3.8 %collective-permute-start.17 = (bf16[96,96]{1,0:T(8,128)(2,1)S(1)}, bf16[96,96]{1,0:T(8,128)(2,1)S(1)}, u32[]{:S(2)}, u32[]{:S(2)}) collective-permute-start(bf16[96,96]{1,0:T(8,128)(2,1)S(1)} %get-tuple-element.64), channel_id=1, source_target_pairs={{0,16},{8,24},{16,0},{24,8},{1,17},{9,25},{17,1},{25,9},{2,18},{10... | collective-permute-start | bytes 55304 | tf_op jit(solution)/shard_map/ppermute | solution.py:413
  70.9 3.5 %collective-permute-start.18 = (bf16[96,96]{1,0:T(8,128)(2,1)S(1)}, bf16[96,96]{1,0:T(8,128)(2,1)S(1)}, u32[]{:S(2)}, u32[]{:S(2)}) collective-permute-start(bf16[96,96]{1,0:T(8,128)(2,1)S(1)} %get-tuple-element.65), channel_id=1, source_target_pairs={{0,24},{8,16},{16,8},{24,0},{1,25},{9,17},{17,9},{25,1},{2,26},{10... | collective-permute-start | bytes 55304 | tf_op jit(solution)/shard_map/ppermute | solution.py:413
  76.0 11.4 %collective-permute-start.19 = (bf16[128,384]{1,0:T(8,128)(2,1)S(1)}, bf16[128,384]{1,0:T(8,128)(2,1)S(1)}, u32[]{:S(2)}, u32[]{:S(2)}) collective-permute-start(bf16[128,384]{1,0:T(8,128)(2,1)S(1)} %get-tuple-element.67), channel_id=1, source_target_pairs={{0,8},{1,9},{2,10},{3,11},{4,12},{5,13},{6,14},{7,15},{8,0},{9,1},... | collective-permute-start | bytes 294920 | tf_op jit(solution)/shard_map/ppermute | solution.py:413
  76.2 11.3 %collective-permute-start.20 = (bf16[128,384]{1,0:T(8,128)(2,1)S(1)}, bf16[128,384]{1,0:T(8,128)(2,1)S(1)}, u32[]{:S(2)}, u32[]{:S(2)}) collective-permute-start(bf16[128,384]{1,0:T(8,128)(2,1)S(1)} %get-tuple-element.68), channel_id=1, source_target_pairs={{0,16},{1,17},{2,18},{3,19},{4,20},{5,21},{6,22},{7,23},{8,24},{9,... | collective-permute-start | bytes 294920 | tf_op jit(solution)/shard_map/ppermute | solution.py:413
  77.0 10.4 %collective-permute-start.21 = (bf16[128,384]{1,0:T(8,128)(2,1)S(1)}, bf16[128,384]{1,0:T(8,128)(2,1)S(1)}, u32[]{:S(2)}, u32[]{:S(2)}) collective-permute-start(bf16[128,384]{1,0:T(8,128)(2,1)S(1)} %get-tuple-element.69), channel_id=1, source_target_pairs={{0,24},{1,25},{2,26},{3,27},{4,28},{5,29},{6,30},{7,31},{8,16},{9,... | collective-permute-start | bytes 294920 | tf_op jit(solution)/shard_map/ppermute | solution.py:413
  78.0 5.7 %collective-permute-start.24 = (bf16[96,96]{1,0:T(8,128)(2,1)S(1)}, bf16[96,96]{1,0:T(8,128)(2,1)S(1)}, u32[]{:S(2)}, u32[]{:S(2)}) collective-permute-start(bf16[96,96]{1,0:T(8,128)(2,1)S(1)} %shard_map.111.rest_0_.refs_0_), channel_id=1, source_target_pairs={{0,6},{1,7},{2,4},{3,5},{4,2},{5,3},{6,0},{7,1},{8,14},{9,15},{10,... | collective-permute-start | bytes 55304 | tf_op jit(solution)/shard_map/ppermute | solution.py:558
  81.7 4.7 %collective-permute-start.23 = (bf16[96,96]{1,0:T(8,128)(2,1)S(1)}, bf16[96,96]{1,0:T(8,128)(2,1)S(1)}, u32[]{:S(2)}, u32[]{:S(2)}) collective-permute-start(bf16[96,96]{1,0:T(8,128)(2,1)S(1)} %shard_map.111.rest_0_.refs_0_), channel_id=1, source_target_pairs={{0,4},{1,5},{2,6},{3,7},{4,0},{5,1},{6,2},{7,3},{8,12},{9,13},{10,... | collective-permute-start | bytes 55304 | tf_op jit(solution)/shard_map/ppermute | solution.py:558
  83.6 3.8 %collective-permute-start.22 = (bf16[96,96]{1,0:T(8,128)(2,1)S(1)}, bf16[96,96]{1,0:T(8,128)(2,1)S(1)}, u32[]{:S(2)}, u32[]{:S(2)}) collective-permute-start(bf16[96,96]{1,0:T(8,128)(2,1)S(1)} %shard_map.111.rest_0_.refs_0_), channel_id=1, source_target_pairs={{0,2},{1,3},{2,0},{3,1},{4,6},{5,7},{6,4},{7,5},{8,10},{9,11},{10,... | collective-permute-start | bytes 55304 | tf_op jit(solution)/shard_map/ppermute | solution.py:558
  88.8 25.0 %all-to-all-start.2 = ((bf16[8,128,384]{2,1,0:T(8,128)(2,1)}), bf16[8,128,384]{2,1,0:T(8,128)(2,1)S(1)}, u32[]{:S(2)}, u32[]{:S(2)}) async-start(bf16[8,128,384]{2,1,0:T(8,128)(2,1)} %shard_map.114), calls=%async_computation.2 | async-start | bytes 1572864 | tf_op jit(solution)/shard_map/all_to_all | solution.py:408
  94.7 8.3 %collective-permute-start.25 = (bf16[4,96,96]{2,1,0:T(8,128)(2,1)S(1)}, bf16[4,96,96]{2,1,0:T(8,128)(2,1)S(1)}, u32[]{:S(2)}, u32[]{:S(2)}) collective-permute-start(bf16[4,96,96]{2,1,0:T(8,128)(2,1)S(1)} %shard_map.113.rest_4_.near), channel_id=1, source_target_pairs={{0,1},{1,0},{2,3},{3,2},{4,5},{5,4},{6,7},{7,6},{8,9},{9,8},{10,11... | collective-permute-start | bytes 221192 | tf_op jit(solution)/shard_map/ppermute | solution.py:565
  103.0 5.7 %collective-permute-start.27 = (bf16[8,96,96]{2,1,0:T(8,128)(2,1)S(1)}, bf16[8,96,96]{2,1,0:T(8,128)(2,1)S(1)}, u32[]{:S(2)}, u32[]{:S(2)}) collective-permute-start(bf16[8,96,96]{2,1,0:T(8,128)(2,1)S(1)} %shard_map.116.rest_0_), channel_id=1, source_target_pairs={{0,16},{8,24},{16,0},{24,8},{1,17},{9,25},{17,1},{25,9},{2,18},{10... | collective-permute-start | bytes 442376 | tf_op jit(solution)/shard_map/ppermute | solution.py:572
  104.1 4.7 %collective-permute-start.26 = (bf16[8,96,96]{2,1,0:T(8,128)(2,1)S(1)}, bf16[8,96,96]{2,1,0:T(8,128)(2,1)S(1)}, u32[]{:S(2)}, u32[]{:S(2)}) collective-permute-start(bf16[8,96,96]{2,1,0:T(8,128)(2,1)S(1)} %shard_map.116.rest_0_), channel_id=1, source_target_pairs={{0,8},{8,0},{16,24},{24,16},{1,9},{9,1},{17,25},{25,17},{2,10},{10... | collective-permute-start | bytes 442376 | tf_op jit(solution)/shard_map/ppermute | solution.py:572
  108.8 1.4 %collective-permute-start.28 = (bf16[8,96,96]{2,1,0:T(8,128)(2,1)S(1)}, bf16[8,96,96]{2,1,0:T(8,128)(2,1)S(1)}, u32[]{:S(2)}, u32[]{:S(2)}) collective-permute-start(bf16[8,96,96]{2,1,0:T(8,128)(2,1)S(1)} %collective-permute-done.27.rest_2_), channel_id=1, source_target_pairs={{0,8},{8,0},{16,24},{24,16},{1,9},{9,1},{17,25},{25,17},{2,10},{10... | collective-permute-start | bytes 442376 | tf_op jit(solution)/shard_map/ppermute | solution.py:572
  (18 other events, 81.8 us)

commit v2 on v1

--- a/solution.py
+++ b/solution.py
@@ -111,19 +111,14 @@
     deal(sent, slots, own[0])
 
 
-def unpack_body(rows_sub, subs, own, packed, field, result, slots, base, mixed, load_sems, save_sems):
+def unpack_body(rows_sub, subs, packed, base, result, mixed, sems):
     cols = base.shape[1]
-    loads = group_copies(field, base, load_sems)
-    saves = group_copies(mixed, result, save_sems)
-    for copy in loads:
-        copy.start()
-    place(slots, [packed], own[0])
+    saves = group_copies(mixed, result, sems)
     for group in range(RQ):
-        loads[group].wait()
         for sub in range(subs):
             row = (group * subs + sub) * rows_sub
             pieces = [
-                slots[sub * NB + block, :, group * BS : (group + 1) * BS] for block in range(NB)
+                packed[sub * NB + block, :, group * BS : (group + 1) * BS] for block in range(NB)
             ]
             update = jnp.concatenate(pieces, axis=1).reshape(rows_sub, cols, NB * BS)
             old = base[row : row + rows_sub]
@@ -374,15 +369,16 @@
 
 
 def sum_body(*refs):
-    refs[-1][...] = sum(value[...].astype(jnp.float32) for value in refs[:-1]).astype(jnp.bfloat16)
-
-
-def stack_body(*refs):
-    for slot, piece in enumerate(refs[:-1]):
-        refs[-1][slot] = piece[...]
-
-
-def blocks_body(own, near, other, blocks):
+    refs[-1][0] = sum(value[...].astype(jnp.float32) for value in refs[:-1]).astype(jnp.bfloat16)
+
+
+def join_body(first, second, joined):
+    count = first.shape[0]
+    joined[:count] = first[...]
+    joined[count:] = second[...]
+
+
+def blocks_body(own, near, other, anchor, blocks):
     for slot in range(near.shape[0]):
         blocks[jnp.bitwise_xor(own[0], 2 * slot)] = near[slot]
         blocks[jnp.bitwise_xor(own[0], 2 * slot + 1)] = other[slot]
@@ -470,10 +466,8 @@
 
     def unpack(source, base):
         body = functools.partial(unpack_body, rows_sub, subs)
-        scratch = [lon_slots] + [pltpu.VMEM(base.shape, bf16)] * 2
-        scratch += [pltpu.SemaphoreType.DMA((RQ,))] * 2
-        result = pltpu.HBM(base.shape, bf16)
-        return kernel_call(body, [result], [lon_index], [source], scratch, far=[base])[0]
+        scratch = [pltpu.VMEM(base.shape, bf16), pltpu.SemaphoreType.DMA((RQ,))]
+        return kernel_call(body, [pltpu.HBM(base.shape, bf16)], [], [source, base], scratch)[0]
 
     def to_spectra(pieces, anchors=()):
         return kernel_call(
@@ -538,7 +532,7 @@
         limit=mid_limit,
     )
     own_share = kernel_call(
-        sum_body, [array((share, BS), bf16)], [], swap(parts, "lat", line_pairs(lat_count))
+        sum_body, [array((1, share, BS), bf16)], [], swap(parts, "lat", line_pairs(lat_count))
     )[0]
     back = kernel_call(
         functools.partial(input_grad_body, pack_modes, 1),
@@ -550,19 +544,20 @@
         limit=mid_limit,
     )
     lon_pairs = line_pairs(lon_count)
-    near = kernel_call(
-        stack_body,
-        [array((lon_count // 2, share, BS), bf16)],
-        [],
-        [own_share]
-        + [lax.ppermute(own_share, "lon", lon_pairs(far)) for far in range(2, lon_count, 2)],
-    )[0]
+    near, step = own_share, 2
+    while step < lon_count:
+        joined = array((2 * near.shape[0], share, BS), bf16)
+        moved = lax.ppermute(near, "lon", lon_pairs(step))
+        near = kernel_call(join_body, [joined], [], [near, moved])[0]
+        step *= 2
     returned = exchange(to_columns(mid_swap(back), [near]))
+    mixed_field = unpack(filtered, features)
     blocks = kernel_call(
         blocks_body,
         [array((lon_count, share, BS), bf16)],
         [lon_index],
         [near, lax.ppermute(near, "lon", lon_pairs(1))],
+        anchors=[mixed_field],
     )[0]
 
     gathered = {0: blocks}
@@ -581,7 +576,7 @@
         gathered,
         [pltpu.VMEM((4, NB, BS, BS), f32)],
     )
-    return (unpack(filtered, features), unpack(returned, cotangent), grad_first, grad_second)
+    return (mixed_field, unpack(returned, cotangent), grad_first, grad_second)
 
 
 def solution(mesh):

time: 117 us -> 117 us (level)
  Pallas kernels: 22.1 us -> 19.8 us
    all_to_all x3, waiting for transfers between devices: 6.18 us -> 9.29 us  [exchange(): lax.all_to_all(source, 'lon', split_axis=0, concat_axis=0, tiled=True)]
    pallas_call x15 -> x16, Pallas kernels: 22.1 us -> 19.8 us  [kernel_call(): pl.pallas_call(body, out_shape=out_shape, in_specs=in_specs, out_specs=[s...]
    ppermute x3, waiting for transfers between devices: 6.14 us -> 4.73 us  [shards(): moved = lax.ppermute(gathered[offset], 'lat', line_pairs(lat_count)(step))]
    unnamed x36 -> x42, local copies, waits for them, and re-layouts: 2.65 us -> 3.79 us
    ppermute x3 -> x2, waiting for transfers between devices: 5.06 us -> 4.47 us  [shards(): moved = lax.ppermute(near, 'lon', lon_pairs(step))]
    ppermute x3 -> x2, starting transfers between devices: 4.42 us -> 4.83 us  [shards(): moved = lax.ppermute(near, 'lon', lon_pairs(step))]
  transfers between devices with their start and end apart: 32 -> 31, of which waited for: 14 -> 13; matrix products, arithmetic and copies ran while one was open for 0% -> 0% of each run, Pallas kernels for 15% -> 13%
where the time goes in v2:
time: 117 us; the launch traced here: 116 us
  starting transfers between devices  46.4 us (40%)
  waiting for transfers between devices  45 us (38%)
  Pallas kernels  19.8 us (17%)
  local copies, waits for them, and re-layouts  3.79 us (3%)
    ppermute x22, starting transfers between devices, swap(): lax.ppermute(piece, axes, partners(offset))  22.4 us
    ppermute x22, waiting for transfers between devices, swap(): lax.ppermute(piece, axes, partners(offset))  20.9 us
    pallas_call x16, Pallas kernels, kernel_call(): pl.pallas_call(body, out_shape=out_shape, in_specs=in_specs, out_specs=[s...  19.8 us
    all_to_all x3, starting transfers between devices, exchange(): lax.all_to_all(source, 'lon', split_axis=0, concat_axis=0, tiled=True)  16.1 us
    all_to_all x3, waiting for transfers between devices, exchange(): lax.all_to_all(source, 'lon', split_axis=0, concat_axis=0, tiled=True)  9.29 us
    ppermute x1, waiting for transfers between devices, shards(): lax.ppermute(near, 'lon', lon_pairs(1))  5.59 us
    ppermute x2, starting transfers between devices, shards(): moved = lax.ppermute(near, 'lon', lon_pairs(step))  4.83 us
    ppermute x3, waiting for transfers between devices, shards(): moved = lax.ppermute(gathered[offset], 'lat', line_pairs(lat_count)(step))  4.73 us
  transfers between devices with their start and end apart: 31, of which 13 were waited for; matrix products, arithmetic and copies ran while one was open for 0% of the time, Pallas kernels for 13%

profile of v2, /device:TPU:0, one launch (start us, length us, event | category | flops | bytes accessed | tf_op | source)
XLA Modules:
  0.0 116.0 jit_solution(9183864151081566192)
XLA Ops:
  0.6 1.7 %shard_map.102 = (bf16[128,384]{1,0:T(8,128)(2,1)S(1)}, bf16[128,384]{1,0:T(8,128)(2,1)S(1)}, bf16[128,384]{1,0:T(8,128)(2,1)S(1)}, bf16[128,384]{1,0:T(8,128)(2...) custom-call(s32[1]{0:T(128)} %bitcast.3.own.own_in, ...), custom_call_target="tpu_custom_call" | custom-call | tf_op jit(solution)/shard_map/pallas_call | solution.py:65
  2.3 3.0 %collective-permute-start = (bf16[128,384]{1,0:T(8,128)(2,1)S(1)}, bf16[128,384]{1,0:T(8,128)(2,1)S(1)}, u32[]{:S(2)}, u32[]{:S(2)}) collective-permute-start(bf16[128,384]{1,0:T(8,128)(2,1)S(1)} %get-tuple-element.39), channel_id=1, source_target_pairs={{0,1},{1,0},{2,3},{3,2},{4,5},{5,4},{6,7},{7,6},{8,9},{9,8},{10,11... | collective-permute-start | bytes 294920 | tf_op jit(solution)/shard_map/ppermute | solution.py:409
  5.4 1.6 %collective-permute-start.1 = (bf16[128,384]{1,0:T(8,128)(2,1)S(1)}, bf16[128,384]{1,0:T(8,128)(2,1)S(1)}, u32[]{:S(2)}, u32[]{:S(2)}) collective-permute-start(bf16[128,384]{1,0:T(8,128)(2,1)S(1)} %get-tuple-element.40), channel_id=1, source_target_pairs={{0,2},{1,3},{2,0},{3,1},{4,6},{5,7},{6,4},{7,5},{8,10},{9,11},{10,... | collective-permute-start | bytes 294920 | tf_op jit(solution)/shard_map/ppermute | solution.py:409
  7.0 3.0 %collective-permute-start.3 = (bf16[128,384]{1,0:T(8,128)(2,1)S(1)}, bf16[128,384]{1,0:T(8,128)(2,1)S(1)}, u32[]{:S(2)}, u32[]{:S(2)}) collective-permute-start(bf16[128,384]{1,0:T(8,128)(2,1)S(1)} %get-tuple-element.42), channel_id=1, source_target_pairs={{0,4},{1,5},{2,6},{3,7},{4,0},{5,1},{6,2},{7,3},{8,12},{9,13},{10,... | collective-permute-start | bytes 294920 | tf_op jit(solution)/shard_map/ppermute | solution.py:409
  9.9 1.3 %collective-permute-start.4 = (bf16[128,384]{1,0:T(8,128)(2,1)S(1)}, bf16[128,384]{1,0:T(8,128)(2,1)S(1)}, u32[]{:S(2)}, u32[]{:S(2)}) collective-permute-start(bf16[128,384]{1,0:T(8,128)(2,1)S(1)} %get-tuple-element.43), channel_id=1, source_target_pairs={{0,5},{1,4},{2,7},{3,6},{4,1},{5,0},{6,3},{7,2},{8,13},{9,12},{10,... | collective-permute-start | bytes 294920 | tf_op jit(solution)/shard_map/ppermute | solution.py:409
  11.2 3.6 %collective-permute-start.5 = (bf16[128,384]{1,0:T(8,128)(2,1)S(1)}, bf16[128,384]{1,0:T(8,128)(2,1)S(1)}, u32[]{:S(2)}, u32[]{:S(2)}) collective-permute-start(bf16[128,384]{1,0:T(8,128)(2,1)S(1)} %get-tuple-element.44), channel_id=1, source_target_pairs={{0,6},{1,7},{2,4},{3,5},{4,2},{5,3},{6,0},{7,1},{8,14},{9,15},{10,... | collective-permute-start | bytes 294920 | tf_op jit(solution)/shard_map/ppermute | solution.py:409
  14.9 1.7 %shard_map.105.refs_0_ = bf16[8,128,384]{2,1,0:T(8,128)(2,1)S(1)} custom-call(s32[1]{0:T(128)} %bitcast.3.own.own_in, bf16[32,16,768]{2,1,0:T(8,128)(2,1)} %base.3), custom_call_target="tpu_custom_call" | custom-call | tf_op jit(solution)/shard_map/pallas_call | solution.py:65
  17.5 7.6 %collective-permute-done.4.rest_5_.refs_5_ = bf16[128,384]{1,0:T(8,128)(2,1)S(1)} collective-permute-done((bf16[128,384]{1,0:T(8,128)(2,1)S(1)}, bf16[128,384]{1,0:T(8,128)(2,1)S(1)}, u32[]{:S(2)}, u32[]{:S(2)}) %collective-permute-start.4) | collective-permute-done | bytes 98336 | tf_op jit(solution)/shard_map/ppermute | solution.py:409
  26.5 5.9 %all-to-all-start = ((bf16[8,128,384]{2,1,0:T(8,128)(2,1)}), bf16[8,128,384]{2,1,0:T(8,128)(2,1)S(1)}, u32[]{:S(2)}, u32[]{:S(2)}) async-start(bf16[8,128,384]{2,1,0:T(8,128)(2,1)} %shard_map.106), calls=%async_computation | async-start | bytes 1572864 | tf_op jit(solution)/shard_map/all_to_all | solution.py:404
  33.2 1.6 %collective-permute-start.8 = (bf16[128,384]{1,0:T(8,128)(2,1)S(1)}, bf16[128,384]{1,0:T(8,128)(2,1)S(1)}, u32[]{:S(2)}, u32[]{:S(2)}) collective-permute-start(bf16[128,384]{1,0:T(8,128)(2,1)S(1)} %get-tuple-element.48), channel_id=1, source_target_pairs={{0,16},{1,17},{2,18},{3,19},{4,20},{5,21},{6,22},{7,23},{8,24},{9,... | collective-permute-start | bytes 294920 | tf_op jit(solution)/shard_map/ppermute | solution.py:409
  35.0 3.8 %collective-permute-done.8.rest_2_ = bf16[128,384]{1,0:T(8,128)(2,1)S(1)} collective-permute-done((bf16[128,384]{1,0:T(8,128)(2,1)S(1)}, bf16[128,384]{1,0:T(8,128)(2,1)S(1)}, u32[]{:S(2)}, u32[]{:S(2)}) %collective-permute-start.8) | collective-permute-done | bytes 98336 | tf_op jit(solution)/shard_map/ppermute | solution.py:409
  40.0 3.7 %shard_map.104 = (bf16[128,384]{1,0:T(8,128)(2,1)S(1)}, bf16[128,384]{1,0:T(8,128)(2,1)S(1)}, bf16[128,384]{1,0:T(8,128)(2,1)S(1)}, bf16[128,384]{1,0:T(8,128)(2...) custom-call(s32[1]{0:T(128)} %bitcast.own_out.member.own_in, s32[1]{0:T(128)} %bitcast.1.first_mode, ...), custom_call_target="tpu_custom_call" | custom-call | tf_op jit(solution)/shard_map/pallas_call | solution.py:65
  44.4 1.5 %collective-permute-start.11 = (bf16[128,384]{1,0:T(8,128)(2,1)S(1)}, bf16[128,384]{1,0:T(8,128)(2,1)S(1)}, u32[]{:S(2)}, u32[]{:S(2)}) collective-permute-start(bf16[128,384]{1,0:T(8,128)(2,1)S(1)} %get-tuple-element.52), channel_id=1, source_target_pairs={{0,16},{1,17},{2,18},{3,19},{4,20},{5,21},{6,22},{7,23},{8,24},{9,... | collective-permute-start | bytes 294920 | tf_op jit(solution)/shard_map/ppermute | solution.py:409
  45.9 6.2 %all-to-all-done.rest_0_ = bf16[8,128,384]{2,1,0:T(8,128)(2,1)S(1)} async-done(((bf16[8,128,384]{2,1,0:T(8,128)(2,1)}), bf16[8,128,384]{2,1,0:T(8,128)(2,1)S(1)}, u32[]{:S(2)}, u32[]{:S(2)}) %all-to-all-start) | async-done | bytes 786464 | tf_op jit(solution)/shard_map/all_to_all | solution.py:404
  53.0 1.2 %shard_map.108 = bf16[8,128,384]{2,1,0:T(8,128)(2,1)} custom-call(s32[1]{0:T(128)} %bitcast.own_out.member.own_in, bf16[512,256]{1,0:T(8,128)(2,1)S(1)} %copy-done.6, bf16[128,384]{1,0:T(8,128)(2,1)S(1)} %get-tuple-element.50.rest_0_, bf16[128,384]{1,0:T(8,128)(2,1)S(1)} %collective-permute-done.10.rest_1_, ...), custom_call_target="tpu_custom_call" | custom-call | tf_op jit(solution)/shard_map/pallas_call | solution.py:65
  54.2 4.0 %all-to-all-start.1 = ((bf16[8,128,384]{2,1,0:T(8,128)(2,1)}), bf16[8,128,384]{2,1,0:T(8,128)(2,1)S(1)}, u32[]{:S(2)}, u32[]{:S(2)}) async-start(bf16[8,128,384]{2,1,0:T(8,128)(2,1)} %shard_map.108), calls=%async_computation.1 | async-start | bytes 1572864 | tf_op jit(solution)/shard_map/all_to_all | solution.py:404
  58.2 1.3 %collective-permute-start.14 = (bf16[128,384]{1,0:T(8,128)(2,1)S(1)}, bf16[128,384]{1,0:T(8,128)(2,1)S(1)}, u32[]{:S(2)}, u32[]{:S(2)}) collective-permute-start(bf16[128,384]{1,0:T(8,128)(2,1)S(1)} %get-tuple-element.57), channel_id=1, source_target_pairs={{0,16},{1,17},{2,18},{3,19},{4,20},{5,21},{6,22},{7,23},{8,24},{9,... | collective-permute-start | bytes 294920 | tf_op jit(solution)/shard_map/ppermute | solution.py:409
  60.1 3.8 %collective-permute-done.14.rest_2_ = bf16[128,384]{1,0:T(8,128)(2,1)S(1)} collective-permute-done((bf16[128,384]{1,0:T(8,128)(2,1)S(1)}, bf16[128,384]{1,0:T(8,128)(2,1)S(1)}, u32[]{:S(2)}, u32[]{:S(2)}) %collective-permute-start.14) | collective-permute-done | bytes 98336 | tf_op jit(solution)/shard_map/ppermute | solution.py:409
  65.0 4.1 %shard_map.110 = (bf16[8,128,192]{2,1,0:T(8,128)(2,1)S(1)}, bf16[192,192]{1,0:T(8,128)(2,1)S(1)}, bf16[96,96]{1,0:T(8,128)(2,1)S(1)}, bf16[96,96]{1,0:T(8,128)(2...) custom-call(s32[1]{0:T(128)} %bitcast.own_out.member.own_in, s32[1]{0:T(128)} %bitcast.1.first_mode, ...), custom_call_target="tpu_custom_call" | custom-call | tf_op jit(solution)/shard_map/pallas_call | solution.py:65
  71.2 2.4 %collective-permute-done.17.refs_2_ = bf16[96,96]{1,0:T(8,128)(2,1)S(1)} collective-permute-done((bf16[96,96]{1,0:T(8,128)(2,1)S(1)}, bf16[96,96]{1,0:T(8,128)(2,1)S(1)}, u32[]{:S(2)}, u32[]{:S(2)}) %collective-permute-start.17) | collective-permute-done | bytes 18464 | tf_op jit(solution)/shard_map/ppermute | solution.py:409
  74.4 1.6 %shard_map.112 = (bf16[128,384]{1,0:T(8,128)(2,1)S(1)}, bf16[128,384]{1,0:T(8,128)(2,1)S(1)}, bf16[128,384]{1,0:T(8,128)(2,1)S(1)}, bf16[128,384]{1,0:T(8,128)(2,1)S(1)}) custom-call(s32[1]{0:T(128)} %bitcast.own_out.member.own_in, bf16[256,256]{1,0:T(8,128)(2,1)S(1)} %copy-done.4, bf16[8,128,192]{2,1,0:T(8,128)(2,1)S(1)} %get-tuple-element.60.grad_pre, ...), custom_call_target="tpu_custom_call" | custom-call | tf_op jit(solution)/shard_map/pallas_call | solution.py:65
  78.0 1.9 %collective-permute-start.22 = (bf16[1,96,96]{2,1,0:T(8,128)(2,1)S(1)}, bf16[1,96,96]{2,1,0:T(8,128)(2,1)S(1)}, u32[]{:S(2)}, u32[]{:S(2)}) collective-permute-start(bf16[1,96,96]{2,1,0:T(8,128)(2,1)S(1)} %shard_map.111.rest_0_.first), channel_id=1, source_target_pairs={{0,2},{1,3},{2,0},{3,1},{4,6},{5,7},{6,4},{7,5},{8,10},{9,11},{10,... | collective-permute-start | bytes 55304 | tf_op jit(solution)/shard_map/ppermute | solution.py:550
  79.9 1.9 %collective-permute-done.22.second = bf16[1,96,96]{2,1,0:T(8,128)(2,1)S(1)} collective-permute-done((bf16[1,96,96]{2,1,0:T(8,128)(2,1)S(1)}, bf16[1,96,96]{2,1,0:T(8,128)(2,1)S(1)}, u32[]{:S(2)}, u32[]{:S(2)}) %collective-permute-start.22) | collective-permute-done | bytes 18464 | tf_op jit(solution)/shard_map/ppermute | solution.py:550
  81.8 2.9 %collective-permute-start.23 = (bf16[2,96,96]{2,1,0:T(8,128)(2,1)S(1)}, bf16[2,96,96]{2,1,0:T(8,128)(2,1)S(1)}, u32[]{:S(2)}, u32[]{:S(2)}) collective-permute-start(bf16[2,96,96]{2,1,0:T(8,128)(2,1)S(1)} %shard_map.113.first), channel_id=1, source_target_pairs={{0,4},{1,5},{2,6},{3,7},{4,0},{5,1},{6,2},{7,3},{8,12},{9,13},{10,... | collective-permute-start | bytes 110600 | tf_op jit(solution)/shard_map/ppermute | solution.py:550
  84.7 2.6 %collective-permute-done.23.second = bf16[2,96,96]{2,1,0:T(8,128)(2,1)S(1)} collective-permute-done((bf16[2,96,96]{2,1,0:T(8,128)(2,1)S(1)}, bf16[2,96,96]{2,1,0:T(8,128)(2,1)S(1)}, u32[]{:S(2)}, u32[]{:S(2)}) %collective-permute-start.23) | collective-permute-done | bytes 36896 | tf_op jit(solution)/shard_map/ppermute | solution.py:550
  87.3 1.2 %shard_map.115 = bf16[8,128,384]{2,1,0:T(8,128)(2,1)} custom-call(s32[1]{0:T(128)} %bitcast.own_out.member.own_in, bf16[512,256]{1,0:T(8,128)(2,1)S(1)} %copy-done.6, bf16[128,384]{1,0:T(8,128)(2,1)S(1)} %get-tuple-element.66.rest_0_, bf16[128,384]{1,0:T(8,128)(2,1)S(1)} %collective-permute-done.19.rest_1_, ...), custom_call_target="tpu_custom_call" | custom-call | tf_op jit(solution)/shard_map/pallas_call | solution.py:65
  88.6 6.2 %all-to-all-start.2 = ((bf16[8,128,384]{2,1,0:T(8,128)(2,1)}), bf16[8,128,384]{2,1,0:T(8,128)(2,1)S(1)}, u32[]{:S(2)}, u32[]{:S(2)}) async-start(bf16[8,128,384]{2,1,0:T(8,128)(2,1)} %shard_map.115), calls=%async_computation.2 | async-start | bytes 1572864 | tf_op jit(solution)/shard_map/all_to_all | solution.py:404
  94.8 2.0 %collective-permute-start.24 = (bf16[4,96,96]{2,1,0:T(8,128)(2,1)S(1)}, bf16[4,96,96]{2,1,0:T(8,128)(2,1)S(1)}, u32[]{:S(2)}, u32[]{:S(2)}) collective-permute-start(bf16[4,96,96]{2,1,0:T(8,128)(2,1)S(1)} %shard_map.114.rest_4_.near), channel_id=1, source_target_pairs={{0,1},{1,0},{2,3},{3,2},{4,5},{5,4},{6,7},{7,6},{8,9},{9,8},{10,11... | collective-permute-start | bytes 221192 | tf_op jit(solution)/shard_map/ppermute | solution.py:559
  97.9 5.6 %collective-permute-done.24.other = bf16[4,96,96]{2,1,0:T(8,128)(2,1)S(1)} collective-permute-done((bf16[4,96,96]{2,1,0:T(8,128)(2,1)S(1)}, bf16[4,96,96]{2,1,0:T(8,128)(2,1)S(1)}, u32[]{:S(2)}, u32[]{:S(2)}) %collective-permute-start.24) | collective-permute-done | bytes 73760 | tf_op jit(solution)/shard_map/ppermute | solution.py:559
  105.7 4.7 %collective-permute-done.26.rest_2_ = bf16[8,96,96]{2,1,0:T(8,128)(2,1)S(1)} collective-permute-done((bf16[8,96,96]{2,1,0:T(8,128)(2,1)S(1)}, bf16[8,96,96]{2,1,0:T(8,128)(2,1)S(1)}, u32[]{:S(2)}, u32[]{:S(2)}) %collective-permute-start.26) | collective-permute-done | bytes 147488 | tf_op jit(solution)/shard_map/ppermute | solution.py:567
  110.4 3.1 %all-to-all-done.2.packed = bf16[8,128,384]{2,1,0:T(8,128)(2,1)S(1)} async-done(((bf16[8,128,384]{2,1,0:T(8,128)(2,1)}), bf16[8,128,384]{2,1,0:T(8,128)(2,1)S(1)}, u32[]{:S(2)}, u32[]{:S(2)}) %all-to-all-start.2) | async-done | bytes 786464 | tf_op jit(solution)/shard_map/all_to_all | solution.py:404
  114.7 1.3 %shard_map.118 = (f32[2,8,96,96]{3,2,1,0:T(8,128)}, f32[2,8,96,96]{3,2,1,0:T(8,128)}) custom-call(s32[1]{0:T(128)} %bitcast.4.lat_own, bf16[8,96,96]{2,1,0:T(8,128)(2,1)S(1)} %shard_map.117.rest_0_, bf16[8,96,96]{2,1,0:T(8,128)(2,1)S(1)} %collective-permute-done.25.rest_1_, bf16[8,96,96]{2,1,0:T(8,128)(2,1)S(1)} %collective-permute-done.26.rest_2_, ...), custom_call_target="tpu_custom_call" | custom-call | tf_op jit(solution)/shard_map/pallas_call | solution.py:65
  (89 shorter events, 16.9 us)
Async XLA Ops:
  2.3 8.9 %collective-permute-start = (bf16[128,384]{1,0:T(8,128)(2,1)S(1)}, bf16[128,384]{1,0:T(8,128)(2,1)S(1)}, u32[]{:S(2)}, u32[]{:S(2)}) collective-permute-start(bf16[128,384]{1,0:T(8,128)(2,1)S(1)} %get-tuple-element.39), channel_id=1, source_target_pairs={{0,1},{1,0},{2,3},{3,2},{4,5},{5,4},{6,7},{7,6},{8,9},{9,8},{10,11... | collective-permute-start | bytes 294920 | tf_op jit(solution)/shard_map/ppermute | solution.py:409
  5.4 9.5 %collective-permute-start.1 = (bf16[128,384]{1,0:T(8,128)(2,1)S(1)}, bf16[128,384]{1,0:T(8,128)(2,1)S(1)}, u32[]{:S(2)}, u32[]{:S(2)}) collective-permute-start(bf16[128,384]{1,0:T(8,128)(2,1)S(1)} %get-tuple-element.40), channel_id=1, source_target_pairs={{0,2},{1,3},{2,0},{3,1},{4,6},{5,7},{6,4},{7,5},{8,10},{9,11},{10,... | collective-permute-start | bytes 294920 | tf_op jit(solution)/shard_map/ppermute | solution.py:409
  7.0 10.5 %collective-permute-start.2 = (bf16[128,384]{1,0:T(8,128)(2,1)S(1)}, bf16[128,384]{1,0:T(8,128)(2,1)S(1)}, u32[]{:S(2)}, u32[]{:S(2)}) collective-permute-start(bf16[128,384]{1,0:T(8,128)(2,1)S(1)} %get-tuple-element.41), channel_id=1, source_target_pairs={{0,3},{1,2},{2,1},{3,0},{4,7},{5,6},{6,5},{7,4},{8,11},{9,10},{10,... | collective-permute-start | bytes 294920 | tf_op jit(solution)/shard_map/ppermute | solution.py:409
  7.0 10.5 %collective-permute-start.3 = (bf16[128,384]{1,0:T(8,128)(2,1)S(1)}, bf16[128,384]{1,0:T(8,128)(2,1)S(1)}, u32[]{:S(2)}, u32[]{:S(2)}) collective-permute-start(bf16[128,384]{1,0:T(8,128)(2,1)S(1)} %get-tuple-element.42), channel_id=1, source_target_pairs={{0,4},{1,5},{2,6},{3,7},{4,0},{5,1},{6,2},{7,3},{8,12},{9,13},{10,... | collective-permute-start | bytes 294920 | tf_op jit(solution)/shard_map/ppermute | solution.py:409
  9.9 15.2 %collective-permute-start.4 = (bf16[128,384]{1,0:T(8,128)(2,1)S(1)}, bf16[128,384]{1,0:T(8,128)(2,1)S(1)}, u32[]{:S(2)}, u32[]{:S(2)}) collective-permute-start(bf16[128,384]{1,0:T(8,128)(2,1)S(1)} %get-tuple-element.43), channel_id=1, source_target_pairs={{0,5},{1,4},{2,7},{3,6},{4,1},{5,0},{6,3},{7,2},{8,13},{9,12},{10,... | collective-permute-start | bytes 294920 | tf_op jit(solution)/shard_map/ppermute | solution.py:409
  11.2 13.9 %collective-permute-start.5 = (bf16[128,384]{1,0:T(8,128)(2,1)S(1)}, bf16[128,384]{1,0:T(8,128)(2,1)S(1)}, u32[]{:S(2)}, u32[]{:S(2)}) collective-permute-start(bf16[128,384]{1,0:T(8,128)(2,1)S(1)} %get-tuple-element.44), channel_id=1, source_target_pairs={{0,6},{1,7},{2,4},{3,5},{4,2},{5,3},{6,0},{7,1},{8,14},{9,15},{10,... | collective-permute-start | bytes 294920 | tf_op jit(solution)/shard_map/ppermute | solution.py:409
  14.8 10.3 %collective-permute-start.6 = (bf16[128,384]{1,0:T(8,128)(2,1)S(1)}, bf16[128,384]{1,0:T(8,128)(2,1)S(1)}, u32[]{:S(2)}, u32[]{:S(2)}) collective-permute-start(bf16[128,384]{1,0:T(8,128)(2,1)S(1)} %get-tuple-element.45), channel_id=1, source_target_pairs={{0,7},{1,6},{2,5},{3,4},{4,3},{5,2},{6,1},{7,0},{8,15},{9,14},{10,... | collective-permute-start | bytes 294920 | tf_op jit(solution)/shard_map/ppermute | solution.py:409
  26.5 25.5 %all-to-all-start = ((bf16[8,128,384]{2,1,0:T(8,128)(2,1)}), bf16[8,128,384]{2,1,0:T(8,128)(2,1)S(1)}, u32[]{:S(2)}, u32[]{:S(2)}) async-start(bf16[8,128,384]{2,1,0:T(8,128)(2,1)} %shard_map.106), calls=%async_computation | async-start | bytes 1572864 | tf_op jit(solution)/shard_map/all_to_all | solution.py:404
  33.1 1.9 %collective-permute-start.7 = (bf16[128,384]{1,0:T(8,128)(2,1)S(1)}, bf16[128,384]{1,0:T(8,128)(2,1)S(1)}, u32[]{:S(2)}, u32[]{:S(2)}) collective-permute-start(bf16[128,384]{1,0:T(8,128)(2,1)S(1)} %get-tuple-element.47), channel_id=1, source_target_pairs={{0,8},{1,9},{2,10},{3,11},{4,12},{5,13},{6,14},{7,15},{8,0},{9,1},... | collective-permute-start | bytes 294920 | tf_op jit(solution)/shard_map/ppermute | solution.py:409
  33.2 5.7 %collective-permute-start.8 = (bf16[128,384]{1,0:T(8,128)(2,1)S(1)}, bf16[128,384]{1,0:T(8,128)(2,1)S(1)}, u32[]{:S(2)}, u32[]{:S(2)}) collective-permute-start(bf16[128,384]{1,0:T(8,128)(2,1)S(1)} %get-tuple-element.48), channel_id=1, source_target_pairs={{0,16},{1,17},{2,18},{3,19},{4,20},{5,21},{6,22},{7,23},{8,24},{9,... | collective-permute-start | bytes 294920 | tf_op jit(solution)/shard_map/ppermute | solution.py:409
  34.7 5.3 %collective-permute-start.9 = (bf16[128,384]{1,0:T(8,128)(2,1)S(1)}, bf16[128,384]{1,0:T(8,128)(2,1)S(1)}, u32[]{:S(2)}, u32[]{:S(2)}) collective-permute-start(bf16[128,384]{1,0:T(8,128)(2,1)S(1)} %get-tuple-element.49), channel_id=1, source_target_pairs={{0,24},{1,25},{2,26},{3,27},{4,28},{5,29},{6,30},{7,31},{8,16},{9,... | collective-permute-start | bytes 294920 | tf_op jit(solution)/shard_map/ppermute | solution.py:409
  43.7 8.8 %collective-permute-start.10 = (bf16[128,384]{1,0:T(8,128)(2,1)S(1)}, bf16[128,384]{1,0:T(8,128)(2,1)S(1)}, u32[]{:S(2)}, u32[]{:S(2)}) collective-permute-start(bf16[128,384]{1,0:T(8,128)(2,1)S(1)} %get-tuple-element.51), channel_id=1, source_target_pairs={{0,8},{1,9},{2,10},{3,11},{4,12},{5,13},{6,14},{7,15},{8,0},{9,1},... | collective-permute-start | bytes 294920 | tf_op jit(solution)/shard_map/ppermute | solution.py:409
  44.4 8.2 %collective-permute-start.11 = (bf16[128,384]{1,0:T(8,128)(2,1)S(1)}, bf16[128,384]{1,0:T(8,128)(2,1)S(1)}, u32[]{:S(2)}, u32[]{:S(2)}) collective-permute-start(bf16[128,384]{1,0:T(8,128)(2,1)S(1)} %get-tuple-element.52), channel_id=1, source_target_pairs={{0,16},{1,17},{2,18},{3,19},{4,20},{5,21},{6,22},{7,23},{8,24},{9,... | collective-permute-start | bytes 294920 | tf_op jit(solution)/shard_map/ppermute | solution.py:409
  45.9 6.7 %collective-permute-start.12 = (bf16[128,384]{1,0:T(8,128)(2,1)S(1)}, bf16[128,384]{1,0:T(8,128)(2,1)S(1)}, u32[]{:S(2)}, u32[]{:S(2)}) collective-permute-start(bf16[128,384]{1,0:T(8,128)(2,1)S(1)} %get-tuple-element.53), channel_id=1, source_target_pairs={{0,24},{1,25},{2,26},{3,27},{4,28},{5,29},{6,30},{7,31},{8,16},{9,... | collective-permute-start | bytes 294920 | tf_op jit(solution)/shard_map/ppermute | solution.py:409
  54.2 34.4 %all-to-all-start.1 = ((bf16[8,128,384]{2,1,0:T(8,128)(2,1)}), bf16[8,128,384]{2,1,0:T(8,128)(2,1)S(1)}, u32[]{:S(2)}, u32[]{:S(2)}) async-start(bf16[8,128,384]{2,1,0:T(8,128)(2,1)} %shard_map.108), calls=%async_computation.1 | async-start | bytes 1572864 | tf_op jit(solution)/shard_map/all_to_all | solution.py:404
  58.2 1.9 %collective-permute-start.13 = (bf16[128,384]{1,0:T(8,128)(2,1)S(1)}, bf16[128,384]{1,0:T(8,128)(2,1)S(1)}, u32[]{:S(2)}, u32[]{:S(2)}) collective-permute-start(bf16[128,384]{1,0:T(8,128)(2,1)S(1)} %get-tuple-element.56), channel_id=1, source_target_pairs={{0,8},{1,9},{2,10},{3,11},{4,12},{5,13},{6,14},{7,15},{8,0},{9,1},... | collective-permute-start | bytes 294920 | tf_op jit(solution)/shard_map/ppermute | solution.py:409
  58.2 5.7 %collective-permute-start.14 = (bf16[128,384]{1,0:T(8,128)(2,1)S(1)}, bf16[128,384]{1,0:T(8,128)(2,1)S(1)}, u32[]{:S(2)}, u32[]{:S(2)}) collective-permute-start(bf16[128,384]{1,0:T(8,128)(2,1)S(1)} %get-tuple-element.57), channel_id=1, source_target_pairs={{0,16},{1,17},{2,18},{3,19},{4,20},{5,21},{6,22},{7,23},{8,24},{9,... | collective-permute-start | bytes 294920 | tf_op jit(solution)/shard_map/ppermute | solution.py:409
  59.5 5.5 %collective-permute-start.15 = (bf16[128,384]{1,0:T(8,128)(2,1)S(1)}, bf16[128,384]{1,0:T(8,128)(2,1)S(1)}, u32[]{:S(2)}, u32[]{:S(2)}) collective-permute-start(bf16[128,384]{1,0:T(8,128)(2,1)S(1)} %get-tuple-element.58), channel_id=1, source_target_pairs={{0,24},{1,25},{2,26},{3,27},{4,28},{5,29},{6,30},{7,31},{8,16},{9,... | collective-permute-start | bytes 294920 | tf_op jit(solution)/shard_map/ppermute | solution.py:409
  69.1 2.1 %collective-permute-start.16 = (bf16[96,96]{1,0:T(8,128)(2,1)S(1)}, bf16[96,96]{1,0:T(8,128)(2,1)S(1)}, u32[]{:S(2)}, u32[]{:S(2)}) collective-permute-start(bf16[96,96]{1,0:T(8,128)(2,1)S(1)} %get-tuple-element.63), channel_id=1, source_target_pairs={{0,8},{8,0},{16,24},{24,16},{1,9},{9,1},{17,25},{25,17},{2,10},{10... | collective-permute-start | bytes 55304 | tf_op jit(solution)/shard_map/ppermute | solution.py:409
  69.8 3.8 %collective-permute-start.17 = (bf16[96,96]{1,0:T(8,128)(2,1)S(1)}, bf16[96,96]{1,0:T(8,128)(2,1)S(1)}, u32[]{:S(2)}, u32[]{:S(2)}) collective-permute-start(bf16[96,96]{1,0:T(8,128)(2,1)S(1)} %get-tuple-element.64), channel_id=1, source_target_pairs={{0,16},{8,24},{16,0},{24,8},{1,17},{9,25},{17,1},{25,9},{2,18},{10... | collective-permute-start | bytes 55304 | tf_op jit(solution)/shard_map/ppermute | solution.py:409
  70.9 3.5 %collective-permute-start.18 = (bf16[96,96]{1,0:T(8,128)(2,1)S(1)}, bf16[96,96]{1,0:T(8,128)(2,1)S(1)}, u32[]{:S(2)}, u32[]{:S(2)}) collective-permute-start(bf16[96,96]{1,0:T(8,128)(2,1)S(1)} %get-tuple-element.65), channel_id=1, source_target_pairs={{0,24},{8,16},{16,8},{24,0},{1,25},{9,17},{17,9},{25,1},{2,26},{10... | collective-permute-start | bytes 55304 | tf_op jit(solution)/shard_map/ppermute | solution.py:409
  76.0 11.3 %collective-permute-start.19 = (bf16[128,384]{1,0:T(8,128)(2,1)S(1)}, bf16[128,384]{1,0:T(8,128)(2,1)S(1)}, u32[]{:S(2)}, u32[]{:S(2)}) collective-permute-start(bf16[128,384]{1,0:T(8,128)(2,1)S(1)} %get-tuple-element.67), channel_id=1, source_target_pairs={{0,8},{1,9},{2,10},{3,11},{4,12},{5,13},{6,14},{7,15},{8,0},{9,1},... | collective-permute-start | bytes 294920 | tf_op jit(solution)/shard_map/ppermute | solution.py:409
  76.2 11.2 %collective-permute-start.20 = (bf16[128,384]{1,0:T(8,128)(2,1)S(1)}, bf16[128,384]{1,0:T(8,128)(2,1)S(1)}, u32[]{:S(2)}, u32[]{:S(2)}) collective-permute-start(bf16[128,384]{1,0:T(8,128)(2,1)S(1)} %get-tuple-element.68), channel_id=1, source_target_pairs={{0,16},{1,17},{2,18},{3,19},{4,20},{5,21},{6,22},{7,23},{8,24},{9,... | collective-permute-start | bytes 294920 | tf_op jit(solution)/shard_map/ppermute | solution.py:409
  77.1 10.3 %collective-permute-start.21 = (bf16[128,384]{1,0:T(8,128)(2,1)S(1)}, bf16[128,384]{1,0:T(8,128)(2,1)S(1)}, u32[]{:S(2)}, u32[]{:S(2)}) collective-permute-start(bf16[128,384]{1,0:T(8,128)(2,1)S(1)} %get-tuple-element.69), channel_id=1, source_target_pairs={{0,24},{1,25},{2,26},{3,27},{4,28},{5,29},{6,30},{7,31},{8,16},{9,... | collective-permute-start | bytes 294920 | tf_op jit(solution)/shard_map/ppermute | solution.py:409
  78.0 3.8 %collective-permute-start.22 = (bf16[1,96,96]{2,1,0:T(8,128)(2,1)S(1)}, bf16[1,96,96]{2,1,0:T(8,128)(2,1)S(1)}, u32[]{:S(2)}, u32[]{:S(2)}) collective-permute-start(bf16[1,96,96]{2,1,0:T(8,128)(2,1)S(1)} %shard_map.111.rest_0_.first), channel_id=1, source_target_pairs={{0,2},{1,3},{2,0},{3,1},{4,6},{5,7},{6,4},{7,5},{8,10},{9,11},{10,... | collective-permute-start | bytes 55304 | tf_op jit(solution)/shard_map/ppermute | solution.py:550
  81.8 5.5 %collective-permute-start.23 = (bf16[2,96,96]{2,1,0:T(8,128)(2,1)S(1)}, bf16[2,96,96]{2,1,0:T(8,128)(2,1)S(1)}, u32[]{:S(2)}, u32[]{:S(2)}) collective-permute-start(bf16[2,96,96]{2,1,0:T(8,128)(2,1)S(1)} %shard_map.113.first), channel_id=1, source_target_pairs={{0,4},{1,5},{2,6},{3,7},{4,0},{5,1},{6,2},{7,3},{8,12},{9,13},{10,... | collective-permute-start | bytes 110600 | tf_op jit(solution)/shard_map/ppermute | solution.py:550
  88.6 24.9 %all-to-all-start.2 = ((bf16[8,128,384]{2,1,0:T(8,128)(2,1)}), bf16[8,128,384]{2,1,0:T(8,128)(2,1)S(1)}, u32[]{:S(2)}, u32[]{:S(2)}) async-start(bf16[8,128,384]{2,1,0:T(8,128)(2,1)} %shard_map.115), calls=%async_computation.2 | async-start | bytes 1572864 | tf_op jit(solution)/shard_map/all_to_all | solution.py:404
  94.8 8.7 %collective-permute-start.24 = (bf16[4,96,96]{2,1,0:T(8,128)(2,1)S(1)}, bf16[4,96,96]{2,1,0:T(8,128)(2,1)S(1)}, u32[]{:S(2)}, u32[]{:S(2)}) collective-permute-start(bf16[4,96,96]{2,1,0:T(8,128)(2,1)S(1)} %shard_map.114.rest_4_.near), channel_id=1, source_target_pairs={{0,1},{1,0},{2,3},{3,2},{4,5},{5,4},{6,7},{7,6},{8,9},{9,8},{10,11... | collective-permute-start | bytes 221192 | tf_op jit(solution)/shard_map/ppermute | solution.py:559
  97.9 15.6 %copy-start.1 = (bf16[32,16,768]{2,1,0:T(8,128)(2,1)S(1)}, bf16[32,16,768]{2,1,0:T(8,128)(2,1)}, u32[]{:S(2)}) copy-start(bf16[32,16,768]{2,1,0:T(8,128)(2,1)} %base.3) | copy-start | bytes 2359300
  104.7 5.7 %collective-permute-start.26 = (bf16[8,96,96]{2,1,0:T(8,128)(2,1)S(1)}, bf16[8,96,96]{2,1,0:T(8,128)(2,1)S(1)}, u32[]{:S(2)}, u32[]{:S(2)}) collective-permute-start(bf16[8,96,96]{2,1,0:T(8,128)(2,1)S(1)} %shard_map.117.rest_0_), channel_id=1, source_target_pairs={{0,16},{8,24},{16,0},{24,8},{1,17},{9,25},{17,1},{25,9},{2,18},{10... | collective-permute-start | bytes 442376 | tf_op jit(solution)/shard_map/ppermute | solution.py:567
  105.7 9.0 %collective-permute-start.25 = (bf16[8,96,96]{2,1,0:T(8,128)(2,1)S(1)}, bf16[8,96,96]{2,1,0:T(8,128)(2,1)S(1)}, u32[]{:S(2)}, u32[]{:S(2)}) collective-permute-start(bf16[8,96,96]{2,1,0:T(8,128)(2,1)S(1)} %shard_map.117.rest_0_), channel_id=1, source_target_pairs={{0,8},{8,0},{16,24},{24,16},{1,9},{9,1},{17,25},{25,17},{2,10},{10... | collective-permute-start | bytes 442376 | tf_op jit(solution)/shard_map/ppermute | solution.py:567
  110.4 4.2 %collective-permute-start.27 = (bf16[8,96,96]{2,1,0:T(8,128)(2,1)S(1)}, bf16[8,96,96]{2,1,0:T(8,128)(2,1)S(1)}, u32[]{:S(2)}, u32[]{:S(2)}) collective-permute-start(bf16[8,96,96]{2,1,0:T(8,128)(2,1)S(1)} %collective-permute-done.26.rest_2_), channel_id=1, source_target_pairs={{0,8},{8,0},{16,24},{24,16},{1,9},{9,1},{17,25},{25,17},{2,10},{10... | collective-permute-start | bytes 442376 | tf_op jit(solution)/shard_map/ppermute | solution.py:567
  (20 other events, 91.2 us)

commit v3 on v2

--- a/solution.py
+++ b/solution.py
@@ -93,6 +93,20 @@
     ]
 
 
+def join_gate(first, second, source, gated):
+    near, anywhere = pl.BlockSpec(memory_space=pltpu.VMEM), pl.BlockSpec(memory_space=pl.ANY)
+    joined = jax.ShapeDtypeStruct((2 * first.shape[0],) + first.shape[1:], first.dtype)
+    passed = [source] if gated else []
+    results = pl.pallas_call(
+        join_body,
+        out_shape=[joined] + [jax.ShapeDtypeStruct(value.shape, value.dtype) for value in passed],
+        in_specs=[near, near] + [anywhere] * len(passed),
+        out_specs=[near] + [anywhere] * len(passed),
+        input_output_aliases={2: 1} if gated else {},
+    )(first, second, *passed)
+    return results[0], results[1] if gated else source
+
+
 def pack_body(rows_sub, subs, own, field, *rest):
     sent, (slots, source, sems) = rest[:-3], rest[-3:]
     cols = source.shape[1]
@@ -111,7 +125,8 @@
     deal(sent, slots, own[0])
 
 
-def unpack_body(rows_sub, subs, packed, base, result, mixed, sems):
+def unpack_body(rows_sub, subs, extra, packed, base, *rest):
+    result, mixed, sems = rest[extra:]
     cols = base.shape[1]
     saves = group_copies(mixed, result, sems)
     for group in range(RQ):
@@ -372,8 +387,8 @@
     refs[-1][0] = sum(value[...].astype(jnp.float32) for value in refs[:-1]).astype(jnp.bfloat16)
 
 
-def join_body(first, second, joined):
-    count = first.shape[0]
+def join_body(first, second, *rest):
+    joined, count = rest[len(rest) // 2], first.shape[0]
     joined[:count] = first[...]
     joined[count:] = second[...]
 
@@ -464,10 +479,10 @@
         scratch = [lon_slots, pltpu.VMEM(source.shape, bf16), pltpu.SemaphoreType.DMA((RQ,))]
         return kernel_call(body, sent, [lon_index], [], scratch, far=[source])
 
-    def unpack(source, base):
-        body = functools.partial(unpack_body, rows_sub, subs)
+    def unpack(source, base, anchors=()):
+        body = functools.partial(unpack_body, rows_sub, subs, len(anchors))
         scratch = [pltpu.VMEM(base.shape, bf16), pltpu.SemaphoreType.DMA((RQ,))]
-        return kernel_call(body, [pltpu.HBM(base.shape, bf16)], [], [source, base], scratch)[0]
+        return kernel_call(body, [pltpu.HBM(base.shape, bf16)], [], [source, base], scratch, anchors)[0]
 
     def to_spectra(pieces, anchors=()):
         return kernel_call(
@@ -500,12 +515,13 @@
     ]
 
     field = swap(pack(features, [lon_piece] * lon_count), "lon", line_pairs(lon_count))
-    field_cot = exchange(gate(pack(cotangent, [lon_whole])[0], field[1:]))
+    spectra = to_spectra(field)
+    field_cot = exchange(gate(pack(cotangent, [lon_whole])[0], spectra[:1]))
     results = kernel_call(
         functools.partial(forward_body, members, pack_modes),
         [mid_piece] * members + [pltpu.HBM(modes, bf16), array((8, 128), f32)],
         [member, member * kept, block],
-        [lat_both, *mid_swap(to_spectra(field))],
+        [lat_both, *mid_swap(spectra)],
         [mid_slots, *mid_scratch],
         far=weights,
         limit=mid_limit,
@@ -544,13 +560,13 @@
         limit=mid_limit,
     )
     lon_pairs = line_pairs(lon_count)
+    columns = to_columns(mid_swap(back))
     near, step = own_share, 2
     while step < lon_count:
-        joined = array((2 * near.shape[0], share, BS), bf16)
         moved = lax.ppermute(near, "lon", lon_pairs(step))
-        near = kernel_call(join_body, [joined], [], [near, moved])[0]
+        near, columns = join_gate(near, moved, columns, step == lon_count // 2)
         step *= 2
-    returned = exchange(to_columns(mid_swap(back), [near]))
+    returned = exchange(columns)
     mixed_field = unpack(filtered, features)
     blocks = kernel_call(
         blocks_body,
@@ -576,7 +592,8 @@
         gathered,
         [pltpu.VMEM((4, NB, BS, BS), f32)],
     )
-    return (mixed_field, unpack(returned, cotangent), grad_first, grad_second)
+    feature_grad = unpack(returned, cotangent, [grad_first])
+    return (mixed_field, feature_grad, grad_first, grad_second)
 
 
 def solution(mesh):

time: 117 us -> 120 us (1.026)
  Pallas kernels: 19.8 us -> 22.7 us
  local copies, waits for them, and re-layouts: 3.79 us -> 5.47 us
    pallas_call x0 -> x2, Pallas kernels: none -> 2.86 us  [join_gate(): pl.pallas_call(join_body, out_shape=[joined] + [jax.ShapeDtypeStruct(valu...]
    all_to_all x3, waiting for transfers between devices: 9.29 us -> 7.26 us  [exchange(): lax.all_to_all(source, 'lon', split_axis=0, concat_axis=0, tiled=True)]
    ppermute x3, waiting for transfers between devices: 4.73 us -> 6.49 us  [shards(): moved = lax.ppermute(gathered[offset], 'lat', line_pairs(lat_count)(step))]
    unnamed x42 -> x28, local copies, waits for them, and re-layouts: 3.79 us -> 5.47 us
    pallas_call x16 -> x14, Pallas kernels: 19.8 us -> 19.8 us  [kernel_call(): pl.pallas_call(body, out_shape=out_shape, in_specs=in_specs, out_specs=[s...]
  transfers between devices with their start and end apart: 31 -> 31, of which waited for: 13 -> 14; matrix products, arithmetic and copies ran while one was open for 0% -> 0% of each run, Pallas kernels for 13% -> 15%
where the time goes in v3:
time: 120 us; the launch traced here: 119 us
  starting transfers between devices  46.3 us (39%)
  waiting for transfers between devices  43.9 us (37%)
  Pallas kernels  22.7 us (19%)
  local copies, waits for them, and re-layouts  5.47 us (5%)
    ppermute x22, starting transfers between devices, swap(): lax.ppermute(piece, axes, partners(offset))  22.5 us
    ppermute x22, waiting for transfers between devices, swap(): lax.ppermute(piece, axes, partners(offset))  21.2 us
    pallas_call x14, Pallas kernels, kernel_call(): pl.pallas_call(body, out_shape=out_shape, in_specs=in_specs, out_specs=[s...  19.8 us
    all_to_all x3, starting transfers between devices, exchange(): lax.all_to_all(source, 'lon', split_axis=0, concat_axis=0, tiled=True)  16.3 us
    all_to_all x3, waiting for transfers between devices, exchange(): lax.all_to_all(source, 'lon', split_axis=0, concat_axis=0, tiled=True)  7.26 us
    ppermute x3, waiting for transfers between devices, shards(): moved = lax.ppermute(gathered[offset], 'lat', line_pairs(lat_count)(step))  6.49 us
    ppermute x1, waiting for transfers between devices, shards(): lax.ppermute(near, 'lon', lon_pairs(1))  5.58 us
    unnamed x28, local copies, waits for them, and re-layouts  5.47 us
  transfers between devices with their start and end apart: 31, of which 14 were waited for; matrix products, arithmetic and copies ran while one was open for 0% of the time, Pallas kernels for 15%

profile of v3, /device:TPU:0, one launch (start us, length us, event | category | flops | bytes accessed | tf_op | source)
XLA Modules:
  0.0 119.2 jit_solution(9515497945352564244)
XLA Ops:
  0.6 1.7 %shard_map.102 = (bf16[128,384]{1,0:T(8,128)(2,1)S(1)}, bf16[128,384]{1,0:T(8,128)(2,1)S(1)}, bf16[128,384]{1,0:T(8,128)(2,1)S(1)}, bf16[128,384]{1,0:T(8,128)(2...) custom-call(s32[1]{0:T(128)} %bitcast.3.own.own_in, ...), custom_call_target="tpu_custom_call" | custom-call | tf_op jit(solution)/shard_map/pallas_call | solution.py:65
  2.3 3.0 %collective-permute-start = (bf16[128,384]{1,0:T(8,128)(2,1)S(1)}, bf16[128,384]{1,0:T(8,128)(2,1)S(1)}, u32[]{:S(2)}, u32[]{:S(2)}) collective-permute-start(bf16[128,384]{1,0:T(8,128)(2,1)S(1)} %get-tuple-element.41), channel_id=1, source_target_pairs={{0,1},{1,0},{2,3},{3,2},{4,5},{5,4},{6,7},{7,6},{8,9},{9,8},{10,11... | collective-permute-start | bytes 294920 | tf_op jit(solution)/shard_map/ppermute | solution.py:424
  5.4 1.6 %collective-permute-start.1 = (bf16[128,384]{1,0:T(8,128)(2,1)S(1)}, bf16[128,384]{1,0:T(8,128)(2,1)S(1)}, u32[]{:S(2)}, u32[]{:S(2)}) collective-permute-start(bf16[128,384]{1,0:T(8,128)(2,1)S(1)} %get-tuple-element.42), channel_id=1, source_target_pairs={{0,2},{1,3},{2,0},{3,1},{4,6},{5,7},{6,4},{7,5},{8,10},{9,11},{10,... | collective-permute-start | bytes 294920 | tf_op jit(solution)/shard_map/ppermute | solution.py:424
  7.0 3.0 %collective-permute-start.3 = (bf16[128,384]{1,0:T(8,128)(2,1)S(1)}, bf16[128,384]{1,0:T(8,128)(2,1)S(1)}, u32[]{:S(2)}, u32[]{:S(2)}) collective-permute-start(bf16[128,384]{1,0:T(8,128)(2,1)S(1)} %get-tuple-element.44), channel_id=1, source_target_pairs={{0,4},{1,5},{2,6},{3,7},{4,0},{5,1},{6,2},{7,3},{8,12},{9,13},{10,... | collective-permute-start | bytes 294920 | tf_op jit(solution)/shard_map/ppermute | solution.py:424
  11.2 3.6 %collective-permute-start.5 = (bf16[128,384]{1,0:T(8,128)(2,1)S(1)}, bf16[128,384]{1,0:T(8,128)(2,1)S(1)}, u32[]{:S(2)}, u32[]{:S(2)}) collective-permute-start(bf16[128,384]{1,0:T(8,128)(2,1)S(1)} %get-tuple-element.46), channel_id=1, source_target_pairs={{0,6},{1,7},{2,4},{3,5},{4,2},{5,3},{6,0},{7,1},{8,14},{9,15},{10,... | collective-permute-start | bytes 294920 | tf_op jit(solution)/shard_map/ppermute | solution.py:424
  14.8 1.7 %shard_map.105.refs_0_ = bf16[8,128,384]{2,1,0:T(8,128)(2,1)S(1)} custom-call(s32[1]{0:T(128)} %bitcast.3.own.own_in, bf16[32,16,768]{2,1,0:T(8,128)(2,1)} %base.3), custom_call_target="tpu_custom_call" | custom-call | tf_op jit(solution)/shard_map/pallas_call | solution.py:65
  17.5 7.7 %collective-permute-done.4.rest_5_ = bf16[128,384]{1,0:T(8,128)(2,1)S(1)} collective-permute-done((bf16[128,384]{1,0:T(8,128)(2,1)S(1)}, bf16[128,384]{1,0:T(8,128)(2,1)S(1)}, u32[]{:S(2)}, u32[]{:S(2)}) %collective-permute-start.4) | collective-permute-done | bytes 98336 | tf_op jit(solution)/shard_map/ppermute | solution.py:424
  26.3 6.6 %all-to-all-start = ((bf16[8,128,384]{2,1,0:T(8,128)(2,1)}), bf16[8,128,384]{2,1,0:T(8,128)(2,1)S(1)}, u32[]{:S(2)}, u32[]{:S(2)}) async-start(bf16[8,128,384]{2,1,0:T(8,128)(2,1)} %shard_map.106), calls=%async_computation | async-start | bytes 1572864 | tf_op jit(solution)/shard_map/all_to_all | solution.py:419
  32.9 1.6 %collective-permute-start.8 = (bf16[128,384]{1,0:T(8,128)(2,1)S(1)}, bf16[128,384]{1,0:T(8,128)(2,1)S(1)}, u32[]{:S(2)}, u32[]{:S(2)}) collective-permute-start(bf16[128,384]{1,0:T(8,128)(2,1)S(1)} %get-tuple-element.50), channel_id=1, source_target_pairs={{0,16},{1,17},{2,18},{3,19},{4,20},{5,21},{6,22},{7,23},{8,24},{9,... | collective-permute-start | bytes 294920 | tf_op jit(solution)/shard_map/ppermute | solution.py:424
  34.8 3.8 %collective-permute-done.8.rest_2_ = bf16[128,384]{1,0:T(8,128)(2,1)S(1)} collective-permute-done((bf16[128,384]{1,0:T(8,128)(2,1)S(1)}, bf16[128,384]{1,0:T(8,128)(2,1)S(1)}, u32[]{:S(2)}, u32[]{:S(2)}) %collective-permute-start.8) | collective-permute-done | bytes 98336 | tf_op jit(solution)/shard_map/ppermute | solution.py:424
  39.8 3.7 %shard_map.104 = (bf16[128,384]{1,0:T(8,128)(2,1)S(1)}, bf16[128,384]{1,0:T(8,128)(2,1)S(1)}, bf16[128,384]{1,0:T(8,128)(2,1)S(1)}, bf16[128,384]{1,0:T(8,128)(2...) custom-call(s32[1]{0:T(128)} %bitcast.own_out.member.own_in, s32[1]{0:T(128)} %bitcast.1.first_mode, ...), custom_call_target="tpu_custom_call" | custom-call | tf_op jit(solution)/shard_map/pallas_call | solution.py:65
  44.1 1.5 %collective-permute-start.11 = (bf16[128,384]{1,0:T(8,128)(2,1)S(1)}, bf16[128,384]{1,0:T(8,128)(2,1)S(1)}, u32[]{:S(2)}, u32[]{:S(2)}) collective-permute-start(bf16[128,384]{1,0:T(8,128)(2,1)S(1)} %get-tuple-element.54), channel_id=1, source_target_pairs={{0,16},{1,17},{2,18},{3,19},{4,20},{5,21},{6,22},{7,23},{8,24},{9,... | collective-permute-start | bytes 294920 | tf_op jit(solution)/shard_map/ppermute | solution.py:424
  45.6 6.9 %all-to-all-done.rest_0_ = bf16[8,128,384]{2,1,0:T(8,128)(2,1)S(1)} async-done(((bf16[8,128,384]{2,1,0:T(8,128)(2,1)}), bf16[8,128,384]{2,1,0:T(8,128)(2,1)S(1)}, u32[]{:S(2)}, u32[]{:S(2)}) %all-to-all-start) | async-done | bytes 786464 | tf_op jit(solution)/shard_map/all_to_all | solution.py:419
  54.7 3.6 %all-to-all-start.1 = ((bf16[8,128,384]{2,1,0:T(8,128)(2,1)}), bf16[8,128,384]{2,1,0:T(8,128)(2,1)S(1)}, u32[]{:S(2)}, u32[]{:S(2)}) async-start(bf16[8,128,384]{2,1,0:T(8,128)(2,1)} %shard_map.108), calls=%async_computation.1 | async-start | bytes 1572864 | tf_op jit(solution)/shard_map/all_to_all | solution.py:419
  58.4 1.6 %collective-permute-start.14 = (bf16[128,384]{1,0:T(8,128)(2,1)S(1)}, bf16[128,384]{1,0:T(8,128)(2,1)S(1)}, u32[]{:S(2)}, u32[]{:S(2)}) collective-permute-start(bf16[128,384]{1,0:T(8,128)(2,1)S(1)} %get-tuple-element.59), channel_id=1, source_target_pairs={{0,16},{1,17},{2,18},{3,19},{4,20},{5,21},{6,22},{7,23},{8,24},{9,... | collective-permute-start | bytes 294920 | tf_op jit(solution)/shard_map/ppermute | solution.py:424
  60.2 3.8 %collective-permute-done.14.rest_2_ = bf16[128,384]{1,0:T(8,128)(2,1)S(1)} collective-permute-done((bf16[128,384]{1,0:T(8,128)(2,1)S(1)}, bf16[128,384]{1,0:T(8,128)(2,1)S(1)}, u32[]{:S(2)}, u32[]{:S(2)}) %collective-permute-start.14) | collective-permute-done | bytes 98336 | tf_op jit(solution)/shard_map/ppermute | solution.py:424
  65.2 4.1 %shard_map.110 = (bf16[8,128,192]{2,1,0:T(8,128)(2,1)S(1)}, bf16[192,192]{1,0:T(8,128)(2,1)S(1)}, bf16[96,96]{1,0:T(8,128)(2,1)S(1)}, bf16[96,96]{1,0:T(8,128)(2...) custom-call(s32[1]{0:T(128)} %bitcast.own_out.member.own_in, s32[1]{0:T(128)} %bitcast.1.first_mode, ...), custom_call_target="tpu_custom_call" | custom-call | tf_op jit(solution)/shard_map/pallas_call | solution.py:65
  69.9 1.5 %collective-permute-start.17 = (bf16[96,96]{1,0:T(8,128)(2,1)S(1)}, bf16[96,96]{1,0:T(8,128)(2,1)S(1)}, u32[]{:S(2)}, u32[]{:S(2)}) collective-permute-start(bf16[96,96]{1,0:T(8,128)(2,1)S(1)} %get-tuple-element.64), channel_id=1, source_target_pairs={{0,16},{8,24},{16,0},{24,8},{1,17},{9,25},{17,1},{25,9},{2,18},{10... | collective-permute-start | bytes 55304 | tf_op jit(solution)/shard_map/ppermute | solution.py:424
  71.4 2.3 %collective-permute-done.17.refs_2_ = bf16[96,96]{1,0:T(8,128)(2,1)S(1)} collective-permute-done((bf16[96,96]{1,0:T(8,128)(2,1)S(1)}, bf16[96,96]{1,0:T(8,128)(2,1)S(1)}, u32[]{:S(2)}, u32[]{:S(2)}) %collective-permute-start.17) | collective-permute-done | bytes 18464 | tf_op jit(solution)/shard_map/ppermute | solution.py:424
  74.9 1.6 %shard_map.113 = (bf16[128,384]{1,0:T(8,128)(2,1)S(1)}, bf16[128,384]{1,0:T(8,128)(2,1)S(1)}, bf16[128,384]{1,0:T(8,128)(2,1)S(1)}, bf16[128,384]{1,0:T(8,128)(2,1)S(1)}) custom-call(s32[1]{0:T(128)} %bitcast.own_out.member.own_in, bf16[256,256]{1,0:T(8,128)(2,1)S(1)} %copy-done.4, bf16[8,128,192]{2,1,0:T(8,128)(2,1)S(1)} %get-tuple-element.66.grad_pre, ...), custom_call_target="tpu_custom_call" | custom-call | tf_op jit(solution)/shard_map/pallas_call | solution.py:65
  78.5 1.9 %collective-permute-start.19 = (bf16[1,96,96]{2,1,0:T(8,128)(2,1)S(1)}, bf16[1,96,96]{2,1,0:T(8,128)(2,1)S(1)}, u32[]{:S(2)}, u32[]{:S(2)}) collective-permute-start(bf16[1,96,96]{2,1,0:T(8,128)(2,1)S(1)} %shard_map.111.first.rest_0_), channel_id=1, source_target_pairs={{0,2},{1,3},{2,0},{3,1},{4,6},{5,7},{6,4},{7,5},{8,10},{9,11},{10,... | collective-permute-start | bytes 55304 | tf_op jit(solution)/shard_map/ppermute | solution.py:566
  80.4 1.9 %collective-permute-done.19.second = bf16[1,96,96]{2,1,0:T(8,128)(2,1)S(1)} collective-permute-done((bf16[1,96,96]{2,1,0:T(8,128)(2,1)S(1)}, bf16[1,96,96]{2,1,0:T(8,128)(2,1)S(1)}, u32[]{:S(2)}, u32[]{:S(2)}) %collective-permute-start.19) | collective-permute-done | bytes 18464 | tf_op jit(solution)/shard_map/ppermute | solution.py:566
  82.9 1.4 %shard_map.112.first = bf16[2,96,96]{2,1,0:T(8,128)(2,1)} custom-call(bf16[1,96,96]{2,1,0:T(8,128)(2,1)} %copy-done.10, bf16[1,96,96]{2,1,0:T(8,128)(2,1)} %copy-done.13), custom_call_target="tpu_custom_call" | custom-call | tf_op jit(solution)/shard_map/pallas_call | solution.py:100
  84.3 2.8 %collective-permute-start.20 = (bf16[2,96,96]{2,1,0:T(8,128)(2,1)}, bf16[2,96,96]{2,1,0:T(8,128)(2,1)S(1)}, u32[]{:S(2)}, u32[]{:S(2)}) collective-permute-start(bf16[2,96,96]{2,1,0:T(8,128)(2,1)} %shard_map.112.first), channel_id=1, source_target_pairs={{0,4},{1,5},{2,6},{3,7},{4,0},{5,1},{6,2},{7,3},{8,12},{9,13},{10,... | collective-permute-start | bytes 110600 | tf_op jit(solution)/shard_map/ppermute | solution.py:566
  88.4 1.5 %collective-permute-done.20.second = bf16[2,96,96]{2,1,0:T(8,128)(2,1)S(1)} collective-permute-done((bf16[2,96,96]{2,1,0:T(8,128)(2,1)}, bf16[2,96,96]{2,1,0:T(8,128)(2,1)S(1)}, u32[]{:S(2)}, u32[]{:S(2)}) %collective-permute-start.20) | collective-permute-done | bytes 36896 | tf_op jit(solution)/shard_map/ppermute | solution.py:566
  90.5 1.5 %shard_map.115 = (bf16[4,96,96]{2,1,0:T(8,128)(2,1)}, bf16[8,128,384]{2,1,0:T(8,128)(2,1)}) custom-call(bf16[2,96,96]{2,1,0:T(8,128)(2,1)} %shard_map.112.first, bf16[2,96,96]{2,1,0:T(8,128)(2,1)} %copy-done.12, bf16[8,128,384]{2,1,0:T(8,128)(2,1)} %shard_map.114.rest_0_), custom_call_target="tpu_custom_call", output_to_operand_aliasing={{1}: (2, {})} | custom-call | tf_op jit(solution)/shard_map/pallas_call | solution.py:100
  92.0 6.1 %all-to-all-start.2 = ((bf16[8,128,384]{2,1,0:T(8,128)(2,1)}), bf16[8,128,384]{2,1,0:T(8,128)(2,1)S(1)}, u32[]{:S(2)}, u32[]{:S(2)}) async-start(bf16[8,128,384]{2,1,0:T(8,128)(2,1)} %get-tuple-element.72), calls=%async_computation.2 | async-start | bytes 1572864 | tf_op jit(solution)/shard_map/all_to_all | solution.py:419
  98.2 2.0 %collective-permute-start.24 = (bf16[4,96,96]{2,1,0:T(8,128)(2,1)S(1)}, bf16[4,96,96]{2,1,0:T(8,128)(2,1)S(1)}, u32[]{:S(2)}, u32[]{:S(2)}) collective-permute-start(bf16[4,96,96]{2,1,0:T(8,128)(2,1)S(1)} %copy-done.11), channel_id=1, source_target_pairs={{0,1},{1,0},{2,3},{3,2},{4,5},{5,4},{6,7},{7,6},{8,9},{9,8},{10,11... | collective-permute-start | bytes 221192 | tf_op jit(solution)/shard_map/ppermute | solution.py:575
  101.3 5.6 %collective-permute-done.24.other = bf16[4,96,96]{2,1,0:T(8,128)(2,1)S(1)} collective-permute-done((bf16[4,96,96]{2,1,0:T(8,128)(2,1)S(1)}, bf16[4,96,96]{2,1,0:T(8,128)(2,1)S(1)}, u32[]{:S(2)}, u32[]{:S(2)}) %collective-permute-start.24) | collective-permute-done | bytes 73760 | tf_op jit(solution)/shard_map/ppermute | solution.py:575
  108.8 5.1 %collective-permute-done.26.rest_2_ = bf16[8,96,96]{2,1,0:T(8,128)(2,1)S(1)} collective-permute-done((bf16[8,96,96]{2,1,0:T(8,128)(2,1)S(1)}, bf16[8,96,96]{2,1,0:T(8,128)(2,1)S(1)}, u32[]{:S(2)}, u32[]{:S(2)}) %collective-permute-start.26) | collective-permute-done | bytes 147488 | tf_op jit(solution)/shard_map/ppermute | solution.py:583
  113.8 1.4 %collective-permute-done.27.rest_3_ = bf16[8,96,96]{2,1,0:T(8,128)(2,1)S(1)} collective-permute-done((bf16[8,96,96]{2,1,0:T(8,128)(2,1)S(1)}, bf16[8,96,96]{2,1,0:T(8,128)(2,1)S(1)}, u32[]{:S(2)}, u32[]{:S(2)}) %collective-permute-start.27) | collective-permute-done | bytes 147488 | tf_op jit(solution)/shard_map/ppermute | solution.py:583
  115.3 1.3 %shard_map.117 = (f32[2,8,96,96]{3,2,1,0:T(8,128)}, f32[2,8,96,96]{3,2,1,0:T(8,128)}) custom-call(s32[1]{0:T(128)} %bitcast.4.lat_own, bf16[8,96,96]{2,1,0:T(8,128)(2,1)S(1)} %shard_map.116.rest_0_, bf16[8,96,96]{2,1,0:T(8,128)(2,1)S(1)} %collective-permute-done.25.rest_1_, bf16[8,96,96]{2,1,0:T(8,128)(2,1)S(1)} %collective-permute-done.26.rest_2_, ...), custom_call_target="tpu_custom_call" | custom-call | tf_op jit(solution)/shard_map/pallas_call | solution.py:65
  (75 shorter events, 21.1 us)
Async XLA Ops:
  2.3 8.9 %collective-permute-start = (bf16[128,384]{1,0:T(8,128)(2,1)S(1)}, bf16[128,384]{1,0:T(8,128)(2,1)S(1)}, u32[]{:S(2)}, u32[]{:S(2)}) collective-permute-start(bf16[128,384]{1,0:T(8,128)(2,1)S(1)} %get-tuple-element.41), channel_id=1, source_target_pairs={{0,1},{1,0},{2,3},{3,2},{4,5},{5,4},{6,7},{7,6},{8,9},{9,8},{10,11... | collective-permute-start | bytes 294920 | tf_op jit(solution)/shard_map/ppermute | solution.py:424
  5.4 9.5 %collective-permute-start.1 = (bf16[128,384]{1,0:T(8,128)(2,1)S(1)}, bf16[128,384]{1,0:T(8,128)(2,1)S(1)}, u32[]{:S(2)}, u32[]{:S(2)}) collective-permute-start(bf16[128,384]{1,0:T(8,128)(2,1)S(1)} %get-tuple-element.42), channel_id=1, source_target_pairs={{0,2},{1,3},{2,0},{3,1},{4,6},{5,7},{6,4},{7,5},{8,10},{9,11},{10,... | collective-permute-start | bytes 294920 | tf_op jit(solution)/shard_map/ppermute | solution.py:424
  7.0 10.5 %collective-permute-start.2 = (bf16[128,384]{1,0:T(8,128)(2,1)S(1)}, bf16[128,384]{1,0:T(8,128)(2,1)S(1)}, u32[]{:S(2)}, u32[]{:S(2)}) collective-permute-start(bf16[128,384]{1,0:T(8,128)(2,1)S(1)} %get-tuple-element.43), channel_id=1, source_target_pairs={{0,3},{1,2},{2,1},{3,0},{4,7},{5,6},{6,5},{7,4},{8,11},{9,10},{10,... | collective-permute-start | bytes 294920 | tf_op jit(solution)/shard_map/ppermute | solution.py:424
  7.0 10.5 %collective-permute-start.3 = (bf16[128,384]{1,0:T(8,128)(2,1)S(1)}, bf16[128,384]{1,0:T(8,128)(2,1)S(1)}, u32[]{:S(2)}, u32[]{:S(2)}) collective-permute-start(bf16[128,384]{1,0:T(8,128)(2,1)S(1)} %get-tuple-element.44), channel_id=1, source_target_pairs={{0,4},{1,5},{2,6},{3,7},{4,0},{5,1},{6,2},{7,3},{8,12},{9,13},{10,... | collective-permute-start | bytes 294920 | tf_op jit(solution)/shard_map/ppermute | solution.py:424
  9.9 15.2 %collective-permute-start.4 = (bf16[128,384]{1,0:T(8,128)(2,1)S(1)}, bf16[128,384]{1,0:T(8,128)(2,1)S(1)}, u32[]{:S(2)}, u32[]{:S(2)}) collective-permute-start(bf16[128,384]{1,0:T(8,128)(2,1)S(1)} %get-tuple-element.45), channel_id=1, source_target_pairs={{0,5},{1,4},{2,7},{3,6},{4,1},{5,0},{6,3},{7,2},{8,13},{9,12},{10,... | collective-permute-start | bytes 294920 | tf_op jit(solution)/shard_map/ppermute | solution.py:424
  11.2 13.9 %collective-permute-start.5 = (bf16[128,384]{1,0:T(8,128)(2,1)S(1)}, bf16[128,384]{1,0:T(8,128)(2,1)S(1)}, u32[]{:S(2)}, u32[]{:S(2)}) collective-permute-start(bf16[128,384]{1,0:T(8,128)(2,1)S(1)} %get-tuple-element.46), channel_id=1, source_target_pairs={{0,6},{1,7},{2,4},{3,5},{4,2},{5,3},{6,0},{7,1},{8,14},{9,15},{10,... | collective-permute-start | bytes 294920 | tf_op jit(solution)/shard_map/ppermute | solution.py:424
  14.8 10.3 %collective-permute-start.6 = (bf16[128,384]{1,0:T(8,128)(2,1)S(1)}, bf16[128,384]{1,0:T(8,128)(2,1)S(1)}, u32[]{:S(2)}, u32[]{:S(2)}) collective-permute-start(bf16[128,384]{1,0:T(8,128)(2,1)S(1)} %get-tuple-element.47), channel_id=1, source_target_pairs={{0,7},{1,6},{2,5},{3,4},{4,3},{5,2},{6,1},{7,0},{8,15},{9,14},{10,... | collective-permute-start | bytes 294920 | tf_op jit(solution)/shard_map/ppermute | solution.py:424
  26.3 26.2 %all-to-all-start = ((bf16[8,128,384]{2,1,0:T(8,128)(2,1)}), bf16[8,128,384]{2,1,0:T(8,128)(2,1)S(1)}, u32[]{:S(2)}, u32[]{:S(2)}) async-start(bf16[8,128,384]{2,1,0:T(8,128)(2,1)} %shard_map.106), calls=%async_computation | async-start | bytes 1572864 | tf_op jit(solution)/shard_map/all_to_all | solution.py:419
  32.9 1.9 %collective-permute-start.7 = (bf16[128,384]{1,0:T(8,128)(2,1)S(1)}, bf16[128,384]{1,0:T(8,128)(2,1)S(1)}, u32[]{:S(2)}, u32[]{:S(2)}) collective-permute-start(bf16[128,384]{1,0:T(8,128)(2,1)S(1)} %get-tuple-element.49), channel_id=1, source_target_pairs={{0,8},{1,9},{2,10},{3,11},{4,12},{5,13},{6,14},{7,15},{8,0},{9,1},... | collective-permute-start | bytes 294920 | tf_op jit(solution)/shard_map/ppermute | solution.py:424
  32.9 5.7 %collective-permute-start.8 = (bf16[128,384]{1,0:T(8,128)(2,1)S(1)}, bf16[128,384]{1,0:T(8,128)(2,1)S(1)}, u32[]{:S(2)}, u32[]{:S(2)}) collective-permute-start(bf16[128,384]{1,0:T(8,128)(2,1)S(1)} %get-tuple-element.50), channel_id=1, source_target_pairs={{0,16},{1,17},{2,18},{3,19},{4,20},{5,21},{6,22},{7,23},{8,24},{9,... | collective-permute-start | bytes 294920 | tf_op jit(solution)/shard_map/ppermute | solution.py:424
  34.5 5.3 %collective-permute-start.9 = (bf16[128,384]{1,0:T(8,128)(2,1)S(1)}, bf16[128,384]{1,0:T(8,128)(2,1)S(1)}, u32[]{:S(2)}, u32[]{:S(2)}) collective-permute-start(bf16[128,384]{1,0:T(8,128)(2,1)S(1)} %get-tuple-element.51), channel_id=1, source_target_pairs={{0,24},{1,25},{2,26},{3,27},{4,28},{5,29},{6,30},{7,31},{8,16},{9,... | collective-permute-start | bytes 294920 | tf_op jit(solution)/shard_map/ppermute | solution.py:424
  43.5 9.5 %collective-permute-start.10 = (bf16[128,384]{1,0:T(8,128)(2,1)S(1)}, bf16[128,384]{1,0:T(8,128)(2,1)S(1)}, u32[]{:S(2)}, u32[]{:S(2)}) collective-permute-start(bf16[128,384]{1,0:T(8,128)(2,1)S(1)} %get-tuple-element.53), channel_id=1, source_target_pairs={{0,8},{1,9},{2,10},{3,11},{4,12},{5,13},{6,14},{7,15},{8,0},{9,1},... | collective-permute-start | bytes 294920 | tf_op jit(solution)/shard_map/ppermute | solution.py:424
  44.1 8.9 %collective-permute-start.11 = (bf16[128,384]{1,0:T(8,128)(2,1)S(1)}, bf16[128,384]{1,0:T(8,128)(2,1)S(1)}, u32[]{:S(2)}, u32[]{:S(2)}) collective-permute-start(bf16[128,384]{1,0:T(8,128)(2,1)S(1)} %get-tuple-element.54), channel_id=1, source_target_pairs={{0,16},{1,17},{2,18},{3,19},{4,20},{5,21},{6,22},{7,23},{8,24},{9,... | collective-permute-start | bytes 294920 | tf_op jit(solution)/shard_map/ppermute | solution.py:424
  45.6 7.4 %collective-permute-start.12 = (bf16[128,384]{1,0:T(8,128)(2,1)S(1)}, bf16[128,384]{1,0:T(8,128)(2,1)S(1)}, u32[]{:S(2)}, u32[]{:S(2)}) collective-permute-start(bf16[128,384]{1,0:T(8,128)(2,1)S(1)} %get-tuple-element.55), channel_id=1, source_target_pairs={{0,24},{1,25},{2,26},{3,27},{4,28},{5,29},{6,30},{7,31},{8,16},{9,... | collective-permute-start | bytes 294920 | tf_op jit(solution)/shard_map/ppermute | solution.py:424
  54.7 37.3 %all-to-all-start.1 = ((bf16[8,128,384]{2,1,0:T(8,128)(2,1)}), bf16[8,128,384]{2,1,0:T(8,128)(2,1)S(1)}, u32[]{:S(2)}, u32[]{:S(2)}) async-start(bf16[8,128,384]{2,1,0:T(8,128)(2,1)} %shard_map.108), calls=%async_computation.1 | async-start | bytes 1572864 | tf_op jit(solution)/shard_map/all_to_all | solution.py:419
  58.3 1.9 %collective-permute-start.13 = (bf16[128,384]{1,0:T(8,128)(2,1)S(1)}, bf16[128,384]{1,0:T(8,128)(2,1)S(1)}, u32[]{:S(2)}, u32[]{:S(2)}) collective-permute-start(bf16[128,384]{1,0:T(8,128)(2,1)S(1)} %get-tuple-element.58), channel_id=1, source_target_pairs={{0,8},{1,9},{2,10},{3,11},{4,12},{5,13},{6,14},{7,15},{8,0},{9,1},... | collective-permute-start | bytes 294920 | tf_op jit(solution)/shard_map/ppermute | solution.py:424
  58.4 5.7 %collective-permute-start.14 = (bf16[128,384]{1,0:T(8,128)(2,1)S(1)}, bf16[128,384]{1,0:T(8,128)(2,1)S(1)}, u32[]{:S(2)}, u32[]{:S(2)}) collective-permute-start(bf16[128,384]{1,0:T(8,128)(2,1)S(1)} %get-tuple-element.59), channel_id=1, source_target_pairs={{0,16},{1,17},{2,18},{3,19},{4,20},{5,21},{6,22},{7,23},{8,24},{9,... | collective-permute-start | bytes 294920 | tf_op jit(solution)/shard_map/ppermute | solution.py:424
  59.9 5.3 %collective-permute-start.15 = (bf16[128,384]{1,0:T(8,128)(2,1)S(1)}, bf16[128,384]{1,0:T(8,128)(2,1)S(1)}, u32[]{:S(2)}, u32[]{:S(2)}) collective-permute-start(bf16[128,384]{1,0:T(8,128)(2,1)S(1)} %get-tuple-element.60), channel_id=1, source_target_pairs={{0,24},{1,25},{2,26},{3,27},{4,28},{5,29},{6,30},{7,31},{8,16},{9,... | collective-permute-start | bytes 294920 | tf_op jit(solution)/shard_map/ppermute | solution.py:424
  69.3 2.1 %collective-permute-start.16 = (bf16[96,96]{1,0:T(8,128)(2,1)S(1)}, bf16[96,96]{1,0:T(8,128)(2,1)S(1)}, u32[]{:S(2)}, u32[]{:S(2)}) collective-permute-start(bf16[96,96]{1,0:T(8,128)(2,1)S(1)} %get-tuple-element.63), channel_id=1, source_target_pairs={{0,8},{8,0},{16,24},{24,16},{1,9},{9,1},{17,25},{25,17},{2,10},{10... | collective-permute-start | bytes 55304 | tf_op jit(solution)/shard_map/ppermute | solution.py:424
  69.9 3.8 %collective-permute-start.17 = (bf16[96,96]{1,0:T(8,128)(2,1)S(1)}, bf16[96,96]{1,0:T(8,128)(2,1)S(1)}, u32[]{:S(2)}, u32[]{:S(2)}) collective-permute-start(bf16[96,96]{1,0:T(8,128)(2,1)S(1)} %get-tuple-element.64), channel_id=1, source_target_pairs={{0,16},{8,24},{16,0},{24,8},{1,17},{9,25},{17,1},{25,9},{2,18},{10... | collective-permute-start | bytes 55304 | tf_op jit(solution)/shard_map/ppermute | solution.py:424
  71.4 3.5 %collective-permute-start.18 = (bf16[96,96]{1,0:T(8,128)(2,1)S(1)}, bf16[96,96]{1,0:T(8,128)(2,1)S(1)}, u32[]{:S(2)}, u32[]{:S(2)}) collective-permute-start(bf16[96,96]{1,0:T(8,128)(2,1)S(1)} %get-tuple-element.65), channel_id=1, source_target_pairs={{0,24},{8,16},{16,8},{24,0},{1,25},{9,17},{17,9},{25,1},{2,26},{10... | collective-permute-start | bytes 55304 | tf_op jit(solution)/shard_map/ppermute | solution.py:424
  76.5 10.6 %collective-permute-start.21 = (bf16[128,384]{1,0:T(8,128)(2,1)S(1)}, bf16[128,384]{1,0:T(8,128)(2,1)S(1)}, u32[]{:S(2)}, u32[]{:S(2)}) collective-permute-start(bf16[128,384]{1,0:T(8,128)(2,1)S(1)} %get-tuple-element.69), channel_id=1, source_target_pairs={{0,8},{1,9},{2,10},{3,11},{4,12},{5,13},{6,14},{7,15},{8,0},{9,1},... | collective-permute-start | bytes 294920 | tf_op jit(solution)/shard_map/ppermute | solution.py:424
  76.7 10.5 %collective-permute-start.22 = (bf16[128,384]{1,0:T(8,128)(2,1)S(1)}, bf16[128,384]{1,0:T(8,128)(2,1)S(1)}, u32[]{:S(2)}, u32[]{:S(2)}) collective-permute-start(bf16[128,384]{1,0:T(8,128)(2,1)S(1)} %get-tuple-element.70), channel_id=1, source_target_pairs={{0,16},{1,17},{2,18},{3,19},{4,20},{5,21},{6,22},{7,23},{8,24},{9,... | collective-permute-start | bytes 294920 | tf_op jit(solution)/shard_map/ppermute | solution.py:424
  77.5 9.6 %collective-permute-start.23 = (bf16[128,384]{1,0:T(8,128)(2,1)S(1)}, bf16[128,384]{1,0:T(8,128)(2,1)S(1)}, u32[]{:S(2)}, u32[]{:S(2)}) collective-permute-start(bf16[128,384]{1,0:T(8,128)(2,1)S(1)} %get-tuple-element.71), channel_id=1, source_target_pairs={{0,24},{1,25},{2,26},{3,27},{4,28},{5,29},{6,30},{7,31},{8,16},{9,... | collective-permute-start | bytes 294920 | tf_op jit(solution)/shard_map/ppermute | solution.py:424
  78.5 3.8 %collective-permute-start.19 = (bf16[1,96,96]{2,1,0:T(8,128)(2,1)S(1)}, bf16[1,96,96]{2,1,0:T(8,128)(2,1)S(1)}, u32[]{:S(2)}, u32[]{:S(2)}) collective-permute-start(bf16[1,96,96]{2,1,0:T(8,128)(2,1)S(1)} %shard_map.111.first.rest_0_), channel_id=1, source_target_pairs={{0,2},{1,3},{2,0},{3,1},{4,6},{5,7},{6,4},{7,5},{8,10},{9,11},{10,... | collective-permute-start | bytes 55304 | tf_op jit(solution)/shard_map/ppermute | solution.py:566
  84.3 5.6 %collective-permute-start.20 = (bf16[2,96,96]{2,1,0:T(8,128)(2,1)}, bf16[2,96,96]{2,1,0:T(8,128)(2,1)S(1)}, u32[]{:S(2)}, u32[]{:S(2)}) collective-permute-start(bf16[2,96,96]{2,1,0:T(8,128)(2,1)} %shard_map.112.first), channel_id=1, source_target_pairs={{0,4},{1,5},{2,6},{3,7},{4,0},{5,1},{6,2},{7,3},{8,12},{9,13},{10,... | collective-permute-start | bytes 110600 | tf_op jit(solution)/shard_map/ppermute | solution.py:566
  92.0 24.9 %all-to-all-start.2 = ((bf16[8,128,384]{2,1,0:T(8,128)(2,1)}), bf16[8,128,384]{2,1,0:T(8,128)(2,1)S(1)}, u32[]{:S(2)}, u32[]{:S(2)}) async-start(bf16[8,128,384]{2,1,0:T(8,128)(2,1)} %get-tuple-element.72), calls=%async_computation.2 | async-start | bytes 1572864 | tf_op jit(solution)/shard_map/all_to_all | solution.py:419
  98.2 8.7 %collective-permute-start.24 = (bf16[4,96,96]{2,1,0:T(8,128)(2,1)S(1)}, bf16[4,96,96]{2,1,0:T(8,128)(2,1)S(1)}, u32[]{:S(2)}, u32[]{:S(2)}) collective-permute-start(bf16[4,96,96]{2,1,0:T(8,128)(2,1)S(1)} %copy-done.11), channel_id=1, source_target_pairs={{0,1},{1,0},{2,3},{3,2},{4,5},{5,4},{6,7},{7,6},{8,9},{9,8},{10,11... | collective-permute-start | bytes 221192 | tf_op jit(solution)/shard_map/ppermute | solution.py:575
  101.3 15.6 %copy-start.1 = (bf16[32,16,768]{2,1,0:T(8,128)(2,1)S(1)}, bf16[32,16,768]{2,1,0:T(8,128)(2,1)}, u32[]{:S(2)}) copy-start(bf16[32,16,768]{2,1,0:T(8,128)(2,1)} %base.3) | copy-start | bytes 2359300
  108.1 5.7 %collective-permute-start.26 = (bf16[8,96,96]{2,1,0:T(8,128)(2,1)S(1)}, bf16[8,96,96]{2,1,0:T(8,128)(2,1)S(1)}, u32[]{:S(2)}, u32[]{:S(2)}) collective-permute-start(bf16[8,96,96]{2,1,0:T(8,128)(2,1)S(1)} %shard_map.116.rest_0_), channel_id=1, source_target_pairs={{0,16},{8,24},{16,0},{24,8},{1,17},{9,25},{17,1},{25,9},{2,18},{10... | collective-permute-start | bytes 442376 | tf_op jit(solution)/shard_map/ppermute | solution.py:583
  108.8 5.1 %collective-permute-start.25 = (bf16[8,96,96]{2,1,0:T(8,128)(2,1)S(1)}, bf16[8,96,96]{2,1,0:T(8,128)(2,1)S(1)}, u32[]{:S(2)}, u32[]{:S(2)}) collective-permute-start(bf16[8,96,96]{2,1,0:T(8,128)(2,1)S(1)} %shard_map.116.rest_0_), channel_id=1, source_target_pairs={{0,8},{8,0},{16,24},{24,16},{1,9},{9,1},{17,25},{25,17},{2,10},{10... | collective-permute-start | bytes 442376 | tf_op jit(solution)/shard_map/ppermute | solution.py:583
  113.8 1.4 %collective-permute-start.27 = (bf16[8,96,96]{2,1,0:T(8,128)(2,1)S(1)}, bf16[8,96,96]{2,1,0:T(8,128)(2,1)S(1)}, u32[]{:S(2)}, u32[]{:S(2)}) collective-permute-start(bf16[8,96,96]{2,1,0:T(8,128)(2,1)S(1)} %collective-permute-done.26.rest_2_), channel_id=1, source_target_pairs={{0,8},{8,0},{16,24},{24,16},{1,9},{9,1},{17,25},{25,17},{2,10},{10... | collective-permute-start | bytes 442376 | tf_op jit(solution)/shard_map/ppermute | solution.py:583
  (13 other events, 61.0 us)

commit v4 on v3

--- a/solution.py
+++ b/solution.py
@@ -80,6 +80,7 @@
         in_specs=[anywhere] * (1 + len(anchors)),
         out_specs=anywhere,
         input_output_aliases={0: 0},
+        compiler_params=pltpu.CompilerParams(vmem_limit_bytes=8 * MIB),
     )(source, *anchors)
 
 
@@ -103,6 +104,7 @@
         in_specs=[near, near] + [anywhere] * len(passed),
         out_specs=[near] + [anywhere] * len(passed),
         input_output_aliases={2: 1} if gated else {},
+        compiler_params=pltpu.CompilerParams(vmem_limit_bytes=8 * MIB),
     )(first, second, *passed)
     return results[0], results[1] if gated else source
 
@@ -592,7 +594,7 @@
         gathered,
         [pltpu.VMEM((4, NB, BS, BS), f32)],
     )
-    feature_grad = unpack(returned, cotangent, [grad_first])
+    feature_grad = unpack(returned, cotangent)
     return (mixed_field, feature_grad, grad_first, grad_second)
 
 

time: 120 us -> 117 us (0.975)
  Pallas kernels: 22.7 us -> 20.7 us
  local copies, waits for them, and re-layouts: 5.47 us -> 3.6 us
    pallas_call x2, Pallas kernels: 2.86 us -> 0.03 us  [join_gate(): pl.pallas_call(join_body, out_shape=[joined] + [jax.ShapeDtypeStruct(valu...]
    all_to_all x3, waiting for transfers between devices: 7.26 us -> 10 us  [exchange(): lax.all_to_all(source, 'lon', split_axis=0, concat_axis=0, tiled=True)]
    unnamed x28 -> x16, local copies, waits for them, and re-layouts: 5.47 us -> 3.6 us
    ppermute x3, waiting for transfers between devices: 6.49 us -> 4.96 us  [shards(): moved = lax.ppermute(gathered[offset], 'lat', line_pairs(lat_count)(step))]
  transfers between devices with their start and end apart: 31 -> 31, of which waited for: 14 -> 13; matrix products, arithmetic and copies ran while one was open for 0% -> 0% of each run, Pallas kernels for 15% -> 14%
where the time goes in v4:
time: 117 us
  starting transfers between devices  46.4 us (40%)
  waiting for transfers between devices  44.9 us (38%)
  Pallas kernels  20.7 us (18%)
  local copies, waits for them, and re-layouts  3.6 us (3%)
    ppermute x22, starting transfers between devices, swap(): lax.ppermute(piece, axes, partners(offset))  22.5 us
    ppermute x22, waiting for transfers between devices, swap(): lax.ppermute(piece, axes, partners(offset))  21.1 us
    pallas_call x14, Pallas kernels, kernel_call(): pl.pallas_call(body, out_shape=out_shape, in_specs=in_specs, out_specs=[s...  20.7 us
    all_to_all x3, starting transfers between devices, exchange(): lax.all_to_all(source, 'lon', split_axis=0, concat_axis=0, tiled=True)  16.3 us
    all_to_all x3, waiting for transfers between devices, exchange(): lax.all_to_all(source, 'lon', split_axis=0, concat_axis=0, tiled=True)  10 us
    ppermute x1, waiting for transfers between devices, shards(): lax.ppermute(near, 'lon', lon_pairs(1))  5.59 us
    ppermute x3, waiting for transfers between devices, shards(): moved = lax.ppermute(gathered[offset], 'lat', line_pairs(lat_count)(step))  4.96 us
    ppermute x2, starting transfers between devices, shards(): moved = lax.ppermute(near, 'lon', lon_pairs(step))  4.82 us
  transfers between devices with their start and end apart: 31, of which 13 were waited for; matrix products, arithmetic and copies ran while one was open for 0% of the time, Pallas kernels for 14%

profile of v4, /device:TPU:0, one launch (start us, length us, event | category | flops | bytes accessed | tf_op | source)
XLA Modules:
  0.0 116.6 jit_solution(2496276896058351082)
XLA Ops:
  0.6 1.7 %shard_map.102 = (bf16[128,384]{1,0:T(8,128)(2,1)S(1)}, bf16[128,384]{1,0:T(8,128)(2,1)S(1)}, bf16[128,384]{1,0:T(8,128)(2,1)S(1)}, bf16[128,384]{1,0:T(8,128)(2...) custom-call(s32[1]{0:T(128)} %bitcast.3.own.own_in, ...), custom_call_target="tpu_custom_call" | custom-call | tf_op jit(solution)/shard_map/pallas_call | solution.py:65
  2.3 3.0 %collective-permute-start = (bf16[128,384]{1,0:T(8,128)(2,1)S(1)}, bf16[128,384]{1,0:T(8,128)(2,1)S(1)}, u32[]{:S(2)}, u32[]{:S(2)}) collective-permute-start(bf16[128,384]{1,0:T(8,128)(2,1)S(1)} %get-tuple-element.41), channel_id=1, source_target_pairs={{0,1},{1,0},{2,3},{3,2},{4,5},{5,4},{6,7},{7,6},{8,9},{9,8},{10,11... | collective-permute-start | bytes 294920 | tf_op jit(solution)/shard_map/ppermute | solution.py:426
  5.4 1.6 %collective-permute-start.1 = (bf16[128,384]{1,0:T(8,128)(2,1)S(1)}, bf16[128,384]{1,0:T(8,128)(2,1)S(1)}, u32[]{:S(2)}, u32[]{:S(2)}) collective-permute-start(bf16[128,384]{1,0:T(8,128)(2,1)S(1)} %get-tuple-element.42), channel_id=1, source_target_pairs={{0,2},{1,3},{2,0},{3,1},{4,6},{5,7},{6,4},{7,5},{8,10},{9,11},{10,... | collective-permute-start | bytes 294920 | tf_op jit(solution)/shard_map/ppermute | solution.py:426
  7.0 3.0 %collective-permute-start.3 = (bf16[128,384]{1,0:T(8,128)(2,1)S(1)}, bf16[128,384]{1,0:T(8,128)(2,1)S(1)}, u32[]{:S(2)}, u32[]{:S(2)}) collective-permute-start(bf16[128,384]{1,0:T(8,128)(2,1)S(1)} %get-tuple-element.44), channel_id=1, source_target_pairs={{0,4},{1,5},{2,6},{3,7},{4,0},{5,1},{6,2},{7,3},{8,12},{9,13},{10,... | collective-permute-start | bytes 294920 | tf_op jit(solution)/shard_map/ppermute | solution.py:426
  9.9 1.3 %collective-permute-start.4 = (bf16[128,384]{1,0:T(8,128)(2,1)S(1)}, bf16[128,384]{1,0:T(8,128)(2,1)S(1)}, u32[]{:S(2)}, u32[]{:S(2)}) collective-permute-start(bf16[128,384]{1,0:T(8,128)(2,1)S(1)} %get-tuple-element.45), channel_id=1, source_target_pairs={{0,5},{1,4},{2,7},{3,6},{4,1},{5,0},{6,3},{7,2},{8,13},{9,12},{10,... | collective-permute-start | bytes 294920 | tf_op jit(solution)/shard_map/ppermute | solution.py:426
  11.2 3.6 %collective-permute-start.5 = (bf16[128,384]{1,0:T(8,128)(2,1)S(1)}, bf16[128,384]{1,0:T(8,128)(2,1)S(1)}, u32[]{:S(2)}, u32[]{:S(2)}) collective-permute-start(bf16[128,384]{1,0:T(8,128)(2,1)S(1)} %get-tuple-element.46), channel_id=1, source_target_pairs={{0,6},{1,7},{2,4},{3,5},{4,2},{5,3},{6,0},{7,1},{8,14},{9,15},{10,... | collective-permute-start | bytes 294920 | tf_op jit(solution)/shard_map/ppermute | solution.py:426
  14.8 2.6 %shard_map.105.refs_0_ = bf16[8,128,384]{2,1,0:T(8,128)(2,1)} custom-call(s32[1]{0:T(128)} %bitcast.3.own.own_in, bf16[32,16,768]{2,1,0:T(8,128)(2,1)} %base.3), custom_call_target="tpu_custom_call" | custom-call | tf_op jit(solution)/shard_map/pallas_call | solution.py:65
  17.5 7.6 %collective-permute-done.4.rest_5_ = bf16[128,384]{1,0:T(8,128)(2,1)S(1)} collective-permute-done((bf16[128,384]{1,0:T(8,128)(2,1)S(1)}, bf16[128,384]{1,0:T(8,128)(2,1)S(1)}, u32[]{:S(2)}, u32[]{:S(2)}) %collective-permute-start.4) | collective-permute-done | bytes 98336 | tf_op jit(solution)/shard_map/ppermute | solution.py:426
  25.7 6.6 %all-to-all-start = ((bf16[8,128,384]{2,1,0:T(8,128)(2,1)}), bf16[8,128,384]{2,1,0:T(8,128)(2,1)S(1)}, u32[]{:S(2)}, u32[]{:S(2)}) async-start(bf16[8,128,384]{2,1,0:T(8,128)(2,1)} %shard_map.106), calls=%async_computation | async-start | bytes 1572864 | tf_op jit(solution)/shard_map/all_to_all | solution.py:421
  32.3 1.6 %collective-permute-start.8 = (bf16[128,384]{1,0:T(8,128)(2,1)S(1)}, bf16[128,384]{1,0:T(8,128)(2,1)S(1)}, u32[]{:S(2)}, u32[]{:S(2)}) collective-permute-start(bf16[128,384]{1,0:T(8,128)(2,1)S(1)} %get-tuple-element.50), channel_id=1, source_target_pairs={{0,16},{1,17},{2,18},{3,19},{4,20},{5,21},{6,22},{7,23},{8,24},{9,... | collective-permute-start | bytes 294920 | tf_op jit(solution)/shard_map/ppermute | solution.py:426
  34.2 3.8 %collective-permute-done.8.rest_2_ = bf16[128,384]{1,0:T(8,128)(2,1)S(1)} collective-permute-done((bf16[128,384]{1,0:T(8,128)(2,1)S(1)}, bf16[128,384]{1,0:T(8,128)(2,1)S(1)}, u32[]{:S(2)}, u32[]{:S(2)}) %collective-permute-start.8) | collective-permute-done | bytes 98336 | tf_op jit(solution)/shard_map/ppermute | solution.py:426
  39.2 3.7 %shard_map.104 = (bf16[128,384]{1,0:T(8,128)(2,1)S(1)}, bf16[128,384]{1,0:T(8,128)(2,1)S(1)}, bf16[128,384]{1,0:T(8,128)(2,1)S(1)}, bf16[128,384]{1,0:T(8,128)(2...) custom-call(s32[1]{0:T(128)} %bitcast.own_out.member.own_in, s32[1]{0:T(128)} %bitcast.1.first_mode, ...), custom_call_target="tpu_custom_call" | custom-call | tf_op jit(solution)/shard_map/pallas_call | solution.py:65
  43.5 1.5 %collective-permute-start.11 = (bf16[128,384]{1,0:T(8,128)(2,1)S(1)}, bf16[128,384]{1,0:T(8,128)(2,1)S(1)}, u32[]{:S(2)}, u32[]{:S(2)}) collective-permute-start(bf16[128,384]{1,0:T(8,128)(2,1)S(1)} %get-tuple-element.54), channel_id=1, source_target_pairs={{0,16},{1,17},{2,18},{3,19},{4,20},{5,21},{6,22},{7,23},{8,24},{9,... | collective-permute-start | bytes 294920 | tf_op jit(solution)/shard_map/ppermute | solution.py:426
  45.0 6.9 %all-to-all-done.rest_0_ = bf16[8,128,384]{2,1,0:T(8,128)(2,1)S(1)} async-done(((bf16[8,128,384]{2,1,0:T(8,128)(2,1)}), bf16[8,128,384]{2,1,0:T(8,128)(2,1)S(1)}, u32[]{:S(2)}, u32[]{:S(2)}) %all-to-all-start) | async-done | bytes 786464 | tf_op jit(solution)/shard_map/all_to_all | solution.py:421
  54.1 3.6 %all-to-all-start.1 = ((bf16[8,128,384]{2,1,0:T(8,128)(2,1)}), bf16[8,128,384]{2,1,0:T(8,128)(2,1)S(1)}, u32[]{:S(2)}, u32[]{:S(2)}) async-start(bf16[8,128,384]{2,1,0:T(8,128)(2,1)} %shard_map.108), calls=%async_computation.1 | async-start | bytes 1572864 | tf_op jit(solution)/shard_map/all_to_all | solution.py:421
  57.7 1.6 %collective-permute-start.14 = (bf16[128,384]{1,0:T(8,128)(2,1)S(1)}, bf16[128,384]{1,0:T(8,128)(2,1)S(1)}, u32[]{:S(2)}, u32[]{:S(2)}) collective-permute-start(bf16[128,384]{1,0:T(8,128)(2,1)S(1)} %get-tuple-element.59), channel_id=1, source_target_pairs={{0,16},{1,17},{2,18},{3,19},{4,20},{5,21},{6,22},{7,23},{8,24},{9,... | collective-permute-start | bytes 294920 | tf_op jit(solution)/shard_map/ppermute | solution.py:426
  59.6 3.8 %collective-permute-done.14.rest_2_ = bf16[128,384]{1,0:T(8,128)(2,1)S(1)} collective-permute-done((bf16[128,384]{1,0:T(8,128)(2,1)S(1)}, bf16[128,384]{1,0:T(8,128)(2,1)S(1)}, u32[]{:S(2)}, u32[]{:S(2)}) %collective-permute-start.14) | collective-permute-done | bytes 98336 | tf_op jit(solution)/shard_map/ppermute | solution.py:426
  64.6 4.1 %shard_map.110 = (bf16[8,128,192]{2,1,0:T(8,128)(2,1)S(1)}, bf16[192,192]{1,0:T(8,128)(2,1)S(1)}, bf16[96,96]{1,0:T(8,128)(2,1)S(1)}, bf16[96,96]{1,0:T(8,128)(2...) custom-call(s32[1]{0:T(128)} %bitcast.own_out.member.own_in, s32[1]{0:T(128)} %bitcast.1.first_mode, ...), custom_call_target="tpu_custom_call" | custom-call | tf_op jit(solution)/shard_map/pallas_call | solution.py:65
  69.3 1.5 %collective-permute-start.17 = (bf16[96,96]{1,0:T(8,128)(2,1)S(1)}, bf16[96,96]{1,0:T(8,128)(2,1)S(1)}, u32[]{:S(2)}, u32[]{:S(2)}) collective-permute-start(bf16[96,96]{1,0:T(8,128)(2,1)S(1)} %get-tuple-element.64), channel_id=1, source_target_pairs={{0,16},{8,24},{16,0},{24,8},{1,17},{9,25},{17,1},{25,9},{2,18},{10... | collective-permute-start | bytes 55304 | tf_op jit(solution)/shard_map/ppermute | solution.py:426
  70.8 2.3 %collective-permute-done.17.refs_2_ = bf16[96,96]{1,0:T(8,128)(2,1)S(1)} collective-permute-done((bf16[96,96]{1,0:T(8,128)(2,1)S(1)}, bf16[96,96]{1,0:T(8,128)(2,1)S(1)}, u32[]{:S(2)}, u32[]{:S(2)}) %collective-permute-start.17) | collective-permute-done | bytes 18464 | tf_op jit(solution)/shard_map/ppermute | solution.py:426
  74.3 1.6 %shard_map.113 = (bf16[128,384]{1,0:T(8,128)(2,1)S(1)}, bf16[128,384]{1,0:T(8,128)(2,1)S(1)}, bf16[128,384]{1,0:T(8,128)(2,1)S(1)}, bf16[128,384]{1,0:T(8,128)(2,1)S(1)}) custom-call(s32[1]{0:T(128)} %bitcast.own_out.member.own_in, bf16[256,256]{1,0:T(8,128)(2,1)S(1)} %copy-done.5, bf16[8,128,192]{2,1,0:T(8,128)(2,1)S(1)} %get-tuple-element.66.grad_pre, ...), custom_call_target="tpu_custom_call" | custom-call | tf_op jit(solution)/shard_map/pallas_call | solution.py:65
  77.8 1.9 %collective-permute-start.19 = (bf16[1,96,96]{2,1,0:T(8,128)(2,1)S(1)}, bf16[1,96,96]{2,1,0:T(8,128)(2,1)S(1)}, u32[]{:S(2)}, u32[]{:S(2)}) collective-permute-start(bf16[1,96,96]{2,1,0:T(8,128)(2,1)S(1)} %shard_map.111.first.rest_0_), channel_id=1, source_target_pairs={{0,2},{1,3},{2,0},{3,1},{4,6},{5,7},{6,4},{7,5},{8,10},{9,11},{10,... | collective-permute-start | bytes 55304 | tf_op jit(solution)/shard_map/ppermute | solution.py:568
  79.8 1.9 %collective-permute-done.19.second = bf16[1,96,96]{2,1,0:T(8,128)(2,1)S(1)} collective-permute-done((bf16[1,96,96]{2,1,0:T(8,128)(2,1)S(1)}, bf16[1,96,96]{2,1,0:T(8,128)(2,1)S(1)}, u32[]{:S(2)}, u32[]{:S(2)}) %collective-permute-start.19) | collective-permute-done | bytes 18464 | tf_op jit(solution)/shard_map/ppermute | solution.py:568
  81.7 2.9 %collective-permute-start.20 = (bf16[2,96,96]{2,1,0:T(8,128)(2,1)S(1)}, bf16[2,96,96]{2,1,0:T(8,128)(2,1)S(1)}, u32[]{:S(2)}, u32[]{:S(2)}) collective-permute-start(bf16[2,96,96]{2,1,0:T(8,128)(2,1)S(1)} %shard_map.112.first), channel_id=1, source_target_pairs={{0,4},{1,5},{2,6},{3,7},{4,0},{5,1},{6,2},{7,3},{8,12},{9,13},{10,... | collective-permute-start | bytes 110600 | tf_op jit(solution)/shard_map/ppermute | solution.py:568
  84.6 1.2 %shard_map.114.rest_0_ = bf16[8,128,384]{2,1,0:T(8,128)(2,1)} custom-call(s32[1]{0:T(128)} %bitcast.own_out.member.own_in, bf16[512,256]{1,0:T(8,128)(2,1)S(1)} %copy-done.7, bf16[128,384]{1,0:T(8,128)(2,1)S(1)} %get-tuple-element.68.rest_0_, bf16[128,384]{1,0:T(8,128)(2,1)S(1)} %collective-permute-done.21.rest_1_, ...), custom_call_target="tpu_custom_call" | custom-call | tf_op jit(solution)/shard_map/pallas_call | solution.py:65
  85.8 1.3 %collective-permute-done.20.second = bf16[2,96,96]{2,1,0:T(8,128)(2,1)S(1)} collective-permute-done((bf16[2,96,96]{2,1,0:T(8,128)(2,1)S(1)}, bf16[2,96,96]{2,1,0:T(8,128)(2,1)S(1)}, u32[]{:S(2)}, u32[]{:S(2)}) %collective-permute-start.20) | collective-permute-done | bytes 36896 | tf_op jit(solution)/shard_map/ppermute | solution.py:568
  89.2 6.1 %all-to-all-start.2 = ((bf16[8,128,384]{2,1,0:T(8,128)(2,1)}), bf16[8,128,384]{2,1,0:T(8,128)(2,1)S(1)}, u32[]{:S(2)}, u32[]{:S(2)}) async-start(bf16[8,128,384]{2,1,0:T(8,128)(2,1)} %copy-done.1), calls=%async_computation.2 | async-start | bytes 1572864 | tf_op jit(solution)/shard_map/all_to_all | solution.py:421
  95.3 2.0 %collective-permute-start.24 = (bf16[4,96,96]{2,1,0:T(8,128)(2,1)S(1)}, bf16[4,96,96]{2,1,0:T(8,128)(2,1)S(1)}, u32[]{:S(2)}, u32[]{:S(2)}) collective-permute-start(bf16[4,96,96]{2,1,0:T(8,128)(2,1)S(1)} %get-tuple-element.73.near), channel_id=1, source_target_pairs={{0,1},{1,0},{2,3},{3,2},{4,5},{5,4},{6,7},{7,6},{8,9},{9,8},{10,11... | collective-permute-start | bytes 221192 | tf_op jit(solution)/shard_map/ppermute | solution.py:577
  98.5 5.6 %collective-permute-done.24.other = bf16[4,96,96]{2,1,0:T(8,128)(2,1)S(1)} collective-permute-done((bf16[4,96,96]{2,1,0:T(8,128)(2,1)S(1)}, bf16[4,96,96]{2,1,0:T(8,128)(2,1)S(1)}, u32[]{:S(2)}, u32[]{:S(2)}) %collective-permute-start.24) | collective-permute-done | bytes 73760 | tf_op jit(solution)/shard_map/ppermute | solution.py:577
  106.0 5.0 %collective-permute-done.26.rest_2_ = bf16[8,96,96]{2,1,0:T(8,128)(2,1)S(1)} collective-permute-done((bf16[8,96,96]{2,1,0:T(8,128)(2,1)S(1)}, bf16[8,96,96]{2,1,0:T(8,128)(2,1)S(1)}, u32[]{:S(2)}, u32[]{:S(2)}) %collective-permute-start.26) | collective-permute-done | bytes 147488 | tf_op jit(solution)/shard_map/ppermute | solution.py:585
  111.0 3.1 %all-to-all-done.2.packed = bf16[8,128,384]{2,1,0:T(8,128)(2,1)S(1)} async-done(((bf16[8,128,384]{2,1,0:T(8,128)(2,1)}), bf16[8,128,384]{2,1,0:T(8,128)(2,1)S(1)}, u32[]{:S(2)}, u32[]{:S(2)}) %all-to-all-start.2) | async-done | bytes 786464 | tf_op jit(solution)/shard_map/all_to_all | solution.py:421
  115.2 1.3 %shard_map.118 = (f32[2,8,96,96]{3,2,1,0:T(8,128)}, f32[2,8,96,96]{3,2,1,0:T(8,128)}) custom-call(s32[1]{0:T(128)} %bitcast.4.lat_own, bf16[8,96,96]{2,1,0:T(8,128)(2,1)S(1)} %shard_map.117.rest_0_, bf16[8,96,96]{2,1,0:T(8,128)(2,1)S(1)} %collective-permute-done.25.rest_1_, bf16[8,96,96]{2,1,0:T(8,128)(2,1)S(1)} %collective-permute-done.26.rest_2_, ...), custom_call_target="tpu_custom_call" | custom-call | tf_op jit(solution)/shard_map/pallas_call | solution.py:65
  (63 shorter events, 16.4 us)
Async XLA Ops:
  2.3 8.9 %collective-permute-start = (bf16[128,384]{1,0:T(8,128)(2,1)S(1)}, bf16[128,384]{1,0:T(8,128)(2,1)S(1)}, u32[]{:S(2)}, u32[]{:S(2)}) collective-permute-start(bf16[128,384]{1,0:T(8,128)(2,1)S(1)} %get-tuple-element.41), channel_id=1, source_target_pairs={{0,1},{1,0},{2,3},{3,2},{4,5},{5,4},{6,7},{7,6},{8,9},{9,8},{10,11... | collective-permute-start | bytes 294920 | tf_op jit(solution)/shard_map/ppermute | solution.py:426
  5.4 9.5 %collective-permute-start.1 = (bf16[128,384]{1,0:T(8,128)(2,1)S(1)}, bf16[128,384]{1,0:T(8,128)(2,1)S(1)}, u32[]{:S(2)}, u32[]{:S(2)}) collective-permute-start(bf16[128,384]{1,0:T(8,128)(2,1)S(1)} %get-tuple-element.42), channel_id=1, source_target_pairs={{0,2},{1,3},{2,0},{3,1},{4,6},{5,7},{6,4},{7,5},{8,10},{9,11},{10,... | collective-permute-start | bytes 294920 | tf_op jit(solution)/shard_map/ppermute | solution.py:426
  7.0 10.5 %collective-permute-start.2 = (bf16[128,384]{1,0:T(8,128)(2,1)S(1)}, bf16[128,384]{1,0:T(8,128)(2,1)S(1)}, u32[]{:S(2)}, u32[]{:S(2)}) collective-permute-start(bf16[128,384]{1,0:T(8,128)(2,1)S(1)} %get-tuple-element.43), channel_id=1, source_target_pairs={{0,3},{1,2},{2,1},{3,0},{4,7},{5,6},{6,5},{7,4},{8,11},{9,10},{10,... | collective-permute-start | bytes 294920 | tf_op jit(solution)/shard_map/ppermute | solution.py:426
  7.0 10.5 %collective-permute-start.3 = (bf16[128,384]{1,0:T(8,128)(2,1)S(1)}, bf16[128,384]{1,0:T(8,128)(2,1)S(1)}, u32[]{:S(2)}, u32[]{:S(2)}) collective-permute-start(bf16[128,384]{1,0:T(8,128)(2,1)S(1)} %get-tuple-element.44), channel_id=1, source_target_pairs={{0,4},{1,5},{2,6},{3,7},{4,0},{5,1},{6,2},{7,3},{8,12},{9,13},{10,... | collective-permute-start | bytes 294920 | tf_op jit(solution)/shard_map/ppermute | solution.py:426
  9.9 15.2 %collective-permute-start.4 = (bf16[128,384]{1,0:T(8,128)(2,1)S(1)}, bf16[128,384]{1,0:T(8,128)(2,1)S(1)}, u32[]{:S(2)}, u32[]{:S(2)}) collective-permute-start(bf16[128,384]{1,0:T(8,128)(2,1)S(1)} %get-tuple-element.45), channel_id=1, source_target_pairs={{0,5},{1,4},{2,7},{3,6},{4,1},{5,0},{6,3},{7,2},{8,13},{9,12},{10,... | collective-permute-start | bytes 294920 | tf_op jit(solution)/shard_map/ppermute | solution.py:426
  11.2 13.9 %collective-permute-start.5 = (bf16[128,384]{1,0:T(8,128)(2,1)S(1)}, bf16[128,384]{1,0:T(8,128)(2,1)S(1)}, u32[]{:S(2)}, u32[]{:S(2)}) collective-permute-start(bf16[128,384]{1,0:T(8,128)(2,1)S(1)} %get-tuple-element.46), channel_id=1, source_target_pairs={{0,6},{1,7},{2,4},{3,5},{4,2},{5,3},{6,0},{7,1},{8,14},{9,15},{10,... | collective-permute-start | bytes 294920 | tf_op jit(solution)/shard_map/ppermute | solution.py:426
  14.8 10.3 %collective-permute-start.6 = (bf16[128,384]{1,0:T(8,128)(2,1)S(1)}, bf16[128,384]{1,0:T(8,128)(2,1)S(1)}, u32[]{:S(2)}, u32[]{:S(2)}) collective-permute-start(bf16[128,384]{1,0:T(8,128)(2,1)S(1)} %get-tuple-element.47), channel_id=1, source_target_pairs={{0,7},{1,6},{2,5},{3,4},{4,3},{5,2},{6,1},{7,0},{8,15},{9,14},{10,... | collective-permute-start | bytes 294920 | tf_op jit(solution)/shard_map/ppermute | solution.py:426
  25.7 26.2 %all-to-all-start = ((bf16[8,128,384]{2,1,0:T(8,128)(2,1)}), bf16[8,128,384]{2,1,0:T(8,128)(2,1)S(1)}, u32[]{:S(2)}, u32[]{:S(2)}) async-start(bf16[8,128,384]{2,1,0:T(8,128)(2,1)} %shard_map.106), calls=%async_computation | async-start | bytes 1572864 | tf_op jit(solution)/shard_map/all_to_all | solution.py:421
  32.3 1.9 %collective-permute-start.7 = (bf16[128,384]{1,0:T(8,128)(2,1)S(1)}, bf16[128,384]{1,0:T(8,128)(2,1)S(1)}, u32[]{:S(2)}, u32[]{:S(2)}) collective-permute-start(bf16[128,384]{1,0:T(8,128)(2,1)S(1)} %get-tuple-element.49), channel_id=1, source_target_pairs={{0,8},{1,9},{2,10},{3,11},{4,12},{5,13},{6,14},{7,15},{8,0},{9,1},... | collective-permute-start | bytes 294920 | tf_op jit(solution)/shard_map/ppermute | solution.py:426
  32.3 5.7 %collective-permute-start.8 = (bf16[128,384]{1,0:T(8,128)(2,1)S(1)}, bf16[128,384]{1,0:T(8,128)(2,1)S(1)}, u32[]{:S(2)}, u32[]{:S(2)}) collective-permute-start(bf16[128,384]{1,0:T(8,128)(2,1)S(1)} %get-tuple-element.50), channel_id=1, source_target_pairs={{0,16},{1,17},{2,18},{3,19},{4,20},{5,21},{6,22},{7,23},{8,24},{9,... | collective-permute-start | bytes 294920 | tf_op jit(solution)/shard_map/ppermute | solution.py:426
  33.9 5.3 %collective-permute-start.9 = (bf16[128,384]{1,0:T(8,128)(2,1)S(1)}, bf16[128,384]{1,0:T(8,128)(2,1)S(1)}, u32[]{:S(2)}, u32[]{:S(2)}) collective-permute-start(bf16[128,384]{1,0:T(8,128)(2,1)S(1)} %get-tuple-element.51), channel_id=1, source_target_pairs={{0,24},{1,25},{2,26},{3,27},{4,28},{5,29},{6,30},{7,31},{8,16},{9,... | collective-permute-start | bytes 294920 | tf_op jit(solution)/shard_map/ppermute | solution.py:426
  42.9 9.5 %collective-permute-start.10 = (bf16[128,384]{1,0:T(8,128)(2,1)S(1)}, bf16[128,384]{1,0:T(8,128)(2,1)S(1)}, u32[]{:S(2)}, u32[]{:S(2)}) collective-permute-start(bf16[128,384]{1,0:T(8,128)(2,1)S(1)} %get-tuple-element.53), channel_id=1, source_target_pairs={{0,8},{1,9},{2,10},{3,11},{4,12},{5,13},{6,14},{7,15},{8,0},{9,1},... | collective-permute-start | bytes 294920 | tf_op jit(solution)/shard_map/ppermute | solution.py:426
  43.5 8.9 %collective-permute-start.11 = (bf16[128,384]{1,0:T(8,128)(2,1)S(1)}, bf16[128,384]{1,0:T(8,128)(2,1)S(1)}, u32[]{:S(2)}, u32[]{:S(2)}) collective-permute-start(bf16[128,384]{1,0:T(8,128)(2,1)S(1)} %get-tuple-element.54), channel_id=1, source_target_pairs={{0,16},{1,17},{2,18},{3,19},{4,20},{5,21},{6,22},{7,23},{8,24},{9,... | collective-permute-start | bytes 294920 | tf_op jit(solution)/shard_map/ppermute | solution.py:426
  45.0 7.4 %collective-permute-start.12 = (bf16[128,384]{1,0:T(8,128)(2,1)S(1)}, bf16[128,384]{1,0:T(8,128)(2,1)S(1)}, u32[]{:S(2)}, u32[]{:S(2)}) collective-permute-start(bf16[128,384]{1,0:T(8,128)(2,1)S(1)} %get-tuple-element.55), channel_id=1, source_target_pairs={{0,24},{1,25},{2,26},{3,27},{4,28},{5,29},{6,30},{7,31},{8,16},{9,... | collective-permute-start | bytes 294920 | tf_op jit(solution)/shard_map/ppermute | solution.py:426
  54.1 35.1 %all-to-all-start.1 = ((bf16[8,128,384]{2,1,0:T(8,128)(2,1)}), bf16[8,128,384]{2,1,0:T(8,128)(2,1)S(1)}, u32[]{:S(2)}, u32[]{:S(2)}) async-start(bf16[8,128,384]{2,1,0:T(8,128)(2,1)} %shard_map.108), calls=%async_computation.1 | async-start | bytes 1572864 | tf_op jit(solution)/shard_map/all_to_all | solution.py:421
  57.7 1.9 %collective-permute-start.13 = (bf16[128,384]{1,0:T(8,128)(2,1)S(1)}, bf16[128,384]{1,0:T(8,128)(2,1)S(1)}, u32[]{:S(2)}, u32[]{:S(2)}) collective-permute-start(bf16[128,384]{1,0:T(8,128)(2,1)S(1)} %get-tuple-element.58), channel_id=1, source_target_pairs={{0,8},{1,9},{2,10},{3,11},{4,12},{5,13},{6,14},{7,15},{8,0},{9,1},... | collective-permute-start | bytes 294920 | tf_op jit(solution)/shard_map/ppermute | solution.py:426
  57.7 5.7 %collective-permute-start.14 = (bf16[128,384]{1,0:T(8,128)(2,1)S(1)}, bf16[128,384]{1,0:T(8,128)(2,1)S(1)}, u32[]{:S(2)}, u32[]{:S(2)}) collective-permute-start(bf16[128,384]{1,0:T(8,128)(2,1)S(1)} %get-tuple-element.59), channel_id=1, source_target_pairs={{0,16},{1,17},{2,18},{3,19},{4,20},{5,21},{6,22},{7,23},{8,24},{9,... | collective-permute-start | bytes 294920 | tf_op jit(solution)/shard_map/ppermute | solution.py:426
  59.3 5.3 %collective-permute-start.15 = (bf16[128,384]{1,0:T(8,128)(2,1)S(1)}, bf16[128,384]{1,0:T(8,128)(2,1)S(1)}, u32[]{:S(2)}, u32[]{:S(2)}) collective-permute-start(bf16[128,384]{1,0:T(8,128)(2,1)S(1)} %get-tuple-element.60), channel_id=1, source_target_pairs={{0,24},{1,25},{2,26},{3,27},{4,28},{5,29},{6,30},{7,31},{8,16},{9,... | collective-permute-start | bytes 294920 | tf_op jit(solution)/shard_map/ppermute | solution.py:426
  68.7 2.1 %collective-permute-start.16 = (bf16[96,96]{1,0:T(8,128)(2,1)S(1)}, bf16[96,96]{1,0:T(8,128)(2,1)S(1)}, u32[]{:S(2)}, u32[]{:S(2)}) collective-permute-start(bf16[96,96]{1,0:T(8,128)(2,1)S(1)} %get-tuple-element.63), channel_id=1, source_target_pairs={{0,8},{8,0},{16,24},{24,16},{1,9},{9,1},{17,25},{25,17},{2,10},{10... | collective-permute-start | bytes 55304 | tf_op jit(solution)/shard_map/ppermute | solution.py:426
  69.3 3.8 %collective-permute-start.17 = (bf16[96,96]{1,0:T(8,128)(2,1)S(1)}, bf16[96,96]{1,0:T(8,128)(2,1)S(1)}, u32[]{:S(2)}, u32[]{:S(2)}) collective-permute-start(bf16[96,96]{1,0:T(8,128)(2,1)S(1)} %get-tuple-element.64), channel_id=1, source_target_pairs={{0,16},{8,24},{16,0},{24,8},{1,17},{9,25},{17,1},{25,9},{2,18},{10... | collective-permute-start | bytes 55304 | tf_op jit(solution)/shard_map/ppermute | solution.py:426
  70.8 3.5 %collective-permute-start.18 = (bf16[96,96]{1,0:T(8,128)(2,1)S(1)}, bf16[96,96]{1,0:T(8,128)(2,1)S(1)}, u32[]{:S(2)}, u32[]{:S(2)}) collective-permute-start(bf16[96,96]{1,0:T(8,128)(2,1)S(1)} %get-tuple-element.65), channel_id=1, source_target_pairs={{0,24},{8,16},{16,8},{24,0},{1,25},{9,17},{17,9},{25,1},{2,26},{10... | collective-permute-start | bytes 55304 | tf_op jit(solution)/shard_map/ppermute | solution.py:426
  75.9 8.7 %collective-permute-start.21 = (bf16[128,384]{1,0:T(8,128)(2,1)S(1)}, bf16[128,384]{1,0:T(8,128)(2,1)S(1)}, u32[]{:S(2)}, u32[]{:S(2)}) collective-permute-start(bf16[128,384]{1,0:T(8,128)(2,1)S(1)} %get-tuple-element.69), channel_id=1, source_target_pairs={{0,8},{1,9},{2,10},{3,11},{4,12},{5,13},{6,14},{7,15},{8,0},{9,1},... | collective-permute-start | bytes 294920 | tf_op jit(solution)/shard_map/ppermute | solution.py:426
  76.1 8.5 %collective-permute-start.22 = (bf16[128,384]{1,0:T(8,128)(2,1)S(1)}, bf16[128,384]{1,0:T(8,128)(2,1)S(1)}, u32[]{:S(2)}, u32[]{:S(2)}) collective-permute-start(bf16[128,384]{1,0:T(8,128)(2,1)S(1)} %get-tuple-element.70), channel_id=1, source_target_pairs={{0,16},{1,17},{2,18},{3,19},{4,20},{5,21},{6,22},{7,23},{8,24},{9,... | collective-permute-start | bytes 294920 | tf_op jit(solution)/shard_map/ppermute | solution.py:426
  76.9 7.7 %collective-permute-start.23 = (bf16[128,384]{1,0:T(8,128)(2,1)S(1)}, bf16[128,384]{1,0:T(8,128)(2,1)S(1)}, u32[]{:S(2)}, u32[]{:S(2)}) collective-permute-start(bf16[128,384]{1,0:T(8,128)(2,1)S(1)} %get-tuple-element.71), channel_id=1, source_target_pairs={{0,24},{1,25},{2,26},{3,27},{4,28},{5,29},{6,30},{7,31},{8,16},{9,... | collective-permute-start | bytes 294920 | tf_op jit(solution)/shard_map/ppermute | solution.py:426
  77.8 3.8 %collective-permute-start.19 = (bf16[1,96,96]{2,1,0:T(8,128)(2,1)S(1)}, bf16[1,96,96]{2,1,0:T(8,128)(2,1)S(1)}, u32[]{:S(2)}, u32[]{:S(2)}) collective-permute-start(bf16[1,96,96]{2,1,0:T(8,128)(2,1)S(1)} %shard_map.111.first.rest_0_), channel_id=1, source_target_pairs={{0,2},{1,3},{2,0},{3,1},{4,6},{5,7},{6,4},{7,5},{8,10},{9,11},{10,... | collective-permute-start | bytes 55304 | tf_op jit(solution)/shard_map/ppermute | solution.py:568
  81.7 5.5 %collective-permute-start.20 = (bf16[2,96,96]{2,1,0:T(8,128)(2,1)S(1)}, bf16[2,96,96]{2,1,0:T(8,128)(2,1)S(1)}, u32[]{:S(2)}, u32[]{:S(2)}) collective-permute-start(bf16[2,96,96]{2,1,0:T(8,128)(2,1)S(1)} %shard_map.112.first), channel_id=1, source_target_pairs={{0,4},{1,5},{2,6},{3,7},{4,0},{5,1},{6,2},{7,3},{8,12},{9,13},{10,... | collective-permute-start | bytes 110600 | tf_op jit(solution)/shard_map/ppermute | solution.py:568
  89.2 24.9 %all-to-all-start.2 = ((bf16[8,128,384]{2,1,0:T(8,128)(2,1)}), bf16[8,128,384]{2,1,0:T(8,128)(2,1)S(1)}, u32[]{:S(2)}, u32[]{:S(2)}) async-start(bf16[8,128,384]{2,1,0:T(8,128)(2,1)} %copy-done.1), calls=%async_computation.2 | async-start | bytes 1572864 | tf_op jit(solution)/shard_map/all_to_all | solution.py:421
  95.3 8.7 %collective-permute-start.24 = (bf16[4,96,96]{2,1,0:T(8,128)(2,1)S(1)}, bf16[4,96,96]{2,1,0:T(8,128)(2,1)S(1)}, u32[]{:S(2)}, u32[]{:S(2)}) collective-permute-start(bf16[4,96,96]{2,1,0:T(8,128)(2,1)S(1)} %get-tuple-element.73.near), channel_id=1, source_target_pairs={{0,1},{1,0},{2,3},{3,2},{4,5},{5,4},{6,7},{7,6},{8,9},{9,8},{10,11... | collective-permute-start | bytes 221192 | tf_op jit(solution)/shard_map/ppermute | solution.py:577
  98.5 15.6 %copy-start.2 = (bf16[32,16,768]{2,1,0:T(8,128)(2,1)S(1)}, bf16[32,16,768]{2,1,0:T(8,128)(2,1)}, u32[]{:S(2)}) copy-start(bf16[32,16,768]{2,1,0:T(8,128)(2,1)} %base.3) | copy-start | bytes 2359300
  105.3 5.7 %collective-permute-start.26 = (bf16[8,96,96]{2,1,0:T(8,128)(2,1)S(1)}, bf16[8,96,96]{2,1,0:T(8,128)(2,1)S(1)}, u32[]{:S(2)}, u32[]{:S(2)}) collective-permute-start(bf16[8,96,96]{2,1,0:T(8,128)(2,1)S(1)} %shard_map.117.rest_0_), channel_id=1, source_target_pairs={{0,16},{8,24},{16,0},{24,8},{1,17},{9,25},{17,1},{25,9},{2,18},{10... | collective-permute-start | bytes 442376 | tf_op jit(solution)/shard_map/ppermute | solution.py:585
  106.0 9.2 %collective-permute-start.25 = (bf16[8,96,96]{2,1,0:T(8,128)(2,1)S(1)}, bf16[8,96,96]{2,1,0:T(8,128)(2,1)S(1)}, u32[]{:S(2)}, u32[]{:S(2)}) collective-permute-start(bf16[8,96,96]{2,1,0:T(8,128)(2,1)S(1)} %shard_map.117.rest_0_), channel_id=1, source_target_pairs={{0,8},{8,0},{16,24},{24,16},{1,9},{9,1},{17,25},{25,17},{2,10},{10... | collective-permute-start | bytes 442376 | tf_op jit(solution)/shard_map/ppermute | solution.py:585
  111.0 4.2 %collective-permute-start.27 = (bf16[8,96,96]{2,1,0:T(8,128)(2,1)S(1)}, bf16[8,96,96]{2,1,0:T(8,128)(2,1)S(1)}, u32[]{:S(2)}, u32[]{:S(2)}) collective-permute-start(bf16[8,96,96]{2,1,0:T(8,128)(2,1)S(1)} %collective-permute-done.26.rest_2_), channel_id=1, source_target_pairs={{0,8},{8,0},{16,24},{24,16},{1,9},{9,1},{17,25},{25,17},{2,10},{10... | collective-permute-start | bytes 442376 | tf_op jit(solution)/shard_map/ppermute | solution.py:585
  (7 other events, 36.0 us)

commit v5 on v4

--- a/solution.py
+++ b/solution.py
@@ -73,15 +73,15 @@
 
 
 def gate(source, anchors):
-    anywhere = pl.BlockSpec(memory_space=pl.ANY)
+    anywhere, distant = pl.BlockSpec(memory_space=pl.ANY), pl.BlockSpec(memory_space=pltpu.HBM)
     return pl.pallas_call(
         lambda *refs: None,
-        out_shape=jax.ShapeDtypeStruct(source.shape, source.dtype),
-        in_specs=[anywhere] * (1 + len(anchors)),
-        out_specs=anywhere,
+        out_shape=pltpu.HBM(source.shape, source.dtype),
+        in_specs=[distant] + [anywhere] * len(anchors),
+        out_specs=distant,
         input_output_aliases={0: 0},
         compiler_params=pltpu.CompilerParams(vmem_limit_bytes=8 * MIB),
-    )(source, *anchors)
+    )(pltpu.with_memory_space_constraint(source, pltpu.HBM), *anchors)
 
 
 def group_copies(source, target, sems):
@@ -95,14 +95,14 @@
 
 
 def join_gate(first, second, source, gated):
-    near, anywhere = pl.BlockSpec(memory_space=pltpu.VMEM), pl.BlockSpec(memory_space=pl.ANY)
+    near, distant = pl.BlockSpec(memory_space=pltpu.VMEM), pl.BlockSpec(memory_space=pltpu.HBM)
     joined = jax.ShapeDtypeStruct((2 * first.shape[0],) + first.shape[1:], first.dtype)
-    passed = [source] if gated else []
+    passed = [pltpu.with_memory_space_constraint(source, pltpu.HBM)] if gated else []
     results = pl.pallas_call(
         join_body,
-        out_shape=[joined] + [jax.ShapeDtypeStruct(value.shape, value.dtype) for value in passed],
-        in_specs=[near, near] + [anywhere] * len(passed),
-        out_specs=[near] + [anywhere] * len(passed),
+        out_shape=[joined] + [pltpu.HBM(value.shape, value.dtype) for value in passed],
+        in_specs=[near, near] + [distant] * len(passed),
+        out_specs=[near] + [distant] * len(passed),
         input_output_aliases={2: 1} if gated else {},
         compiler_params=pltpu.CompilerParams(vmem_limit_bytes=8 * MIB),
     )(first, second, *passed)

time: 117 us -> 115 us (0.983)
    unnamed x16 -> x14, local copies, waits for them, and re-layouts: 3.6 us -> 2.47 us
  transfers between devices with their start and end apart: 31 -> 31, of which waited for: 13 -> 13; matrix products, arithmetic and copies ran while one was open for 0% -> 0% of each run, Pallas kernels for 14% -> 13%
where the time goes in v5:
time: 115 us
  starting transfers between devices  46.4 us (40%)
  waiting for transfers between devices  44.9 us (39%)
  Pallas kernels  19.8 us (17%)
  local copies, waits for them, and re-layouts  2.47 us (2%)
    ppermute x22, starting transfers between devices, swap(): lax.ppermute(piece, axes, partners(offset))  22.5 us
    ppermute x22, waiting for transfers between devices, swap(): lax.ppermute(piece, axes, partners(offset))  21.2 us
    pallas_call x14, Pallas kernels, kernel_call(): pl.pallas_call(body, out_shape=out_shape, in_specs=in_specs, out_specs=[s...  19.8 us
    all_to_all x3, starting transfers between devices, exchange(): lax.all_to_all(source, 'lon', split_axis=0, concat_axis=0, tiled=True)  16.3 us
    all_to_all x3, waiting for transfers between devices, exchange(): lax.all_to_all(source, 'lon', split_axis=0, concat_axis=0, tiled=True)  10 us
    ppermute x1, waiting for transfers between devices, shards(): lax.ppermute(near, 'lon', lon_pairs(1))  5.59 us
    ppermute x3, waiting for transfers between devices, shards(): moved = lax.ppermute(gathered[offset], 'lat', line_pairs(lat_count)(step))  4.96 us
    ppermute x2, starting transfers between devices, shards(): moved = lax.ppermute(near, 'lon', lon_pairs(step))  4.82 us
  transfers between devices with their start and end apart: 31, of which 13 were waited for; matrix products, arithmetic and copies ran while one was open for 0% of the time, Pallas kernels for 13%

profile of v5, /device:TPU:0, one launch (start us, length us, event | category | flops | bytes accessed | tf_op | source)
XLA Modules:
  0.0 114.6 jit_solution(3628736564459978490)
XLA Ops:
  0.6 1.7 %shard_map.102 = (bf16[128,384]{1,0:T(8,128)(2,1)S(1)}, bf16[128,384]{1,0:T(8,128)(2,1)S(1)}, bf16[128,384]{1,0:T(8,128)(2,1)S(1)}, bf16[128,384]{1,0:T(8,128)(2...) custom-call(s32[1]{0:T(128)} %bitcast.3.own.own_in, ...), custom_call_target="tpu_custom_call" | custom-call | tf_op jit(solution)/shard_map/pallas_call | solution.py:65
  2.3 3.0 %collective-permute-start = (bf16[128,384]{1,0:T(8,128)(2,1)S(1)}, bf16[128,384]{1,0:T(8,128)(2,1)S(1)}, u32[]{:S(2)}, u32[]{:S(2)}) collective-permute-start(bf16[128,384]{1,0:T(8,128)(2,1)S(1)} %get-tuple-element.41), channel_id=1, source_target_pairs={{0,1},{1,0},{2,3},{3,2},{4,5},{5,4},{6,7},{7,6},{8,9},{9,8},{10,11... | collective-permute-start | bytes 294920 | tf_op jit(solution)/shard_map/ppermute | solution.py:426
  5.4 1.6 %collective-permute-start.1 = (bf16[128,384]{1,0:T(8,128)(2,1)S(1)}, bf16[128,384]{1,0:T(8,128)(2,1)S(1)}, u32[]{:S(2)}, u32[]{:S(2)}) collective-permute-start(bf16[128,384]{1,0:T(8,128)(2,1)S(1)} %get-tuple-element.42), channel_id=1, source_target_pairs={{0,2},{1,3},{2,0},{3,1},{4,6},{5,7},{6,4},{7,5},{8,10},{9,11},{10,... | collective-permute-start | bytes 294920 | tf_op jit(solution)/shard_map/ppermute | solution.py:426
  7.0 3.0 %collective-permute-start.3 = (bf16[128,384]{1,0:T(8,128)(2,1)S(1)}, bf16[128,384]{1,0:T(8,128)(2,1)S(1)}, u32[]{:S(2)}, u32[]{:S(2)}) collective-permute-start(bf16[128,384]{1,0:T(8,128)(2,1)S(1)} %get-tuple-element.44), channel_id=1, source_target_pairs={{0,4},{1,5},{2,6},{3,7},{4,0},{5,1},{6,2},{7,3},{8,12},{9,13},{10,... | collective-permute-start | bytes 294920 | tf_op jit(solution)/shard_map/ppermute | solution.py:426
  9.9 1.3 %collective-permute-start.4 = (bf16[128,384]{1,0:T(8,128)(2,1)S(1)}, bf16[128,384]{1,0:T(8,128)(2,1)S(1)}, u32[]{:S(2)}, u32[]{:S(2)}) collective-permute-start(bf16[128,384]{1,0:T(8,128)(2,1)S(1)} %get-tuple-element.45), channel_id=1, source_target_pairs={{0,5},{1,4},{2,7},{3,6},{4,1},{5,0},{6,3},{7,2},{8,13},{9,12},{10,... | collective-permute-start | bytes 294920 | tf_op jit(solution)/shard_map/ppermute | solution.py:426
  11.2 3.6 %collective-permute-start.5 = (bf16[128,384]{1,0:T(8,128)(2,1)S(1)}, bf16[128,384]{1,0:T(8,128)(2,1)S(1)}, u32[]{:S(2)}, u32[]{:S(2)}) collective-permute-start(bf16[128,384]{1,0:T(8,128)(2,1)S(1)} %get-tuple-element.46), channel_id=1, source_target_pairs={{0,6},{1,7},{2,4},{3,5},{4,2},{5,3},{6,0},{7,1},{8,14},{9,15},{10,... | collective-permute-start | bytes 294920 | tf_op jit(solution)/shard_map/ppermute | solution.py:426
  14.8 1.7 %shard_map.105.refs_0_ = bf16[8,128,384]{2,1,0:T(8,128)(2,1)S(1)} custom-call(s32[1]{0:T(128)} %bitcast.3.own.own_in, bf16[32,16,768]{2,1,0:T(8,128)(2,1)} %base.3), custom_call_target="tpu_custom_call" | custom-call | tf_op jit(solution)/shard_map/pallas_call | solution.py:65
  17.5 7.7 %collective-permute-done.4.rest_5_ = bf16[128,384]{1,0:T(8,128)(2,1)S(1)} collective-permute-done((bf16[128,384]{1,0:T(8,128)(2,1)S(1)}, bf16[128,384]{1,0:T(8,128)(2,1)S(1)}, u32[]{:S(2)}, u32[]{:S(2)}) %collective-permute-start.4) | collective-permute-done | bytes 98336 | tf_op jit(solution)/shard_map/ppermute | solution.py:426
  25.7 6.6 %all-to-all-start = ((bf16[8,128,384]{2,1,0:T(8,128)(2,1)}), bf16[8,128,384]{2,1,0:T(8,128)(2,1)S(1)}, u32[]{:S(2)}, u32[]{:S(2)}) async-start(bf16[8,128,384]{2,1,0:T(8,128)(2,1)} %shard_map.106), calls=%async_computation | async-start | bytes 1572864 | tf_op jit(solution)/shard_map/all_to_all | solution.py:421
  32.3 1.6 %collective-permute-start.8 = (bf16[128,384]{1,0:T(8,128)(2,1)S(1)}, bf16[128,384]{1,0:T(8,128)(2,1)S(1)}, u32[]{:S(2)}, u32[]{:S(2)}) collective-permute-start(bf16[128,384]{1,0:T(8,128)(2,1)S(1)} %get-tuple-element.50), channel_id=1, source_target_pairs={{0,16},{1,17},{2,18},{3,19},{4,20},{5,21},{6,22},{7,23},{8,24},{9,... | collective-permute-start | bytes 294920 | tf_op jit(solution)/shard_map/ppermute | solution.py:426
  34.2 3.8 %collective-permute-done.8.rest_2_ = bf16[128,384]{1,0:T(8,128)(2,1)S(1)} collective-permute-done((bf16[128,384]{1,0:T(8,128)(2,1)S(1)}, bf16[128,384]{1,0:T(8,128)(2,1)S(1)}, u32[]{:S(2)}, u32[]{:S(2)}) %collective-permute-start.8) | collective-permute-done | bytes 98336 | tf_op jit(solution)/shard_map/ppermute | solution.py:426
  39.2 3.7 %shard_map.104 = (bf16[128,384]{1,0:T(8,128)(2,1)S(1)}, bf16[128,384]{1,0:T(8,128)(2,1)S(1)}, bf16[128,384]{1,0:T(8,128)(2,1)S(1)}, bf16[128,384]{1,0:T(8,128)(2...) custom-call(s32[1]{0:T(128)} %bitcast.own_out.member.own_in, s32[1]{0:T(128)} %bitcast.1.first_mode, ...), custom_call_target="tpu_custom_call" | custom-call | tf_op jit(solution)/shard_map/pallas_call | solution.py:65
  43.5 1.5 %collective-permute-start.11 = (bf16[128,384]{1,0:T(8,128)(2,1)S(1)}, bf16[128,384]{1,0:T(8,128)(2,1)S(1)}, u32[]{:S(2)}, u32[]{:S(2)}) collective-permute-start(bf16[128,384]{1,0:T(8,128)(2,1)S(1)} %get-tuple-element.54), channel_id=1, source_target_pairs={{0,16},{1,17},{2,18},{3,19},{4,20},{5,21},{6,22},{7,23},{8,24},{9,... | collective-permute-start | bytes 294920 | tf_op jit(solution)/shard_map/ppermute | solution.py:426
  45.0 6.9 %all-to-all-done.rest_0_ = bf16[8,128,384]{2,1,0:T(8,128)(2,1)S(1)} async-done(((bf16[8,128,384]{2,1,0:T(8,128)(2,1)}), bf16[8,128,384]{2,1,0:T(8,128)(2,1)S(1)}, u32[]{:S(2)}, u32[]{:S(2)}) %all-to-all-start) | async-done | bytes 786464 | tf_op jit(solution)/shard_map/all_to_all | solution.py:421
  54.1 3.6 %all-to-all-start.1 = ((bf16[8,128,384]{2,1,0:T(8,128)(2,1)}), bf16[8,128,384]{2,1,0:T(8,128)(2,1)S(1)}, u32[]{:S(2)}, u32[]{:S(2)}) async-start(bf16[8,128,384]{2,1,0:T(8,128)(2,1)} %shard_map.108), calls=%async_computation.1 | async-start | bytes 1572864 | tf_op jit(solution)/shard_map/all_to_all | solution.py:421
  57.7 1.6 %collective-permute-start.14 = (bf16[128,384]{1,0:T(8,128)(2,1)S(1)}, bf16[128,384]{1,0:T(8,128)(2,1)S(1)}, u32[]{:S(2)}, u32[]{:S(2)}) collective-permute-start(bf16[128,384]{1,0:T(8,128)(2,1)S(1)} %get-tuple-element.59), channel_id=1, source_target_pairs={{0,16},{1,17},{2,18},{3,19},{4,20},{5,21},{6,22},{7,23},{8,24},{9,... | collective-permute-start | bytes 294920 | tf_op jit(solution)/shard_map/ppermute | solution.py:426
  59.6 3.8 %collective-permute-done.14.rest_2_ = bf16[128,384]{1,0:T(8,128)(2,1)S(1)} collective-permute-done((bf16[128,384]{1,0:T(8,128)(2,1)S(1)}, bf16[128,384]{1,0:T(8,128)(2,1)S(1)}, u32[]{:S(2)}, u32[]{:S(2)}) %collective-permute-start.14) | collective-permute-done | bytes 98336 | tf_op jit(solution)/shard_map/ppermute | solution.py:426
  64.6 4.1 %shard_map.110 = (bf16[8,128,192]{2,1,0:T(8,128)(2,1)S(1)}, bf16[192,192]{1,0:T(8,128)(2,1)S(1)}, bf16[96,96]{1,0:T(8,128)(2,1)S(1)}, bf16[96,96]{1,0:T(8,128)(2...) custom-call(s32[1]{0:T(128)} %bitcast.own_out.member.own_in, s32[1]{0:T(128)} %bitcast.1.first_mode, ...), custom_call_target="tpu_custom_call" | custom-call | tf_op jit(solution)/shard_map/pallas_call | solution.py:65
  69.3 1.5 %collective-permute-start.17 = (bf16[96,96]{1,0:T(8,128)(2,1)S(1)}, bf16[96,96]{1,0:T(8,128)(2,1)S(1)}, u32[]{:S(2)}, u32[]{:S(2)}) collective-permute-start(bf16[96,96]{1,0:T(8,128)(2,1)S(1)} %get-tuple-element.64), channel_id=1, source_target_pairs={{0,16},{8,24},{16,0},{24,8},{1,17},{9,25},{17,1},{25,9},{2,18},{10... | collective-permute-start | bytes 55304 | tf_op jit(solution)/shard_map/ppermute | solution.py:426
  70.8 2.3 %collective-permute-done.17.refs_2_ = bf16[96,96]{1,0:T(8,128)(2,1)S(1)} collective-permute-done((bf16[96,96]{1,0:T(8,128)(2,1)S(1)}, bf16[96,96]{1,0:T(8,128)(2,1)S(1)}, u32[]{:S(2)}, u32[]{:S(2)}) %collective-permute-start.17) | collective-permute-done | bytes 18464 | tf_op jit(solution)/shard_map/ppermute | solution.py:426
  74.3 1.6 %shard_map.113 = (bf16[128,384]{1,0:T(8,128)(2,1)S(1)}, bf16[128,384]{1,0:T(8,128)(2,1)S(1)}, bf16[128,384]{1,0:T(8,128)(2,1)S(1)}, bf16[128,384]{1,0:T(8,128)(2,1)S(1)}) custom-call(s32[1]{0:T(128)} %bitcast.own_out.member.own_in, bf16[256,256]{1,0:T(8,128)(2,1)S(1)} %copy-done.4, bf16[8,128,192]{2,1,0:T(8,128)(2,1)S(1)} %get-tuple-element.66.grad_pre, ...), custom_call_target="tpu_custom_call" | custom-call | tf_op jit(solution)/shard_map/pallas_call | solution.py:65
  77.8 1.9 %collective-permute-start.19 = (bf16[1,96,96]{2,1,0:T(8,128)(2,1)S(1)}, bf16[1,96,96]{2,1,0:T(8,128)(2,1)S(1)}, u32[]{:S(2)}, u32[]{:S(2)}) collective-permute-start(bf16[1,96,96]{2,1,0:T(8,128)(2,1)S(1)} %shard_map.111.first.rest_0_), channel_id=1, source_target_pairs={{0,2},{1,3},{2,0},{3,1},{4,6},{5,7},{6,4},{7,5},{8,10},{9,11},{10,... | collective-permute-start | bytes 55304 | tf_op jit(solution)/shard_map/ppermute | solution.py:568
  79.8 1.9 %collective-permute-done.19.second = bf16[1,96,96]{2,1,0:T(8,128)(2,1)S(1)} collective-permute-done((bf16[1,96,96]{2,1,0:T(8,128)(2,1)S(1)}, bf16[1,96,96]{2,1,0:T(8,128)(2,1)S(1)}, u32[]{:S(2)}, u32[]{:S(2)}) %collective-permute-start.19) | collective-permute-done | bytes 18464 | tf_op jit(solution)/shard_map/ppermute | solution.py:568
  81.7 2.9 %collective-permute-start.20 = (bf16[2,96,96]{2,1,0:T(8,128)(2,1)S(1)}, bf16[2,96,96]{2,1,0:T(8,128)(2,1)S(1)}, u32[]{:S(2)}, u32[]{:S(2)}) collective-permute-start(bf16[2,96,96]{2,1,0:T(8,128)(2,1)S(1)} %shard_map.112.first), channel_id=1, source_target_pairs={{0,4},{1,5},{2,6},{3,7},{4,0},{5,1},{6,2},{7,3},{8,12},{9,13},{10,... | collective-permute-start | bytes 110600 | tf_op jit(solution)/shard_map/ppermute | solution.py:568
  84.6 1.2 %shard_map.114.rest_0_ = bf16[8,128,384]{2,1,0:T(8,128)(2,1)} custom-call(s32[1]{0:T(128)} %bitcast.own_out.member.own_in, bf16[512,256]{1,0:T(8,128)(2,1)S(1)} %copy-done.6, bf16[128,384]{1,0:T(8,128)(2,1)S(1)} %get-tuple-element.68.rest_0_, bf16[128,384]{1,0:T(8,128)(2,1)S(1)} %collective-permute-done.21.rest_1_, ...), custom_call_target="tpu_custom_call" | custom-call | tf_op jit(solution)/shard_map/pallas_call | solution.py:65
  85.8 1.3 %collective-permute-done.20.second = bf16[2,96,96]{2,1,0:T(8,128)(2,1)S(1)} collective-permute-done((bf16[2,96,96]{2,1,0:T(8,128)(2,1)S(1)}, bf16[2,96,96]{2,1,0:T(8,128)(2,1)S(1)}, u32[]{:S(2)}, u32[]{:S(2)}) %collective-permute-start.20) | collective-permute-done | bytes 36896 | tf_op jit(solution)/shard_map/ppermute | solution.py:568
  87.2 6.2 %all-to-all-start.2 = ((bf16[8,128,384]{2,1,0:T(8,128)(2,1)}), bf16[8,128,384]{2,1,0:T(8,128)(2,1)S(1)}, u32[]{:S(2)}, u32[]{:S(2)}) async-start(bf16[8,128,384]{2,1,0:T(8,128)(2,1)} %get-tuple-element.72), calls=%async_computation.2 | async-start | bytes 1572864 | tf_op jit(solution)/shard_map/all_to_all | solution.py:421
  93.4 2.0 %collective-permute-start.24 = (bf16[4,96,96]{2,1,0:T(8,128)(2,1)S(1)}, bf16[4,96,96]{2,1,0:T(8,128)(2,1)S(1)}, u32[]{:S(2)}, u32[]{:S(2)}) collective-permute-start(bf16[4,96,96]{2,1,0:T(8,128)(2,1)S(1)} %get-tuple-element.73.near), channel_id=1, source_target_pairs={{0,1},{1,0},{2,3},{3,2},{4,5},{5,4},{6,7},{7,6},{8,9},{9,8},{10,11... | collective-permute-start | bytes 221192 | tf_op jit(solution)/shard_map/ppermute | solution.py:577
  96.5 5.6 %collective-permute-done.24.other = bf16[4,96,96]{2,1,0:T(8,128)(2,1)S(1)} collective-permute-done((bf16[4,96,96]{2,1,0:T(8,128)(2,1)S(1)}, bf16[4,96,96]{2,1,0:T(8,128)(2,1)S(1)}, u32[]{:S(2)}, u32[]{:S(2)}) %collective-permute-start.24) | collective-permute-done | bytes 73760 | tf_op jit(solution)/shard_map/ppermute | solution.py:577
  104.1 5.0 %collective-permute-done.26.rest_2_ = bf16[8,96,96]{2,1,0:T(8,128)(2,1)S(1)} collective-permute-done((bf16[8,96,96]{2,1,0:T(8,128)(2,1)S(1)}, bf16[8,96,96]{2,1,0:T(8,128)(2,1)S(1)}, u32[]{:S(2)}, u32[]{:S(2)}) %collective-permute-start.26) | collective-permute-done | bytes 147488 | tf_op jit(solution)/shard_map/ppermute | solution.py:585
  109.0 3.1 %all-to-all-done.2.packed = bf16[8,128,384]{2,1,0:T(8,128)(2,1)S(1)} async-done(((bf16[8,128,384]{2,1,0:T(8,128)(2,1)}), bf16[8,128,384]{2,1,0:T(8,128)(2,1)S(1)}, u32[]{:S(2)}, u32[]{:S(2)}) %all-to-all-start.2) | async-done | bytes 786464 | tf_op jit(solution)/shard_map/all_to_all | solution.py:421
  113.3 1.3 %shard_map.118 = (f32[2,8,96,96]{3,2,1,0:T(8,128)}, f32[2,8,96,96]{3,2,1,0:T(8,128)}) custom-call(s32[1]{0:T(128)} %bitcast.4.lat_own, bf16[8,96,96]{2,1,0:T(8,128)(2,1)S(1)} %shard_map.117.rest_0_, bf16[8,96,96]{2,1,0:T(8,128)(2,1)S(1)} %collective-permute-done.25.rest_1_, bf16[8,96,96]{2,1,0:T(8,128)(2,1)S(1)} %collective-permute-done.26.rest_2_, ...), custom_call_target="tpu_custom_call" | custom-call | tf_op jit(solution)/shard_map/pallas_call | solution.py:65
  (61 shorter events, 15.3 us)
Async XLA Ops:
  2.3 8.9 %collective-permute-start = (bf16[128,384]{1,0:T(8,128)(2,1)S(1)}, bf16[128,384]{1,0:T(8,128)(2,1)S(1)}, u32[]{:S(2)}, u32[]{:S(2)}) collective-permute-start(bf16[128,384]{1,0:T(8,128)(2,1)S(1)} %get-tuple-element.41), channel_id=1, source_target_pairs={{0,1},{1,0},{2,3},{3,2},{4,5},{5,4},{6,7},{7,6},{8,9},{9,8},{10,11... | collective-permute-start | bytes 294920 | tf_op jit(solution)/shard_map/ppermute | solution.py:426
  5.4 9.5 %collective-permute-start.1 = (bf16[128,384]{1,0:T(8,128)(2,1)S(1)}, bf16[128,384]{1,0:T(8,128)(2,1)S(1)}, u32[]{:S(2)}, u32[]{:S(2)}) collective-permute-start(bf16[128,384]{1,0:T(8,128)(2,1)S(1)} %get-tuple-element.42), channel_id=1, source_target_pairs={{0,2},{1,3},{2,0},{3,1},{4,6},{5,7},{6,4},{7,5},{8,10},{9,11},{10,... | collective-permute-start | bytes 294920 | tf_op jit(solution)/shard_map/ppermute | solution.py:426
  7.0 10.5 %collective-permute-start.2 = (bf16[128,384]{1,0:T(8,128)(2,1)S(1)}, bf16[128,384]{1,0:T(8,128)(2,1)S(1)}, u32[]{:S(2)}, u32[]{:S(2)}) collective-permute-start(bf16[128,384]{1,0:T(8,128)(2,1)S(1)} %get-tuple-element.43), channel_id=1, source_target_pairs={{0,3},{1,2},{2,1},{3,0},{4,7},{5,6},{6,5},{7,4},{8,11},{9,10},{10,... | collective-permute-start | bytes 294920 | tf_op jit(solution)/shard_map/ppermute | solution.py:426
  7.0 10.5 %collective-permute-start.3 = (bf16[128,384]{1,0:T(8,128)(2,1)S(1)}, bf16[128,384]{1,0:T(8,128)(2,1)S(1)}, u32[]{:S(2)}, u32[]{:S(2)}) collective-permute-start(bf16[128,384]{1,0:T(8,128)(2,1)S(1)} %get-tuple-element.44), channel_id=1, source_target_pairs={{0,4},{1,5},{2,6},{3,7},{4,0},{5,1},{6,2},{7,3},{8,12},{9,13},{10,... | collective-permute-start | bytes 294920 | tf_op jit(solution)/shard_map/ppermute | solution.py:426
  9.9 15.2 %collective-permute-start.4 = (bf16[128,384]{1,0:T(8,128)(2,1)S(1)}, bf16[128,384]{1,0:T(8,128)(2,1)S(1)}, u32[]{:S(2)}, u32[]{:S(2)}) collective-permute-start(bf16[128,384]{1,0:T(8,128)(2,1)S(1)} %get-tuple-element.45), channel_id=1, source_target_pairs={{0,5},{1,4},{2,7},{3,6},{4,1},{5,0},{6,3},{7,2},{8,13},{9,12},{10,... | collective-permute-start | bytes 294920 | tf_op jit(solution)/shard_map/ppermute | solution.py:426
  11.2 13.9 %collective-permute-start.5 = (bf16[128,384]{1,0:T(8,128)(2,1)S(1)}, bf16[128,384]{1,0:T(8,128)(2,1)S(1)}, u32[]{:S(2)}, u32[]{:S(2)}) collective-permute-start(bf16[128,384]{1,0:T(8,128)(2,1)S(1)} %get-tuple-element.46), channel_id=1, source_target_pairs={{0,6},{1,7},{2,4},{3,5},{4,2},{5,3},{6,0},{7,1},{8,14},{9,15},{10,... | collective-permute-start | bytes 294920 | tf_op jit(solution)/shard_map/ppermute | solution.py:426
  14.8 10.3 %collective-permute-start.6 = (bf16[128,384]{1,0:T(8,128)(2,1)S(1)}, bf16[128,384]{1,0:T(8,128)(2,1)S(1)}, u32[]{:S(2)}, u32[]{:S(2)}) collective-permute-start(bf16[128,384]{1,0:T(8,128)(2,1)S(1)} %get-tuple-element.47), channel_id=1, source_target_pairs={{0,7},{1,6},{2,5},{3,4},{4,3},{5,2},{6,1},{7,0},{8,15},{9,14},{10,... | collective-permute-start | bytes 294920 | tf_op jit(solution)/shard_map/ppermute | solution.py:426
  25.7 26.2 %all-to-all-start = ((bf16[8,128,384]{2,1,0:T(8,128)(2,1)}), bf16[8,128,384]{2,1,0:T(8,128)(2,1)S(1)}, u32[]{:S(2)}, u32[]{:S(2)}) async-start(bf16[8,128,384]{2,1,0:T(8,128)(2,1)} %shard_map.106), calls=%async_computation | async-start | bytes 1572864 | tf_op jit(solution)/shard_map/all_to_all | solution.py:421
  32.3 1.9 %collective-permute-start.7 = (bf16[128,384]{1,0:T(8,128)(2,1)S(1)}, bf16[128,384]{1,0:T(8,128)(2,1)S(1)}, u32[]{:S(2)}, u32[]{:S(2)}) collective-permute-start(bf16[128,384]{1,0:T(8,128)(2,1)S(1)} %get-tuple-element.49), channel_id=1, source_target_pairs={{0,8},{1,9},{2,10},{3,11},{4,12},{5,13},{6,14},{7,15},{8,0},{9,1},... | collective-permute-start | bytes 294920 | tf_op jit(solution)/shard_map/ppermute | solution.py:426
  32.3 5.7 %collective-permute-start.8 = (bf16[128,384]{1,0:T(8,128)(2,1)S(1)}, bf16[128,384]{1,0:T(8,128)(2,1)S(1)}, u32[]{:S(2)}, u32[]{:S(2)}) collective-permute-start(bf16[128,384]{1,0:T(8,128)(2,1)S(1)} %get-tuple-element.50), channel_id=1, source_target_pairs={{0,16},{1,17},{2,18},{3,19},{4,20},{5,21},{6,22},{7,23},{8,24},{9,... | collective-permute-start | bytes 294920 | tf_op jit(solution)/shard_map/ppermute | solution.py:426
  33.9 5.3 %collective-permute-start.9 = (bf16[128,384]{1,0:T(8,128)(2,1)S(1)}, bf16[128,384]{1,0:T(8,128)(2,1)S(1)}, u32[]{:S(2)}, u32[]{:S(2)}) collective-permute-start(bf16[128,384]{1,0:T(8,128)(2,1)S(1)} %get-tuple-element.51), channel_id=1, source_target_pairs={{0,24},{1,25},{2,26},{3,27},{4,28},{5,29},{6,30},{7,31},{8,16},{9,... | collective-permute-start | bytes 294920 | tf_op jit(solution)/shard_map/ppermute | solution.py:426
  42.9 9.5 %collective-permute-start.10 = (bf16[128,384]{1,0:T(8,128)(2,1)S(1)}, bf16[128,384]{1,0:T(8,128)(2,1)S(1)}, u32[]{:S(2)}, u32[]{:S(2)}) collective-permute-start(bf16[128,384]{1,0:T(8,128)(2,1)S(1)} %get-tuple-element.53), channel_id=1, source_target_pairs={{0,8},{1,9},{2,10},{3,11},{4,12},{5,13},{6,14},{7,15},{8,0},{9,1},... | collective-permute-start | bytes 294920 | tf_op jit(solution)/shard_map/ppermute | solution.py:426
  43.5 8.9 %collective-permute-start.11 = (bf16[128,384]{1,0:T(8,128)(2,1)S(1)}, bf16[128,384]{1,0:T(8,128)(2,1)S(1)}, u32[]{:S(2)}, u32[]{:S(2)}) collective-permute-start(bf16[128,384]{1,0:T(8,128)(2,1)S(1)} %get-tuple-element.54), channel_id=1, source_target_pairs={{0,16},{1,17},{2,18},{3,19},{4,20},{5,21},{6,22},{7,23},{8,24},{9,... | collective-permute-start | bytes 294920 | tf_op jit(solution)/shard_map/ppermute | solution.py:426
  45.0 7.4 %collective-permute-start.12 = (bf16[128,384]{1,0:T(8,128)(2,1)S(1)}, bf16[128,384]{1,0:T(8,128)(2,1)S(1)}, u32[]{:S(2)}, u32[]{:S(2)}) collective-permute-start(bf16[128,384]{1,0:T(8,128)(2,1)S(1)} %get-tuple-element.55), channel_id=1, source_target_pairs={{0,24},{1,25},{2,26},{3,27},{4,28},{5,29},{6,30},{7,31},{8,16},{9,... | collective-permute-start | bytes 294920 | tf_op jit(solution)/shard_map/ppermute | solution.py:426
  54.1 33.1 %all-to-all-start.1 = ((bf16[8,128,384]{2,1,0:T(8,128)(2,1)}), bf16[8,128,384]{2,1,0:T(8,128)(2,1)S(1)}, u32[]{:S(2)}, u32[]{:S(2)}) async-start(bf16[8,128,384]{2,1,0:T(8,128)(2,1)} %shard_map.108), calls=%async_computation.1 | async-start | bytes 1572864 | tf_op jit(solution)/shard_map/all_to_all | solution.py:421
  57.7 1.9 %collective-permute-start.13 = (bf16[128,384]{1,0:T(8,128)(2,1)S(1)}, bf16[128,384]{1,0:T(8,128)(2,1)S(1)}, u32[]{:S(2)}, u32[]{:S(2)}) collective-permute-start(bf16[128,384]{1,0:T(8,128)(2,1)S(1)} %get-tuple-element.58), channel_id=1, source_target_pairs={{0,8},{1,9},{2,10},{3,11},{4,12},{5,13},{6,14},{7,15},{8,0},{9,1},... | collective-permute-start | bytes 294920 | tf_op jit(solution)/shard_map/ppermute | solution.py:426
  57.7 5.7 %collective-permute-start.14 = (bf16[128,384]{1,0:T(8,128)(2,1)S(1)}, bf16[128,384]{1,0:T(8,128)(2,1)S(1)}, u32[]{:S(2)}, u32[]{:S(2)}) collective-permute-start(bf16[128,384]{1,0:T(8,128)(2,1)S(1)} %get-tuple-element.59), channel_id=1, source_target_pairs={{0,16},{1,17},{2,18},{3,19},{4,20},{5,21},{6,22},{7,23},{8,24},{9,... | collective-permute-start | bytes 294920 | tf_op jit(solution)/shard_map/ppermute | solution.py:426
  59.3 5.3 %collective-permute-start.15 = (bf16[128,384]{1,0:T(8,128)(2,1)S(1)}, bf16[128,384]{1,0:T(8,128)(2,1)S(1)}, u32[]{:S(2)}, u32[]{:S(2)}) collective-permute-start(bf16[128,384]{1,0:T(8,128)(2,1)S(1)} %get-tuple-element.60), channel_id=1, source_target_pairs={{0,24},{1,25},{2,26},{3,27},{4,28},{5,29},{6,30},{7,31},{8,16},{9,... | collective-permute-start | bytes 294920 | tf_op jit(solution)/shard_map/ppermute | solution.py:426
  68.7 2.1 %collective-permute-start.16 = (bf16[96,96]{1,0:T(8,128)(2,1)S(1)}, bf16[96,96]{1,0:T(8,128)(2,1)S(1)}, u32[]{:S(2)}, u32[]{:S(2)}) collective-permute-start(bf16[96,96]{1,0:T(8,128)(2,1)S(1)} %get-tuple-element.63), channel_id=1, source_target_pairs={{0,8},{8,0},{16,24},{24,16},{1,9},{9,1},{17,25},{25,17},{2,10},{10... | collective-permute-start | bytes 55304 | tf_op jit(solution)/shard_map/ppermute | solution.py:426
  69.3 3.8 %collective-permute-start.17 = (bf16[96,96]{1,0:T(8,128)(2,1)S(1)}, bf16[96,96]{1,0:T(8,128)(2,1)S(1)}, u32[]{:S(2)}, u32[]{:S(2)}) collective-permute-start(bf16[96,96]{1,0:T(8,128)(2,1)S(1)} %get-tuple-element.64), channel_id=1, source_target_pairs={{0,16},{8,24},{16,0},{24,8},{1,17},{9,25},{17,1},{25,9},{2,18},{10... | collective-permute-start | bytes 55304 | tf_op jit(solution)/shard_map/ppermute | solution.py:426
  70.8 3.5 %collective-permute-start.18 = (bf16[96,96]{1,0:T(8,128)(2,1)S(1)}, bf16[96,96]{1,0:T(8,128)(2,1)S(1)}, u32[]{:S(2)}, u32[]{:S(2)}) collective-permute-start(bf16[96,96]{1,0:T(8,128)(2,1)S(1)} %get-tuple-element.65), channel_id=1, source_target_pairs={{0,24},{8,16},{16,8},{24,0},{1,25},{9,17},{17,9},{25,1},{2,26},{10... | collective-permute-start | bytes 55304 | tf_op jit(solution)/shard_map/ppermute | solution.py:426
  75.9 8.7 %collective-permute-start.21 = (bf16[128,384]{1,0:T(8,128)(2,1)S(1)}, bf16[128,384]{1,0:T(8,128)(2,1)S(1)}, u32[]{:S(2)}, u32[]{:S(2)}) collective-permute-start(bf16[128,384]{1,0:T(8,128)(2,1)S(1)} %get-tuple-element.69), channel_id=1, source_target_pairs={{0,8},{1,9},{2,10},{3,11},{4,12},{5,13},{6,14},{7,15},{8,0},{9,1},... | collective-permute-start | bytes 294920 | tf_op jit(solution)/shard_map/ppermute | solution.py:426
  76.1 8.5 %collective-permute-start.22 = (bf16[128,384]{1,0:T(8,128)(2,1)S(1)}, bf16[128,384]{1,0:T(8,128)(2,1)S(1)}, u32[]{:S(2)}, u32[]{:S(2)}) collective-permute-start(bf16[128,384]{1,0:T(8,128)(2,1)S(1)} %get-tuple-element.70), channel_id=1, source_target_pairs={{0,16},{1,17},{2,18},{3,19},{4,20},{5,21},{6,22},{7,23},{8,24},{9,... | collective-permute-start | bytes 294920 | tf_op jit(solution)/shard_map/ppermute | solution.py:426
  76.9 7.7 %collective-permute-start.23 = (bf16[128,384]{1,0:T(8,128)(2,1)S(1)}, bf16[128,384]{1,0:T(8,128)(2,1)S(1)}, u32[]{:S(2)}, u32[]{:S(2)}) collective-permute-start(bf16[128,384]{1,0:T(8,128)(2,1)S(1)} %get-tuple-element.71), channel_id=1, source_target_pairs={{0,24},{1,25},{2,26},{3,27},{4,28},{5,29},{6,30},{7,31},{8,16},{9,... | collective-permute-start | bytes 294920 | tf_op jit(solution)/shard_map/ppermute | solution.py:426
  77.8 3.8 %collective-permute-start.19 = (bf16[1,96,96]{2,1,0:T(8,128)(2,1)S(1)}, bf16[1,96,96]{2,1,0:T(8,128)(2,1)S(1)}, u32[]{:S(2)}, u32[]{:S(2)}) collective-permute-start(bf16[1,96,96]{2,1,0:T(8,128)(2,1)S(1)} %shard_map.111.first.rest_0_), channel_id=1, source_target_pairs={{0,2},{1,3},{2,0},{3,1},{4,6},{5,7},{6,4},{7,5},{8,10},{9,11},{10,... | collective-permute-start | bytes 55304 | tf_op jit(solution)/shard_map/ppermute | solution.py:568
  81.7 5.5 %collective-permute-start.20 = (bf16[2,96,96]{2,1,0:T(8,128)(2,1)S(1)}, bf16[2,96,96]{2,1,0:T(8,128)(2,1)S(1)}, u32[]{:S(2)}, u32[]{:S(2)}) collective-permute-start(bf16[2,96,96]{2,1,0:T(8,128)(2,1)S(1)} %shard_map.112.first), channel_id=1, source_target_pairs={{0,4},{1,5},{2,6},{3,7},{4,0},{5,1},{6,2},{7,3},{8,12},{9,13},{10,... | collective-permute-start | bytes 110600 | tf_op jit(solution)/shard_map/ppermute | solution.py:568
  87.2 24.9 %all-to-all-start.2 = ((bf16[8,128,384]{2,1,0:T(8,128)(2,1)}), bf16[8,128,384]{2,1,0:T(8,128)(2,1)S(1)}, u32[]{:S(2)}, u32[]{:S(2)}) async-start(bf16[8,128,384]{2,1,0:T(8,128)(2,1)} %get-tuple-element.72), calls=%async_computation.2 | async-start | bytes 1572864 | tf_op jit(solution)/shard_map/all_to_all | solution.py:421
  93.4 8.7 %collective-permute-start.24 = (bf16[4,96,96]{2,1,0:T(8,128)(2,1)S(1)}, bf16[4,96,96]{2,1,0:T(8,128)(2,1)S(1)}, u32[]{:S(2)}, u32[]{:S(2)}) collective-permute-start(bf16[4,96,96]{2,1,0:T(8,128)(2,1)S(1)} %get-tuple-element.73.near), channel_id=1, source_target_pairs={{0,1},{1,0},{2,3},{3,2},{4,5},{5,4},{6,7},{7,6},{8,9},{9,8},{10,11... | collective-permute-start | bytes 221192 | tf_op jit(solution)/shard_map/ppermute | solution.py:577
  96.5 15.6 %copy-start.1 = (bf16[32,16,768]{2,1,0:T(8,128)(2,1)S(1)}, bf16[32,16,768]{2,1,0:T(8,128)(2,1)}, u32[]{:S(2)}) copy-start(bf16[32,16,768]{2,1,0:T(8,128)(2,1)} %base.3) | copy-start | bytes 2359300
  103.3 5.7 %collective-permute-start.26 = (bf16[8,96,96]{2,1,0:T(8,128)(2,1)S(1)}, bf16[8,96,96]{2,1,0:T(8,128)(2,1)S(1)}, u32[]{:S(2)}, u32[]{:S(2)}) collective-permute-start(bf16[8,96,96]{2,1,0:T(8,128)(2,1)S(1)} %shard_map.117.rest_0_), channel_id=1, source_target_pairs={{0,16},{8,24},{16,0},{24,8},{1,17},{9,25},{17,1},{25,9},{2,18},{10... | collective-permute-start | bytes 442376 | tf_op jit(solution)/shard_map/ppermute | solution.py:585
  104.0 9.2 %collective-permute-start.25 = (bf16[8,96,96]{2,1,0:T(8,128)(2,1)S(1)}, bf16[8,96,96]{2,1,0:T(8,128)(2,1)S(1)}, u32[]{:S(2)}, u32[]{:S(2)}) collective-permute-start(bf16[8,96,96]{2,1,0:T(8,128)(2,1)S(1)} %shard_map.117.rest_0_), channel_id=1, source_target_pairs={{0,8},{8,0},{16,24},{24,16},{1,9},{9,1},{17,25},{25,17},{2,10},{10... | collective-permute-start | bytes 442376 | tf_op jit(solution)/shard_map/ppermute | solution.py:585
  109.0 4.2 %collective-permute-start.27 = (bf16[8,96,96]{2,1,0:T(8,128)(2,1)S(1)}, bf16[8,96,96]{2,1,0:T(8,128)(2,1)S(1)}, u32[]{:S(2)}, u32[]{:S(2)}) collective-permute-start(bf16[8,96,96]{2,1,0:T(8,128)(2,1)S(1)} %collective-permute-done.26.rest_2_), channel_id=1, source_target_pairs={{0,8},{8,0},{16,24},{24,16},{1,9},{9,1},{17,25},{25,17},{2,10},{10... | collective-permute-start | bytes 442376 | tf_op jit(solution)/shard_map/ppermute | solution.py:585
  (6 other events, 34.9 us)

commit v6 on v5

--- a/solution.py
+++ b/solution.py
@@ -127,8 +127,7 @@
     deal(sent, slots, own[0])
 
 
-def unpack_body(rows_sub, subs, extra, packed, base, *rest):
-    result, mixed, sems = rest[extra:]
+def unpack_body(rows_sub, subs, packed, base, result, mixed, sems):
     cols = base.shape[1]
     saves = group_copies(mixed, result, sems)
     for group in range(RQ):
@@ -401,8 +400,23 @@
         blocks[jnp.bitwise_xor(own[0], 2 * slot + 1)] = other[slot]
 
 
-def assemble_body(lat_count, subs, lat_own, *rest):
-    gathered, (first, second, slots) = rest[:lat_count], rest[lat_count:]
+def last_body(lat_count, rows_sub, subs, lat_own, packed, base, *rest):
+    gathered, (result, first, second, mixed, sems, slots, grad_sems) = (
+        rest[:lat_count],
+        rest[lat_count:],
+    )
+    assemble(lat_own, gathered, slots, subs)
+    copies = [
+        pltpu.make_async_copy(slots.at[pl.ds(2 * at, 2)], full, grad_sems.at[at])
+        for at, full in enumerate((first, second))
+    ]
+    for copy in copies:
+        copy.start()
+    unpack_body(rows_sub, subs, packed, base, result, mixed, sems)
+    finish(copies)
+
+
+def assemble(lat_own, gathered, slots, subs):
     rows = gathered[0].shape[1]
     for offset, pieces in enumerate(gathered):
         start = jnp.bitwise_xor(lat_own[0], offset) * rows
@@ -413,8 +427,6 @@
                 value = pieces[sub * NB + block].astype(jnp.float32)
                 total = value if total is None else total + value
             slots[matrix, block, pl.ds(row, rows)] = total
-    first[...] = slots[:2]
-    second[...] = slots[2:]
 
 
 def exchange(source):
@@ -481,10 +493,8 @@
         scratch = [lon_slots, pltpu.VMEM(source.shape, bf16), pltpu.SemaphoreType.DMA((RQ,))]
         return kernel_call(body, sent, [lon_index], [], scratch, far=[source])
 
-    def unpack(source, base, anchors=()):
-        body = functools.partial(unpack_body, rows_sub, subs, len(anchors))
-        scratch = [pltpu.VMEM(base.shape, bf16), pltpu.SemaphoreType.DMA((RQ,))]
-        return kernel_call(body, [pltpu.HBM(base.shape, bf16)], [], [source, base], scratch, anchors)[0]
+    unpack_scratch = [pltpu.VMEM(features.shape, bf16), pltpu.SemaphoreType.DMA((RQ,))]
+    unpacked = pltpu.HBM(features.shape, bf16)
 
     def to_spectra(pieces, anchors=()):
         return kernel_call(
@@ -569,7 +579,13 @@
         near, columns = join_gate(near, moved, columns, step == lon_count // 2)
         step *= 2
     returned = exchange(columns)
-    mixed_field = unpack(filtered, features)
+    mixed_field = kernel_call(
+        functools.partial(unpack_body, rows_sub, subs),
+        [unpacked],
+        [],
+        [filtered, features],
+        unpack_scratch,
+    )[0]
     blocks = kernel_call(
         blocks_body,
         [array((lon_count, share, BS), bf16)],
@@ -586,15 +602,18 @@
             gathered[offset | step] = moved
         step //= 2
     gathered = [gathered[offset] for offset in range(lat_count)]
-    full = array((2, NB, BS, BS), f32)
-    grad_first, grad_second = kernel_call(
-        functools.partial(assemble_body, lat_count, subs),
-        [full, full],
+    full = pltpu.HBM((2, NB, BS, BS), f32)
+    feature_grad, grad_first, grad_second = kernel_call(
+        functools.partial(last_body, lat_count, rows_sub, subs),
+        [unpacked, full, full],
         [lat_index],
-        gathered,
-        [pltpu.VMEM((4, NB, BS, BS), f32)],
-    )
-    feature_grad = unpack(returned, cotangent)
+        [returned, cotangent, *gathered],
+        [
+            *unpack_scratch,
+            pltpu.VMEM((4, NB, BS, BS), f32),
+            pltpu.SemaphoreType.DMA((2,)),
+        ],
+    )
     return (mixed_field, feature_grad, grad_first, grad_second)
 
 

time: 115 us -> 114 us (level)
    pallas_call x14 -> x13, Pallas kernels: 19.8 us -> 19.1 us  [kernel_call(): pl.pallas_call(body, out_shape=out_shape, in_specs=in_specs, out_specs=[s...]
  transfers between devices with their start and end apart: 31 -> 31, of which waited for: 13 -> 13; matrix products, arithmetic and copies ran while one was open for 0% -> 0% of each run, Pallas kernels for 13% -> 12%
where the time goes in v6:
time: 114 us
  starting transfers between devices  46.4 us (41%)
  waiting for transfers between devices  44.9 us (39%)
  Pallas kernels  19.1 us (17%)
  local copies, waits for them, and re-layouts  2.47 us (2%)
    ppermute x22, starting transfers between devices, swap(): lax.ppermute(piece, axes, partners(offset))  22.5 us
    ppermute x22, waiting for transfers between devices, swap(): lax.ppermute(piece, axes, partners(offset))  21.2 us
    pallas_call x13, Pallas kernels, kernel_call(): pl.pallas_call(body, out_shape=out_shape, in_specs=in_specs, out_specs=[s...  19.1 us
    all_to_all x3, starting transfers between devices, exchange(): lax.all_to_all(source, 'lon', split_axis=0, concat_axis=0, tiled=True)  16.3 us
    all_to_all x3, waiting for transfers between devices, exchange(): lax.all_to_all(source, 'lon', split_axis=0, concat_axis=0, tiled=True)  10 us
    ppermute x1, waiting for transfers between devices, shards(): lax.ppermute(near, 'lon', lon_pairs(1))  5.59 us
    ppermute x3, waiting for transfers between devices, shards(): moved = lax.ppermute(gathered[offset], 'lat', line_pairs(lat_count)(step))  4.96 us
    ppermute x2, starting transfers between devices, shards(): moved = lax.ppermute(near, 'lon', lon_pairs(step))  4.82 us
  transfers between devices with their start and end apart: 31, of which 13 were waited for; matrix products, arithmetic and copies ran while one was open for 0% of the time, Pallas kernels for 12%

profile of v6, /device:TPU:0, one launch (start us, length us, event | category | flops | bytes accessed | tf_op | source)
XLA Modules:
  0.0 113.8 jit_solution(17604953712406104247)
XLA Ops:
  0.6 1.7 %shard_map.102 = (bf16[128,384]{1,0:T(8,128)(2,1)S(1)}, bf16[128,384]{1,0:T(8,128)(2,1)S(1)}, bf16[128,384]{1,0:T(8,128)(2,1)S(1)}, bf16[128,384]{1,0:T(8,128)(2...) custom-call(s32[1]{0:T(128)} %bitcast.3.own.own_in, ...), custom_call_target="tpu_custom_call" | custom-call | tf_op jit(solution)/shard_map/pallas_call | solution.py:65
  2.3 3.0 %collective-permute-start = (bf16[128,384]{1,0:T(8,128)(2,1)S(1)}, bf16[128,384]{1,0:T(8,128)(2,1)S(1)}, u32[]{:S(2)}, u32[]{:S(2)}) collective-permute-start(bf16[128,384]{1,0:T(8,128)(2,1)S(1)} %get-tuple-element.42), channel_id=1, source_target_pairs={{0,1},{1,0},{2,3},{3,2},{4,5},{5,4},{6,7},{7,6},{8,9},{9,8},{10,11... | collective-permute-start | bytes 294920 | tf_op jit(solution)/shard_map/ppermute | solution.py:438
  5.4 1.6 %collective-permute-start.1 = (bf16[128,384]{1,0:T(8,128)(2,1)S(1)}, bf16[128,384]{1,0:T(8,128)(2,1)S(1)}, u32[]{:S(2)}, u32[]{:S(2)}) collective-permute-start(bf16[128,384]{1,0:T(8,128)(2,1)S(1)} %get-tuple-element.43), channel_id=1, source_target_pairs={{0,2},{1,3},{2,0},{3,1},{4,6},{5,7},{6,4},{7,5},{8,10},{9,11},{10,... | collective-permute-start | bytes 294920 | tf_op jit(solution)/shard_map/ppermute | solution.py:438
  7.0 3.0 %collective-permute-start.3 = (bf16[128,384]{1,0:T(8,128)(2,1)S(1)}, bf16[128,384]{1,0:T(8,128)(2,1)S(1)}, u32[]{:S(2)}, u32[]{:S(2)}) collective-permute-start(bf16[128,384]{1,0:T(8,128)(2,1)S(1)} %get-tuple-element.45), channel_id=1, source_target_pairs={{0,4},{1,5},{2,6},{3,7},{4,0},{5,1},{6,2},{7,3},{8,12},{9,13},{10,... | collective-permute-start | bytes 294920 | tf_op jit(solution)/shard_map/ppermute | solution.py:438
  9.9 1.3 %collective-permute-start.4 = (bf16[128,384]{1,0:T(8,128)(2,1)S(1)}, bf16[128,384]{1,0:T(8,128)(2,1)S(1)}, u32[]{:S(2)}, u32[]{:S(2)}) collective-permute-start(bf16[128,384]{1,0:T(8,128)(2,1)S(1)} %get-tuple-element.46), channel_id=1, source_target_pairs={{0,5},{1,4},{2,7},{3,6},{4,1},{5,0},{6,3},{7,2},{8,13},{9,12},{10,... | collective-permute-start | bytes 294920 | tf_op jit(solution)/shard_map/ppermute | solution.py:438
  11.2 3.6 %collective-permute-start.5 = (bf16[128,384]{1,0:T(8,128)(2,1)S(1)}, bf16[128,384]{1,0:T(8,128)(2,1)S(1)}, u32[]{:S(2)}, u32[]{:S(2)}) collective-permute-start(bf16[128,384]{1,0:T(8,128)(2,1)S(1)} %get-tuple-element.47), channel_id=1, source_target_pairs={{0,6},{1,7},{2,4},{3,5},{4,2},{5,3},{6,0},{7,1},{8,14},{9,15},{10,... | collective-permute-start | bytes 294920 | tf_op jit(solution)/shard_map/ppermute | solution.py:438
  14.8 1.7 %shard_map.105.refs_0_ = bf16[8,128,384]{2,1,0:T(8,128)(2,1)S(1)} custom-call(s32[1]{0:T(128)} %bitcast.3.own.own_in, bf16[32,16,768]{2,1,0:T(8,128)(2,1)} %base.3), custom_call_target="tpu_custom_call" | custom-call | tf_op jit(solution)/shard_map/pallas_call | solution.py:65
  17.5 7.7 %collective-permute-done.4.rest_5_ = bf16[128,384]{1,0:T(8,128)(2,1)S(1)} collective-permute-done((bf16[128,384]{1,0:T(8,128)(2,1)S(1)}, bf16[128,384]{1,0:T(8,128)(2,1)S(1)}, u32[]{:S(2)}, u32[]{:S(2)}) %collective-permute-start.4) | collective-permute-done | bytes 98336 | tf_op jit(solution)/shard_map/ppermute | solution.py:438
  25.7 6.6 %all-to-all-start = ((bf16[8,128,384]{2,1,0:T(8,128)(2,1)}), bf16[8,128,384]{2,1,0:T(8,128)(2,1)S(1)}, u32[]{:S(2)}, u32[]{:S(2)}) async-start(bf16[8,128,384]{2,1,0:T(8,128)(2,1)} %shard_map.106), calls=%async_computation | async-start | bytes 1572864 | tf_op jit(solution)/shard_map/all_to_all | solution.py:433
  32.3 1.6 %collective-permute-start.8 = (bf16[128,384]{1,0:T(8,128)(2,1)S(1)}, bf16[128,384]{1,0:T(8,128)(2,1)S(1)}, u32[]{:S(2)}, u32[]{:S(2)}) collective-permute-start(bf16[128,384]{1,0:T(8,128)(2,1)S(1)} %get-tuple-element.51), channel_id=1, source_target_pairs={{0,16},{1,17},{2,18},{3,19},{4,20},{5,21},{6,22},{7,23},{8,24},{9,... | collective-permute-start | bytes 294920 | tf_op jit(solution)/shard_map/ppermute | solution.py:438
  34.2 3.8 %collective-permute-done.8.rest_2_ = bf16[128,384]{1,0:T(8,128)(2,1)S(1)} collective-permute-done((bf16[128,384]{1,0:T(8,128)(2,1)S(1)}, bf16[128,384]{1,0:T(8,128)(2,1)S(1)}, u32[]{:S(2)}, u32[]{:S(2)}) %collective-permute-start.8) | collective-permute-done | bytes 98336 | tf_op jit(solution)/shard_map/ppermute | solution.py:438
  39.2 3.7 %shard_map.104 = (bf16[128,384]{1,0:T(8,128)(2,1)S(1)}, bf16[128,384]{1,0:T(8,128)(2,1)S(1)}, bf16[128,384]{1,0:T(8,128)(2,1)S(1)}, bf16[128,384]{1,0:T(8,128)(2...) custom-call(s32[1]{0:T(128)} %bitcast.own_out.member.own_in, s32[1]{0:T(128)} %bitcast.1.first_mode, ...), custom_call_target="tpu_custom_call" | custom-call | tf_op jit(solution)/shard_map/pallas_call | solution.py:65
  43.5 1.5 %collective-permute-start.11 = (bf16[128,384]{1,0:T(8,128)(2,1)S(1)}, bf16[128,384]{1,0:T(8,128)(2,1)S(1)}, u32[]{:S(2)}, u32[]{:S(2)}) collective-permute-start(bf16[128,384]{1,0:T(8,128)(2,1)S(1)} %get-tuple-element.55), channel_id=1, source_target_pairs={{0,16},{1,17},{2,18},{3,19},{4,20},{5,21},{6,22},{7,23},{8,24},{9,... | collective-permute-start | bytes 294920 | tf_op jit(solution)/shard_map/ppermute | solution.py:438
  45.0 6.9 %all-to-all-done.rest_0_ = bf16[8,128,384]{2,1,0:T(8,128)(2,1)S(1)} async-done(((bf16[8,128,384]{2,1,0:T(8,128)(2,1)}), bf16[8,128,384]{2,1,0:T(8,128)(2,1)S(1)}, u32[]{:S(2)}, u32[]{:S(2)}) %all-to-all-start) | async-done | bytes 786464 | tf_op jit(solution)/shard_map/all_to_all | solution.py:433
  54.1 3.6 %all-to-all-start.1 = ((bf16[8,128,384]{2,1,0:T(8,128)(2,1)}), bf16[8,128,384]{2,1,0:T(8,128)(2,1)S(1)}, u32[]{:S(2)}, u32[]{:S(2)}) async-start(bf16[8,128,384]{2,1,0:T(8,128)(2,1)} %shard_map.108), calls=%async_computation.1 | async-start | bytes 1572864 | tf_op jit(solution)/shard_map/all_to_all | solution.py:433
  57.7 1.6 %collective-permute-start.14 = (bf16[128,384]{1,0:T(8,128)(2,1)S(1)}, bf16[128,384]{1,0:T(8,128)(2,1)S(1)}, u32[]{:S(2)}, u32[]{:S(2)}) collective-permute-start(bf16[128,384]{1,0:T(8,128)(2,1)S(1)} %get-tuple-element.60), channel_id=1, source_target_pairs={{0,16},{1,17},{2,18},{3,19},{4,20},{5,21},{6,22},{7,23},{8,24},{9,... | collective-permute-start | bytes 294920 | tf_op jit(solution)/shard_map/ppermute | solution.py:438
  59.6 3.8 %collective-permute-done.14.rest_2_ = bf16[128,384]{1,0:T(8,128)(2,1)S(1)} collective-permute-done((bf16[128,384]{1,0:T(8,128)(2,1)S(1)}, bf16[128,384]{1,0:T(8,128)(2,1)S(1)}, u32[]{:S(2)}, u32[]{:S(2)}) %collective-permute-start.14) | collective-permute-done | bytes 98336 | tf_op jit(solution)/shard_map/ppermute | solution.py:438
  64.6 4.1 %shard_map.110 = (bf16[8,128,192]{2,1,0:T(8,128)(2,1)S(1)}, bf16[192,192]{1,0:T(8,128)(2,1)S(1)}, bf16[96,96]{1,0:T(8,128)(2,1)S(1)}, bf16[96,96]{1,0:T(8,128)(2...) custom-call(s32[1]{0:T(128)} %bitcast.own_out.member.own_in, s32[1]{0:T(128)} %bitcast.1.first_mode, ...), custom_call_target="tpu_custom_call" | custom-call | tf_op jit(solution)/shard_map/pallas_call | solution.py:65
  69.3 1.5 %collective-permute-start.17 = (bf16[96,96]{1,0:T(8,128)(2,1)S(1)}, bf16[96,96]{1,0:T(8,128)(2,1)S(1)}, u32[]{:S(2)}, u32[]{:S(2)}) collective-permute-start(bf16[96,96]{1,0:T(8,128)(2,1)S(1)} %get-tuple-element.65), channel_id=1, source_target_pairs={{0,16},{8,24},{16,0},{24,8},{1,17},{9,25},{17,1},{25,9},{2,18},{10... | collective-permute-start | bytes 55304 | tf_op jit(solution)/shard_map/ppermute | solution.py:438
  70.8 2.3 %collective-permute-done.17.refs_2_ = bf16[96,96]{1,0:T(8,128)(2,1)S(1)} collective-permute-done((bf16[96,96]{1,0:T(8,128)(2,1)S(1)}, bf16[96,96]{1,0:T(8,128)(2,1)S(1)}, u32[]{:S(2)}, u32[]{:S(2)}) %collective-permute-start.17) | collective-permute-done | bytes 18464 | tf_op jit(solution)/shard_map/ppermute | solution.py:438
  74.3 1.6 %shard_map.113 = (bf16[128,384]{1,0:T(8,128)(2,1)S(1)}, bf16[128,384]{1,0:T(8,128)(2,1)S(1)}, bf16[128,384]{1,0:T(8,128)(2,1)S(1)}, bf16[128,384]{1,0:T(8,128)(2,1)S(1)}) custom-call(s32[1]{0:T(128)} %bitcast.own_out.member.own_in, bf16[256,256]{1,0:T(8,128)(2,1)S(1)} %copy-done.4, bf16[8,128,192]{2,1,0:T(8,128)(2,1)S(1)} %get-tuple-element.67.grad_pre, ...), custom_call_target="tpu_custom_call" | custom-call | tf_op jit(solution)/shard_map/pallas_call | solution.py:65
  77.8 1.9 %collective-permute-start.19 = (bf16[1,96,96]{2,1,0:T(8,128)(2,1)S(1)}, bf16[1,96,96]{2,1,0:T(8,128)(2,1)S(1)}, u32[]{:S(2)}, u32[]{:S(2)}) collective-permute-start(bf16[1,96,96]{2,1,0:T(8,128)(2,1)S(1)} %shard_map.111.first.rest_0_), channel_id=1, source_target_pairs={{0,2},{1,3},{2,0},{3,1},{4,6},{5,7},{6,4},{7,5},{8,10},{9,11},{10,... | collective-permute-start | bytes 55304 | tf_op jit(solution)/shard_map/ppermute | solution.py:578
  79.8 1.9 %collective-permute-done.19.second = bf16[1,96,96]{2,1,0:T(8,128)(2,1)S(1)} collective-permute-done((bf16[1,96,96]{2,1,0:T(8,128)(2,1)S(1)}, bf16[1,96,96]{2,1,0:T(8,128)(2,1)S(1)}, u32[]{:S(2)}, u32[]{:S(2)}) %collective-permute-start.19) | collective-permute-done | bytes 18464 | tf_op jit(solution)/shard_map/ppermute | solution.py:578
  81.7 2.9 %collective-permute-start.20 = (bf16[2,96,96]{2,1,0:T(8,128)(2,1)S(1)}, bf16[2,96,96]{2,1,0:T(8,128)(2,1)S(1)}, u32[]{:S(2)}, u32[]{:S(2)}) collective-permute-start(bf16[2,96,96]{2,1,0:T(8,128)(2,1)S(1)} %shard_map.112.first), channel_id=1, source_target_pairs={{0,4},{1,5},{2,6},{3,7},{4,0},{5,1},{6,2},{7,3},{8,12},{9,13},{10,... | collective-permute-start | bytes 110600 | tf_op jit(solution)/shard_map/ppermute | solution.py:578
  84.6 1.2 %shard_map.114.rest_0_ = bf16[8,128,384]{2,1,0:T(8,128)(2,1)} custom-call(s32[1]{0:T(128)} %bitcast.own_out.member.own_in, bf16[512,256]{1,0:T(8,128)(2,1)S(1)} %copy-done.6, bf16[128,384]{1,0:T(8,128)(2,1)S(1)} %get-tuple-element.69.rest_0_, bf16[128,384]{1,0:T(8,128)(2,1)S(1)} %collective-permute-done.21.rest_1_, ...), custom_call_target="tpu_custom_call" | custom-call | tf_op jit(solution)/shard_map/pallas_call | solution.py:65
  85.8 1.3 %collective-permute-done.20.second = bf16[2,96,96]{2,1,0:T(8,128)(2,1)S(1)} collective-permute-done((bf16[2,96,96]{2,1,0:T(8,128)(2,1)S(1)}, bf16[2,96,96]{2,1,0:T(8,128)(2,1)S(1)}, u32[]{:S(2)}, u32[]{:S(2)}) %collective-permute-start.20) | collective-permute-done | bytes 36896 | tf_op jit(solution)/shard_map/ppermute | solution.py:578
  87.2 6.2 %all-to-all-start.2 = ((bf16[8,128,384]{2,1,0:T(8,128)(2,1)}), bf16[8,128,384]{2,1,0:T(8,128)(2,1)S(1)}, u32[]{:S(2)}, u32[]{:S(2)}) async-start(bf16[8,128,384]{2,1,0:T(8,128)(2,1)} %get-tuple-element.73), calls=%async_computation.2 | async-start | bytes 1572864 | tf_op jit(solution)/shard_map/all_to_all | solution.py:433
  93.4 2.0 %collective-permute-start.24 = (bf16[4,96,96]{2,1,0:T(8,128)(2,1)S(1)}, bf16[4,96,96]{2,1,0:T(8,128)(2,1)S(1)}, u32[]{:S(2)}, u32[]{:S(2)}) collective-permute-start(bf16[4,96,96]{2,1,0:T(8,128)(2,1)S(1)} %get-tuple-element.74.near), channel_id=1, source_target_pairs={{0,1},{1,0},{2,3},{3,2},{4,5},{5,4},{6,7},{7,6},{8,9},{9,8},{10,11... | collective-permute-start | bytes 221192 | tf_op jit(solution)/shard_map/ppermute | solution.py:593
  96.5 5.6 %collective-permute-done.24.other = bf16[4,96,96]{2,1,0:T(8,128)(2,1)S(1)} collective-permute-done((bf16[4,96,96]{2,1,0:T(8,128)(2,1)S(1)}, bf16[4,96,96]{2,1,0:T(8,128)(2,1)S(1)}, u32[]{:S(2)}, u32[]{:S(2)}) %collective-permute-start.24) | collective-permute-done | bytes 73760 | tf_op jit(solution)/shard_map/ppermute | solution.py:593
  104.1 5.0 %collective-permute-done.26.rest_2_ = bf16[8,96,96]{2,1,0:T(8,128)(2,1)S(1)} collective-permute-done((bf16[8,96,96]{2,1,0:T(8,128)(2,1)S(1)}, bf16[8,96,96]{2,1,0:T(8,128)(2,1)S(1)}, u32[]{:S(2)}, u32[]{:S(2)}) %collective-permute-start.26) | collective-permute-done | bytes 147488 | tf_op jit(solution)/shard_map/ppermute | solution.py:601
  109.0 3.1 %all-to-all-done.2.packed = bf16[8,128,384]{2,1,0:T(8,128)(2,1)S(1)} async-done(((bf16[8,128,384]{2,1,0:T(8,128)(2,1)}), bf16[8,128,384]{2,1,0:T(8,128)(2,1)S(1)}, u32[]{:S(2)}, u32[]{:S(2)}) %all-to-all-start.2) | async-done | bytes 786464 | tf_op jit(solution)/shard_map/all_to_all | solution.py:433
  112.1 1.7 %shard_map.117 = (bf16[32,16,768]{2,1,0:T(8,128)(2,1)}, f32[2,8,96,96]{3,2,1,0:T(8,128)}, f32[2,8,96,96]{3,2,1,0:T(8,128)}) custom-call(s32[1]{0:T(128)} %bitcast.4.lat_own, bf16[8,128,384]{2,1,0:T(8,128)(2,1)S(1)} %all-to-all-done.2.packed, bf16[32,16,768]{2,1,0:T(8,128)(2,1)S(1)} %copy-done.1, bf16[8,96,96]{2,1,0:T(8,128)(2,1)S(1)} %shard_map.116.rest_0_, ...), custom_call_target="tpu_custom_call" | custom-call | tf_op jit(solution)/shard_map/pallas_call | solution.py:65
  (60 shorter events, 14.2 us)
Async XLA Ops:
  2.3 8.9 %collective-permute-start = (bf16[128,384]{1,0:T(8,128)(2,1)S(1)}, bf16[128,384]{1,0:T(8,128)(2,1)S(1)}, u32[]{:S(2)}, u32[]{:S(2)}) collective-permute-start(bf16[128,384]{1,0:T(8,128)(2,1)S(1)} %get-tuple-element.42), channel_id=1, source_target_pairs={{0,1},{1,0},{2,3},{3,2},{4,5},{5,4},{6,7},{7,6},{8,9},{9,8},{10,11... | collective-permute-start | bytes 294920 | tf_op jit(solution)/shard_map/ppermute | solution.py:438
  5.4 9.5 %collective-permute-start.1 = (bf16[128,384]{1,0:T(8,128)(2,1)S(1)}, bf16[128,384]{1,0:T(8,128)(2,1)S(1)}, u32[]{:S(2)}, u32[]{:S(2)}) collective-permute-start(bf16[128,384]{1,0:T(8,128)(2,1)S(1)} %get-tuple-element.43), channel_id=1, source_target_pairs={{0,2},{1,3},{2,0},{3,1},{4,6},{5,7},{6,4},{7,5},{8,10},{9,11},{10,... | collective-permute-start | bytes 294920 | tf_op jit(solution)/shard_map/ppermute | solution.py:438
  7.0 10.5 %collective-permute-start.2 = (bf16[128,384]{1,0:T(8,128)(2,1)S(1)}, bf16[128,384]{1,0:T(8,128)(2,1)S(1)}, u32[]{:S(2)}, u32[]{:S(2)}) collective-permute-start(bf16[128,384]{1,0:T(8,128)(2,1)S(1)} %get-tuple-element.44), channel_id=1, source_target_pairs={{0,3},{1,2},{2,1},{3,0},{4,7},{5,6},{6,5},{7,4},{8,11},{9,10},{10,... | collective-permute-start | bytes 294920 | tf_op jit(solution)/shard_map/ppermute | solution.py:438
  7.0 10.5 %collective-permute-start.3 = (bf16[128,384]{1,0:T(8,128)(2,1)S(1)}, bf16[128,384]{1,0:T(8,128)(2,1)S(1)}, u32[]{:S(2)}, u32[]{:S(2)}) collective-permute-start(bf16[128,384]{1,0:T(8,128)(2,1)S(1)} %get-tuple-element.45), channel_id=1, source_target_pairs={{0,4},{1,5},{2,6},{3,7},{4,0},{5,1},{6,2},{7,3},{8,12},{9,13},{10,... | collective-permute-start | bytes 294920 | tf_op jit(solution)/shard_map/ppermute | solution.py:438
  9.9 15.2 %collective-permute-start.4 = (bf16[128,384]{1,0:T(8,128)(2,1)S(1)}, bf16[128,384]{1,0:T(8,128)(2,1)S(1)}, u32[]{:S(2)}, u32[]{:S(2)}) collective-permute-start(bf16[128,384]{1,0:T(8,128)(2,1)S(1)} %get-tuple-element.46), channel_id=1, source_target_pairs={{0,5},{1,4},{2,7},{3,6},{4,1},{5,0},{6,3},{7,2},{8,13},{9,12},{10,... | collective-permute-start | bytes 294920 | tf_op jit(solution)/shard_map/ppermute | solution.py:438
  11.2 13.9 %collective-permute-start.5 = (bf16[128,384]{1,0:T(8,128)(2,1)S(1)}, bf16[128,384]{1,0:T(8,128)(2,1)S(1)}, u32[]{:S(2)}, u32[]{:S(2)}) collective-permute-start(bf16[128,384]{1,0:T(8,128)(2,1)S(1)} %get-tuple-element.47), channel_id=1, source_target_pairs={{0,6},{1,7},{2,4},{3,5},{4,2},{5,3},{6,0},{7,1},{8,14},{9,15},{10,... | collective-permute-start | bytes 294920 | tf_op jit(solution)/shard_map/ppermute | solution.py:438
  14.8 10.3 %collective-permute-start.6 = (bf16[128,384]{1,0:T(8,128)(2,1)S(1)}, bf16[128,384]{1,0:T(8,128)(2,1)S(1)}, u32[]{:S(2)}, u32[]{:S(2)}) collective-permute-start(bf16[128,384]{1,0:T(8,128)(2,1)S(1)} %get-tuple-element.48), channel_id=1, source_target_pairs={{0,7},{1,6},{2,5},{3,4},{4,3},{5,2},{6,1},{7,0},{8,15},{9,14},{10,... | collective-permute-start | bytes 294920 | tf_op jit(solution)/shard_map/ppermute | solution.py:438
  25.7 26.2 %all-to-all-start = ((bf16[8,128,384]{2,1,0:T(8,128)(2,1)}), bf16[8,128,384]{2,1,0:T(8,128)(2,1)S(1)}, u32[]{:S(2)}, u32[]{:S(2)}) async-start(bf16[8,128,384]{2,1,0:T(8,128)(2,1)} %shard_map.106), calls=%async_computation | async-start | bytes 1572864 | tf_op jit(solution)/shard_map/all_to_all | solution.py:433
  32.3 1.9 %collective-permute-start.7 = (bf16[128,384]{1,0:T(8,128)(2,1)S(1)}, bf16[128,384]{1,0:T(8,128)(2,1)S(1)}, u32[]{:S(2)}, u32[]{:S(2)}) collective-permute-start(bf16[128,384]{1,0:T(8,128)(2,1)S(1)} %get-tuple-element.50), channel_id=1, source_target_pairs={{0,8},{1,9},{2,10},{3,11},{4,12},{5,13},{6,14},{7,15},{8,0},{9,1},... | collective-permute-start | bytes 294920 | tf_op jit(solution)/shard_map/ppermute | solution.py:438
  32.3 5.7 %collective-permute-start.8 = (bf16[128,384]{1,0:T(8,128)(2,1)S(1)}, bf16[128,384]{1,0:T(8,128)(2,1)S(1)}, u32[]{:S(2)}, u32[]{:S(2)}) collective-permute-start(bf16[128,384]{1,0:T(8,128)(2,1)S(1)} %get-tuple-element.51), channel_id=1, source_target_pairs={{0,16},{1,17},{2,18},{3,19},{4,20},{5,21},{6,22},{7,23},{8,24},{9,... | collective-permute-start | bytes 294920 | tf_op jit(solution)/shard_map/ppermute | solution.py:438
  33.9 5.3 %collective-permute-start.9 = (bf16[128,384]{1,0:T(8,128)(2,1)S(1)}, bf16[128,384]{1,0:T(8,128)(2,1)S(1)}, u32[]{:S(2)}, u32[]{:S(2)}) collective-permute-start(bf16[128,384]{1,0:T(8,128)(2,1)S(1)} %get-tuple-element.52), channel_id=1, source_target_pairs={{0,24},{1,25},{2,26},{3,27},{4,28},{5,29},{6,30},{7,31},{8,16},{9,... | collective-permute-start | bytes 294920 | tf_op jit(solution)/shard_map/ppermute | solution.py:438
  42.9 9.5 %collective-permute-start.10 = (bf16[128,384]{1,0:T(8,128)(2,1)S(1)}, bf16[128,384]{1,0:T(8,128)(2,1)S(1)}, u32[]{:S(2)}, u32[]{:S(2)}) collective-permute-start(bf16[128,384]{1,0:T(8,128)(2,1)S(1)} %get-tuple-element.54), channel_id=1, source_target_pairs={{0,8},{1,9},{2,10},{3,11},{4,12},{5,13},{6,14},{7,15},{8,0},{9,1},... | collective-permute-start | bytes 294920 | tf_op jit(solution)/shard_map/ppermute | solution.py:438
  43.5 8.9 %collective-permute-start.11 = (bf16[128,384]{1,0:T(8,128)(2,1)S(1)}, bf16[128,384]{1,0:T(8,128)(2,1)S(1)}, u32[]{:S(2)}, u32[]{:S(2)}) collective-permute-start(bf16[128,384]{1,0:T(8,128)(2,1)S(1)} %get-tuple-element.55), channel_id=1, source_target_pairs={{0,16},{1,17},{2,18},{3,19},{4,20},{5,21},{6,22},{7,23},{8,24},{9,... | collective-permute-start | bytes 294920 | tf_op jit(solution)/shard_map/ppermute | solution.py:438
  45.0 7.4 %collective-permute-start.12 = (bf16[128,384]{1,0:T(8,128)(2,1)S(1)}, bf16[128,384]{1,0:T(8,128)(2,1)S(1)}, u32[]{:S(2)}, u32[]{:S(2)}) collective-permute-start(bf16[128,384]{1,0:T(8,128)(2,1)S(1)} %get-tuple-element.56), channel_id=1, source_target_pairs={{0,24},{1,25},{2,26},{3,27},{4,28},{5,29},{6,30},{7,31},{8,16},{9,... | collective-permute-start | bytes 294920 | tf_op jit(solution)/shard_map/ppermute | solution.py:438
  54.1 33.1 %all-to-all-start.1 = ((bf16[8,128,384]{2,1,0:T(8,128)(2,1)}), bf16[8,128,384]{2,1,0:T(8,128)(2,1)S(1)}, u32[]{:S(2)}, u32[]{:S(2)}) async-start(bf16[8,128,384]{2,1,0:T(8,128)(2,1)} %shard_map.108), calls=%async_computation.1 | async-start | bytes 1572864 | tf_op jit(solution)/shard_map/all_to_all | solution.py:433
  57.7 1.9 %collective-permute-start.13 = (bf16[128,384]{1,0:T(8,128)(2,1)S(1)}, bf16[128,384]{1,0:T(8,128)(2,1)S(1)}, u32[]{:S(2)}, u32[]{:S(2)}) collective-permute-start(bf16[128,384]{1,0:T(8,128)(2,1)S(1)} %get-tuple-element.59), channel_id=1, source_target_pairs={{0,8},{1,9},{2,10},{3,11},{4,12},{5,13},{6,14},{7,15},{8,0},{9,1},... | collective-permute-start | bytes 294920 | tf_op jit(solution)/shard_map/ppermute | solution.py:438
  57.7 5.7 %collective-permute-start.14 = (bf16[128,384]{1,0:T(8,128)(2,1)S(1)}, bf16[128,384]{1,0:T(8,128)(2,1)S(1)}, u32[]{:S(2)}, u32[]{:S(2)}) collective-permute-start(bf16[128,384]{1,0:T(8,128)(2,1)S(1)} %get-tuple-element.60), channel_id=1, source_target_pairs={{0,16},{1,17},{2,18},{3,19},{4,20},{5,21},{6,22},{7,23},{8,24},{9,... | collective-permute-start | bytes 294920 | tf_op jit(solution)/shard_map/ppermute | solution.py:438
  59.3 5.3 %collective-permute-start.15 = (bf16[128,384]{1,0:T(8,128)(2,1)S(1)}, bf16[128,384]{1,0:T(8,128)(2,1)S(1)}, u32[]{:S(2)}, u32[]{:S(2)}) collective-permute-start(bf16[128,384]{1,0:T(8,128)(2,1)S(1)} %get-tuple-element.61), channel_id=1, source_target_pairs={{0,24},{1,25},{2,26},{3,27},{4,28},{5,29},{6,30},{7,31},{8,16},{9,... | collective-permute-start | bytes 294920 | tf_op jit(solution)/shard_map/ppermute | solution.py:438
  68.7 2.1 %collective-permute-start.16 = (bf16[96,96]{1,0:T(8,128)(2,1)S(1)}, bf16[96,96]{1,0:T(8,128)(2,1)S(1)}, u32[]{:S(2)}, u32[]{:S(2)}) collective-permute-start(bf16[96,96]{1,0:T(8,128)(2,1)S(1)} %get-tuple-element.64), channel_id=1, source_target_pairs={{0,8},{8,0},{16,24},{24,16},{1,9},{9,1},{17,25},{25,17},{2,10},{10... | collective-permute-start | bytes 55304 | tf_op jit(solution)/shard_map/ppermute | solution.py:438
  69.3 3.8 %collective-permute-start.17 = (bf16[96,96]{1,0:T(8,128)(2,1)S(1)}, bf16[96,96]{1,0:T(8,128)(2,1)S(1)}, u32[]{:S(2)}, u32[]{:S(2)}) collective-permute-start(bf16[96,96]{1,0:T(8,128)(2,1)S(1)} %get-tuple-element.65), channel_id=1, source_target_pairs={{0,16},{8,24},{16,0},{24,8},{1,17},{9,25},{17,1},{25,9},{2,18},{10... | collective-permute-start | bytes 55304 | tf_op jit(solution)/shard_map/ppermute | solution.py:438
  70.8 3.5 %collective-permute-start.18 = (bf16[96,96]{1,0:T(8,128)(2,1)S(1)}, bf16[96,96]{1,0:T(8,128)(2,1)S(1)}, u32[]{:S(2)}, u32[]{:S(2)}) collective-permute-start(bf16[96,96]{1,0:T(8,128)(2,1)S(1)} %get-tuple-element.66), channel_id=1, source_target_pairs={{0,24},{8,16},{16,8},{24,0},{1,25},{9,17},{17,9},{25,1},{2,26},{10... | collective-permute-start | bytes 55304 | tf_op jit(solution)/shard_map/ppermute | solution.py:438
  75.9 8.7 %collective-permute-start.21 = (bf16[128,384]{1,0:T(8,128)(2,1)S(1)}, bf16[128,384]{1,0:T(8,128)(2,1)S(1)}, u32[]{:S(2)}, u32[]{:S(2)}) collective-permute-start(bf16[128,384]{1,0:T(8,128)(2,1)S(1)} %get-tuple-element.70), channel_id=1, source_target_pairs={{0,8},{1,9},{2,10},{3,11},{4,12},{5,13},{6,14},{7,15},{8,0},{9,1},... | collective-permute-start | bytes 294920 | tf_op jit(solution)/shard_map/ppermute | solution.py:438
  76.1 8.5 %collective-permute-start.22 = (bf16[128,384]{1,0:T(8,128)(2,1)S(1)}, bf16[128,384]{1,0:T(8,128)(2,1)S(1)}, u32[]{:S(2)}, u32[]{:S(2)}) collective-permute-start(bf16[128,384]{1,0:T(8,128)(2,1)S(1)} %get-tuple-element.71), channel_id=1, source_target_pairs={{0,16},{1,17},{2,18},{3,19},{4,20},{5,21},{6,22},{7,23},{8,24},{9,... | collective-permute-start | bytes 294920 | tf_op jit(solution)/shard_map/ppermute | solution.py:438
  76.9 7.7 %collective-permute-start.23 = (bf16[128,384]{1,0:T(8,128)(2,1)S(1)}, bf16[128,384]{1,0:T(8,128)(2,1)S(1)}, u32[]{:S(2)}, u32[]{:S(2)}) collective-permute-start(bf16[128,384]{1,0:T(8,128)(2,1)S(1)} %get-tuple-element.72), channel_id=1, source_target_pairs={{0,24},{1,25},{2,26},{3,27},{4,28},{5,29},{6,30},{7,31},{8,16},{9,... | collective-permute-start | bytes 294920 | tf_op jit(solution)/shard_map/ppermute | solution.py:438
  77.8 3.8 %collective-permute-start.19 = (bf16[1,96,96]{2,1,0:T(8,128)(2,1)S(1)}, bf16[1,96,96]{2,1,0:T(8,128)(2,1)S(1)}, u32[]{:S(2)}, u32[]{:S(2)}) collective-permute-start(bf16[1,96,96]{2,1,0:T(8,128)(2,1)S(1)} %shard_map.111.first.rest_0_), channel_id=1, source_target_pairs={{0,2},{1,3},{2,0},{3,1},{4,6},{5,7},{6,4},{7,5},{8,10},{9,11},{10,... | collective-permute-start | bytes 55304 | tf_op jit(solution)/shard_map/ppermute | solution.py:578
  81.7 5.5 %collective-permute-start.20 = (bf16[2,96,96]{2,1,0:T(8,128)(2,1)S(1)}, bf16[2,96,96]{2,1,0:T(8,128)(2,1)S(1)}, u32[]{:S(2)}, u32[]{:S(2)}) collective-permute-start(bf16[2,96,96]{2,1,0:T(8,128)(2,1)S(1)} %shard_map.112.first), channel_id=1, source_target_pairs={{0,4},{1,5},{2,6},{3,7},{4,0},{5,1},{6,2},{7,3},{8,12},{9,13},{10,... | collective-permute-start | bytes 110600 | tf_op jit(solution)/shard_map/ppermute | solution.py:578
  87.2 24.9 %all-to-all-start.2 = ((bf16[8,128,384]{2,1,0:T(8,128)(2,1)}), bf16[8,128,384]{2,1,0:T(8,128)(2,1)S(1)}, u32[]{:S(2)}, u32[]{:S(2)}) async-start(bf16[8,128,384]{2,1,0:T(8,128)(2,1)} %get-tuple-element.73), calls=%async_computation.2 | async-start | bytes 1572864 | tf_op jit(solution)/shard_map/all_to_all | solution.py:433
  93.4 8.7 %collective-permute-start.24 = (bf16[4,96,96]{2,1,0:T(8,128)(2,1)S(1)}, bf16[4,96,96]{2,1,0:T(8,128)(2,1)S(1)}, u32[]{:S(2)}, u32[]{:S(2)}) collective-permute-start(bf16[4,96,96]{2,1,0:T(8,128)(2,1)S(1)} %get-tuple-element.74.near), channel_id=1, source_target_pairs={{0,1},{1,0},{2,3},{3,2},{4,5},{5,4},{6,7},{7,6},{8,9},{9,8},{10,11... | collective-permute-start | bytes 221192 | tf_op jit(solution)/shard_map/ppermute | solution.py:593
  96.5 15.6 %copy-start.1 = (bf16[32,16,768]{2,1,0:T(8,128)(2,1)S(1)}, bf16[32,16,768]{2,1,0:T(8,128)(2,1)}, u32[]{:S(2)}) copy-start(bf16[32,16,768]{2,1,0:T(8,128)(2,1)} %base.3) | copy-start | bytes 2359300
  103.3 5.7 %collective-permute-start.26 = (bf16[8,96,96]{2,1,0:T(8,128)(2,1)S(1)}, bf16[8,96,96]{2,1,0:T(8,128)(2,1)S(1)}, u32[]{:S(2)}, u32[]{:S(2)}) collective-permute-start(bf16[8,96,96]{2,1,0:T(8,128)(2,1)S(1)} %shard_map.116.rest_0_), channel_id=1, source_target_pairs={{0,16},{8,24},{16,0},{24,8},{1,17},{9,25},{17,1},{25,9},{2,18},{10... | collective-permute-start | bytes 442376 | tf_op jit(solution)/shard_map/ppermute | solution.py:601
  104.0 5.0 %collective-permute-start.25 = (bf16[8,96,96]{2,1,0:T(8,128)(2,1)S(1)}, bf16[8,96,96]{2,1,0:T(8,128)(2,1)S(1)}, u32[]{:S(2)}, u32[]{:S(2)}) collective-permute-start(bf16[8,96,96]{2,1,0:T(8,128)(2,1)S(1)} %shard_map.116.rest_0_), channel_id=1, source_target_pairs={{0,8},{8,0},{16,24},{24,16},{1,9},{9,1},{17,25},{25,17},{2,10},{10... | collective-permute-start | bytes 442376 | tf_op jit(solution)/shard_map/ppermute | solution.py:601
  109.0 3.1 %collective-permute-start.27 = (bf16[8,96,96]{2,1,0:T(8,128)(2,1)S(1)}, bf16[8,96,96]{2,1,0:T(8,128)(2,1)S(1)}, u32[]{:S(2)}, u32[]{:S(2)}) collective-permute-start(bf16[8,96,96]{2,1,0:T(8,128)(2,1)S(1)} %collective-permute-done.26.rest_2_), channel_id=1, source_target_pairs={{0,8},{8,0},{16,24},{24,16},{1,9},{9,1},{17,25},{25,17},{2,10},{10... | collective-permute-start | bytes 442376 | tf_op jit(solution)/shard_map/ppermute | solution.py:601
  (6 other events, 34.9 us)

commit v7 on v6

--- a/solution.py
+++ b/solution.py
@@ -33,12 +33,11 @@
     return cos, sin
 
 
-def lon_tables(kept, cols, lon_count, rows):
+def lon_table(kept, cols, lon_count, rows):
     cos, sin = wave_table(np.arange(kept), np.arange(cols), cols)
     parts = np.stack([cos, -sin], axis=1).reshape(kept, 2, lon_count, cols // lon_count)
     eye = np.eye(rows, dtype=np.float32)
-    forward = np.einsum("kpgw,rs->kprgsw", parts, eye).reshape(2 * kept * rows, -1)
-    return forward, forward.T
+    return np.einsum("kpgw,rs->kprgsw", parts, eye).reshape(2 * kept * rows, -1)
 
 
 def lat_table(rows, lat_count, subs, rows_sub, rows_cut, pack_modes):
@@ -197,9 +196,10 @@
     modes = slots_in.shape[0] * kept
     split = slots_in[...].astype(jnp.float32).reshape(modes, cuts, -1, PACK)
     flats = [split[:, cut].reshape(-1, PACK).astype(jnp.bfloat16) for cut in range(cuts)]
+    inverse = table[...].T
     copies = []
     for cut, flat in enumerate(flats):
-        part = product(table[...], flat).astype(jnp.bfloat16)
+        part = product(inverse, flat).astype(jnp.bfloat16)
         rows = pl.ds(cut * each, each)
         slots_out[:, rows] = part.reshape(slots_out.shape[0], each, PACK)
         copies.append(
@@ -475,7 +475,7 @@
     def line_pairs(count):
         return lambda offset: [(place, place ^ offset) for place in range(count)]
 
-    lon_fwd, lon_inv = map(constant, lon_tables(kept_total, cols_total, lon_count, rows_cut))
+    lon_fwd = constant(lon_table(kept_total, cols_total, lon_count, rows_cut))
     lat_both = constant(lat_table(rows_total, lat_count, subs, rows_sub, rows_cut, pack_modes))
     lon_piece = array((rows_sub * band_cols, PACK), bf16)
     lon_whole = array((lon_count, rows_sub * band_cols, PACK), bf16)
@@ -511,7 +511,7 @@
             functools.partial(columns_body, members, len(anchors), cuts, kept),
             [pltpu.HBM(lon_whole.shape, bf16)],
             [member],
-            [lon_inv, *pieces],
+            [lon_fwd, *pieces],
             [mid_slots, lon_slots, pltpu.SemaphoreType.DMA((cuts,))],
             anchors,
         )[0]

time: 114 us -> 114 us (level)
    unnamed x14 -> x12, local copies, waits for them, and re-layouts: 2.47 us -> 2.03 us
where the time goes in v7:
time: 114 us; the launch traced here: 113 us
  starting transfers between devices  46.6 us (41%)
  waiting for transfers between devices  44.8 us (39%)
  Pallas kernels  19.1 us (17%)
  local copies, waits for them, and re-layouts  2.03 us (2%)
    ppermute x22, starting transfers between devices, swap(): lax.ppermute(piece, axes, partners(offset))  22.4 us
    ppermute x22, waiting for transfers between devices, swap(): lax.ppermute(piece, axes, partners(offset))  21.2 us
    pallas_call x13, Pallas kernels, kernel_call(): pl.pallas_call(body, out_shape=out_shape, in_specs=in_specs, out_specs=[s...  19.1 us
    all_to_all x3, starting transfers between devices, exchange(): lax.all_to_all(source, 'lon', split_axis=0, concat_axis=0, tiled=True)  16.4 us
    all_to_all x3, waiting for transfers between devices, exchange(): lax.all_to_all(source, 'lon', split_axis=0, concat_axis=0, tiled=True)  10 us
    ppermute x1, waiting for transfers between devices, shards(): lax.ppermute(near, 'lon', lon_pairs(1))  5.59 us
    ppermute x3, waiting for transfers between devices, shards(): moved = lax.ppermute(gathered[offset], 'lat', line_pairs(lat_count)(step))  4.84 us
    ppermute x2, starting transfers between devices, shards(): moved = lax.ppermute(near, 'lon', lon_pairs(step))  4.83 us
  transfers between devices with their start and end apart: 31, of which 13 were waited for; matrix products, arithmetic and copies ran while one was open for 0% of the time, Pallas kernels for 12%

profile of v7, /device:TPU:0, one launch (start us, length us, event | category | flops | bytes accessed | tf_op | source)
XLA Modules:
  0.0 113.4 jit_solution(2871028939440681731)
XLA Ops:
  0.6 1.7 %shard_map.93 = (bf16[128,384]{1,0:T(8,128)(2,1)S(1)}, bf16[128,384]{1,0:T(8,128)(2,1)S(1)}, bf16[128,384]{1,0:T(8,128)(2,1)S(1)}, bf16[128,384]{1,0:T(8,128)(2,...) custom-call(s32[1]{0:T(128)} %bitcast.3.own.own_in, ...), custom_call_target="tpu_custom_call" | custom-call | tf_op jit(solution)/shard_map/pallas_call | solution.py:64
  2.3 3.0 %collective-permute-start = (bf16[128,384]{1,0:T(8,128)(2,1)S(1)}, bf16[128,384]{1,0:T(8,128)(2,1)S(1)}, u32[]{:S(2)}, u32[]{:S(2)}) collective-permute-start(bf16[128,384]{1,0:T(8,128)(2,1)S(1)} %get-tuple-element.42), channel_id=1, source_target_pairs={{0,1},{1,0},{2,3},{3,2},{4,5},{5,4},{6,7},{7,6},{8,9},{9,8},{10,11... | collective-permute-start | bytes 294920 | tf_op jit(solution)/shard_map/ppermute | solution.py:438
  5.4 1.6 %collective-permute-start.1 = (bf16[128,384]{1,0:T(8,128)(2,1)S(1)}, bf16[128,384]{1,0:T(8,128)(2,1)S(1)}, u32[]{:S(2)}, u32[]{:S(2)}) collective-permute-start(bf16[128,384]{1,0:T(8,128)(2,1)S(1)} %get-tuple-element.43), channel_id=1, source_target_pairs={{0,2},{1,3},{2,0},{3,1},{4,6},{5,7},{6,4},{7,5},{8,10},{9,11},{10,... | collective-permute-start | bytes 294920 | tf_op jit(solution)/shard_map/ppermute | solution.py:438
  7.0 3.0 %collective-permute-start.3 = (bf16[128,384]{1,0:T(8,128)(2,1)S(1)}, bf16[128,384]{1,0:T(8,128)(2,1)S(1)}, u32[]{:S(2)}, u32[]{:S(2)}) collective-permute-start(bf16[128,384]{1,0:T(8,128)(2,1)S(1)} %get-tuple-element.45), channel_id=1, source_target_pairs={{0,4},{1,5},{2,6},{3,7},{4,0},{5,1},{6,2},{7,3},{8,12},{9,13},{10,... | collective-permute-start | bytes 294920 | tf_op jit(solution)/shard_map/ppermute | solution.py:438
  9.9 1.3 %collective-permute-start.4 = (bf16[128,384]{1,0:T(8,128)(2,1)S(1)}, bf16[128,384]{1,0:T(8,128)(2,1)S(1)}, u32[]{:S(2)}, u32[]{:S(2)}) collective-permute-start(bf16[128,384]{1,0:T(8,128)(2,1)S(1)} %get-tuple-element.46), channel_id=1, source_target_pairs={{0,5},{1,4},{2,7},{3,6},{4,1},{5,0},{6,3},{7,2},{8,13},{9,12},{10,... | collective-permute-start | bytes 294920 | tf_op jit(solution)/shard_map/ppermute | solution.py:438
  11.2 3.6 %collective-permute-start.5 = (bf16[128,384]{1,0:T(8,128)(2,1)S(1)}, bf16[128,384]{1,0:T(8,128)(2,1)S(1)}, u32[]{:S(2)}, u32[]{:S(2)}) collective-permute-start(bf16[128,384]{1,0:T(8,128)(2,1)S(1)} %get-tuple-element.47), channel_id=1, source_target_pairs={{0,6},{1,7},{2,4},{3,5},{4,2},{5,3},{6,0},{7,1},{8,14},{9,15},{10,... | collective-permute-start | bytes 294920 | tf_op jit(solution)/shard_map/ppermute | solution.py:438
  14.8 1.7 %shard_map.96.refs_0_ = bf16[8,128,384]{2,1,0:T(8,128)(2,1)S(1)} custom-call(s32[1]{0:T(128)} %bitcast.3.own.own_in, bf16[32,16,768]{2,1,0:T(8,128)(2,1)} %base.3), custom_call_target="tpu_custom_call" | custom-call | tf_op jit(solution)/shard_map/pallas_call | solution.py:64
  17.5 7.7 %collective-permute-done.4.rest_5_ = bf16[128,384]{1,0:T(8,128)(2,1)S(1)} collective-permute-done((bf16[128,384]{1,0:T(8,128)(2,1)S(1)}, bf16[128,384]{1,0:T(8,128)(2,1)S(1)}, u32[]{:S(2)}, u32[]{:S(2)}) %collective-permute-start.4) | collective-permute-done | bytes 98336 | tf_op jit(solution)/shard_map/ppermute | solution.py:438
  25.7 6.6 %all-to-all-start = ((bf16[8,128,384]{2,1,0:T(8,128)(2,1)}), bf16[8,128,384]{2,1,0:T(8,128)(2,1)S(1)}, u32[]{:S(2)}, u32[]{:S(2)}) async-start(bf16[8,128,384]{2,1,0:T(8,128)(2,1)} %shard_map.97), calls=%async_computation | async-start | bytes 1572864 | tf_op jit(solution)/shard_map/all_to_all | solution.py:433
  32.3 1.6 %collective-permute-start.8 = (bf16[128,384]{1,0:T(8,128)(2,1)S(1)}, bf16[128,384]{1,0:T(8,128)(2,1)S(1)}, u32[]{:S(2)}, u32[]{:S(2)}) collective-permute-start(bf16[128,384]{1,0:T(8,128)(2,1)S(1)} %get-tuple-element.51), channel_id=1, source_target_pairs={{0,16},{1,17},{2,18},{3,19},{4,20},{5,21},{6,22},{7,23},{8,24},{9,... | collective-permute-start | bytes 294920 | tf_op jit(solution)/shard_map/ppermute | solution.py:438
  34.2 3.8 %collective-permute-done.8.rest_2_ = bf16[128,384]{1,0:T(8,128)(2,1)S(1)} collective-permute-done((bf16[128,384]{1,0:T(8,128)(2,1)S(1)}, bf16[128,384]{1,0:T(8,128)(2,1)S(1)}, u32[]{:S(2)}, u32[]{:S(2)}) %collective-permute-start.8) | collective-permute-done | bytes 98336 | tf_op jit(solution)/shard_map/ppermute | solution.py:438
  39.2 3.7 %shard_map.95 = (bf16[128,384]{1,0:T(8,128)(2,1)S(1)}, bf16[128,384]{1,0:T(8,128)(2,1)S(1)}, bf16[128,384]{1,0:T(8,128)(2,1)S(1)}, bf16[128,384]{1,0:T(8,128)(2,...) custom-call(s32[1]{0:T(128)} %bitcast.own_out.member.own_in, s32[1]{0:T(128)} %bitcast.1.first_mode, ...), custom_call_target="tpu_custom_call" | custom-call | tf_op jit(solution)/shard_map/pallas_call | solution.py:64
  43.5 1.5 %collective-permute-start.11 = (bf16[128,384]{1,0:T(8,128)(2,1)S(1)}, bf16[128,384]{1,0:T(8,128)(2,1)S(1)}, u32[]{:S(2)}, u32[]{:S(2)}) collective-permute-start(bf16[128,384]{1,0:T(8,128)(2,1)S(1)} %get-tuple-element.55), channel_id=1, source_target_pairs={{0,16},{1,17},{2,18},{3,19},{4,20},{5,21},{6,22},{7,23},{8,24},{9,... | collective-permute-start | bytes 294920 | tf_op jit(solution)/shard_map/ppermute | solution.py:438
  45.0 6.9 %all-to-all-done.rest_0_ = bf16[8,128,384]{2,1,0:T(8,128)(2,1)S(1)} async-done(((bf16[8,128,384]{2,1,0:T(8,128)(2,1)}), bf16[8,128,384]{2,1,0:T(8,128)(2,1)S(1)}, u32[]{:S(2)}, u32[]{:S(2)}) %all-to-all-start) | async-done | bytes 786464 | tf_op jit(solution)/shard_map/all_to_all | solution.py:433
  53.7 3.7 %all-to-all-start.1 = ((bf16[8,128,384]{2,1,0:T(8,128)(2,1)}), bf16[8,128,384]{2,1,0:T(8,128)(2,1)S(1)}, u32[]{:S(2)}, u32[]{:S(2)}) async-start(bf16[8,128,384]{2,1,0:T(8,128)(2,1)} %shard_map.99), calls=%async_computation.1 | async-start | bytes 1572864 | tf_op jit(solution)/shard_map/all_to_all | solution.py:433
  57.4 1.5 %collective-permute-start.14 = (bf16[128,384]{1,0:T(8,128)(2,1)S(1)}, bf16[128,384]{1,0:T(8,128)(2,1)S(1)}, u32[]{:S(2)}, u32[]{:S(2)}) collective-permute-start(bf16[128,384]{1,0:T(8,128)(2,1)S(1)} %get-tuple-element.60), channel_id=1, source_target_pairs={{0,16},{1,17},{2,18},{3,19},{4,20},{5,21},{6,22},{7,23},{8,24},{9,... | collective-permute-start | bytes 294920 | tf_op jit(solution)/shard_map/ppermute | solution.py:438
  59.2 3.8 %collective-permute-done.14.rest_2_ = bf16[128,384]{1,0:T(8,128)(2,1)S(1)} collective-permute-done((bf16[128,384]{1,0:T(8,128)(2,1)S(1)}, bf16[128,384]{1,0:T(8,128)(2,1)S(1)}, u32[]{:S(2)}, u32[]{:S(2)}) %collective-permute-start.14) | collective-permute-done | bytes 98336 | tf_op jit(solution)/shard_map/ppermute | solution.py:438
  64.2 4.1 %shard_map.101 = (bf16[8,128,192]{2,1,0:T(8,128)(2,1)S(1)}, bf16[192,192]{1,0:T(8,128)(2,1)S(1)}, bf16[96,96]{1,0:T(8,128)(2,1)S(1)}, bf16[96,96]{1,0:T(8,128)(2...) custom-call(s32[1]{0:T(128)} %bitcast.own_out.member.own_in, s32[1]{0:T(128)} %bitcast.1.first_mode, ...), custom_call_target="tpu_custom_call" | custom-call | tf_op jit(solution)/shard_map/pallas_call | solution.py:64
  68.9 1.5 %collective-permute-start.17 = (bf16[96,96]{1,0:T(8,128)(2,1)S(1)}, bf16[96,96]{1,0:T(8,128)(2,1)S(1)}, u32[]{:S(2)}, u32[]{:S(2)}) collective-permute-start(bf16[96,96]{1,0:T(8,128)(2,1)S(1)} %get-tuple-element.65), channel_id=1, source_target_pairs={{0,16},{8,24},{16,0},{24,8},{1,17},{9,25},{17,1},{25,9},{2,18},{10... | collective-permute-start | bytes 55304 | tf_op jit(solution)/shard_map/ppermute | solution.py:438
  70.4 2.4 %collective-permute-done.17.refs_2_ = bf16[96,96]{1,0:T(8,128)(2,1)S(1)} collective-permute-done((bf16[96,96]{1,0:T(8,128)(2,1)S(1)}, bf16[96,96]{1,0:T(8,128)(2,1)S(1)}, u32[]{:S(2)}, u32[]{:S(2)}) %collective-permute-start.17) | collective-permute-done | bytes 18464 | tf_op jit(solution)/shard_map/ppermute | solution.py:438
  73.9 1.6 %shard_map.104 = (bf16[128,384]{1,0:T(8,128)(2,1)S(1)}, bf16[128,384]{1,0:T(8,128)(2,1)S(1)}, bf16[128,384]{1,0:T(8,128)(2,1)S(1)}, bf16[128,384]{1,0:T(8,128)(2,1)S(1)}) custom-call(s32[1]{0:T(128)} %bitcast.own_out.member.own_in, bf16[256,256]{1,0:T(8,128)(2,1)S(1)} %copy-done.5, bf16[8,128,192]{2,1,0:T(8,128)(2,1)S(1)} %get-tuple-element.67.grad_pre, ...), custom_call_target="tpu_custom_call" | custom-call | tf_op jit(solution)/shard_map/pallas_call | solution.py:64
  77.4 1.9 %collective-permute-start.19 = (bf16[1,96,96]{2,1,0:T(8,128)(2,1)S(1)}, bf16[1,96,96]{2,1,0:T(8,128)(2,1)S(1)}, u32[]{:S(2)}, u32[]{:S(2)}) collective-permute-start(bf16[1,96,96]{2,1,0:T(8,128)(2,1)S(1)} %shard_map.102.first.rest_0_), channel_id=1, source_target_pairs={{0,2},{1,3},{2,0},{3,1},{4,6},{5,7},{6,4},{7,5},{8,10},{9,11},{10,... | collective-permute-start | bytes 55304 | tf_op jit(solution)/shard_map/ppermute | solution.py:578
  79.3 1.9 %collective-permute-done.19.second = bf16[1,96,96]{2,1,0:T(8,128)(2,1)S(1)} collective-permute-done((bf16[1,96,96]{2,1,0:T(8,128)(2,1)S(1)}, bf16[1,96,96]{2,1,0:T(8,128)(2,1)S(1)}, u32[]{:S(2)}, u32[]{:S(2)}) %collective-permute-start.19) | collective-permute-done | bytes 18464 | tf_op jit(solution)/shard_map/ppermute | solution.py:578
  81.2 2.9 %collective-permute-start.20 = (bf16[2,96,96]{2,1,0:T(8,128)(2,1)S(1)}, bf16[2,96,96]{2,1,0:T(8,128)(2,1)S(1)}, u32[]{:S(2)}, u32[]{:S(2)}) collective-permute-start(bf16[2,96,96]{2,1,0:T(8,128)(2,1)S(1)} %shard_map.103.first), channel_id=1, source_target_pairs={{0,4},{1,5},{2,6},{3,7},{4,0},{5,1},{6,2},{7,3},{8,12},{9,13},{10,... | collective-permute-start | bytes 110600 | tf_op jit(solution)/shard_map/ppermute | solution.py:578
  84.2 1.3 %shard_map.105.rest_0_ = bf16[8,128,384]{2,1,0:T(8,128)(2,1)} custom-call(s32[1]{0:T(128)} %bitcast.own_out.member.own_in, bf16[256,512]{1,0:T(8,128)(2,1)S(1)} %copy-done.1, bf16[128,384]{1,0:T(8,128)(2,1)S(1)} %get-tuple-element.69.rest_0_, bf16[128,384]{1,0:T(8,128)(2,1)S(1)} %collective-permute-done.21.rest_1_, ...), custom_call_target="tpu_custom_call" | custom-call | tf_op jit(solution)/shard_map/pallas_call | solution.py:64
  85.4 1.3 %collective-permute-done.20.second = bf16[2,96,96]{2,1,0:T(8,128)(2,1)S(1)} collective-permute-done((bf16[2,96,96]{2,1,0:T(8,128)(2,1)S(1)}, bf16[2,96,96]{2,1,0:T(8,128)(2,1)S(1)}, u32[]{:S(2)}, u32[]{:S(2)}) %collective-permute-start.20) | collective-permute-done | bytes 36896 | tf_op jit(solution)/shard_map/ppermute | solution.py:578
  86.8 6.2 %all-to-all-start.2 = ((bf16[8,128,384]{2,1,0:T(8,128)(2,1)}), bf16[8,128,384]{2,1,0:T(8,128)(2,1)S(1)}, u32[]{:S(2)}, u32[]{:S(2)}) async-start(bf16[8,128,384]{2,1,0:T(8,128)(2,1)} %get-tuple-element.73), calls=%async_computation.2 | async-start | bytes 1572864 | tf_op jit(solution)/shard_map/all_to_all | solution.py:433
  92.9 2.0 %collective-permute-start.24 = (bf16[4,96,96]{2,1,0:T(8,128)(2,1)S(1)}, bf16[4,96,96]{2,1,0:T(8,128)(2,1)S(1)}, u32[]{:S(2)}, u32[]{:S(2)}) collective-permute-start(bf16[4,96,96]{2,1,0:T(8,128)(2,1)S(1)} %get-tuple-element.74.near), channel_id=1, source_target_pairs={{0,1},{1,0},{2,3},{3,2},{4,5},{5,4},{6,7},{7,6},{8,9},{9,8},{10,11... | collective-permute-start | bytes 221192 | tf_op jit(solution)/shard_map/ppermute | solution.py:593
  96.1 5.6 %collective-permute-done.24.other = bf16[4,96,96]{2,1,0:T(8,128)(2,1)S(1)} collective-permute-done((bf16[4,96,96]{2,1,0:T(8,128)(2,1)S(1)}, bf16[4,96,96]{2,1,0:T(8,128)(2,1)S(1)}, u32[]{:S(2)}, u32[]{:S(2)}) %collective-permute-start.24) | collective-permute-done | bytes 73760 | tf_op jit(solution)/shard_map/ppermute | solution.py:593
  103.7 4.8 %collective-permute-done.26.rest_2_ = bf16[8,96,96]{2,1,0:T(8,128)(2,1)S(1)} collective-permute-done((bf16[8,96,96]{2,1,0:T(8,128)(2,1)S(1)}, bf16[8,96,96]{2,1,0:T(8,128)(2,1)S(1)}, u32[]{:S(2)}, u32[]{:S(2)}) %collective-permute-start.26) | collective-permute-done | bytes 147488 | tf_op jit(solution)/shard_map/ppermute | solution.py:601
  108.6 3.1 %all-to-all-done.2.packed = bf16[8,128,384]{2,1,0:T(8,128)(2,1)S(1)} async-done(((bf16[8,128,384]{2,1,0:T(8,128)(2,1)}), bf16[8,128,384]{2,1,0:T(8,128)(2,1)S(1)}, u32[]{:S(2)}, u32[]{:S(2)}) %all-to-all-start.2) | async-done | bytes 786464 | tf_op jit(solution)/shard_map/all_to_all | solution.py:433
  111.7 1.7 %shard_map.108 = (bf16[32,16,768]{2,1,0:T(8,128)(2,1)}, f32[2,8,96,96]{3,2,1,0:T(8,128)}, f32[2,8,96,96]{3,2,1,0:T(8,128)}) custom-call(s32[1]{0:T(128)} %bitcast.4.lat_own, bf16[8,128,384]{2,1,0:T(8,128)(2,1)S(1)} %all-to-all-done.2.packed, bf16[32,16,768]{2,1,0:T(8,128)(2,1)S(1)} %copy-done.2, bf16[8,96,96]{2,1,0:T(8,128)(2,1)S(1)} %shard_map.107.rest_0_, ...), custom_call_target="tpu_custom_call" | custom-call | tf_op jit(solution)/shard_map/pallas_call | solution.py:64
  (58 shorter events, 13.8 us)
Async XLA Ops:
  2.3 8.9 %collective-permute-start = (bf16[128,384]{1,0:T(8,128)(2,1)S(1)}, bf16[128,384]{1,0:T(8,128)(2,1)S(1)}, u32[]{:S(2)}, u32[]{:S(2)}) collective-permute-start(bf16[128,384]{1,0:T(8,128)(2,1)S(1)} %get-tuple-element.42), channel_id=1, source_target_pairs={{0,1},{1,0},{2,3},{3,2},{4,5},{5,4},{6,7},{7,6},{8,9},{9,8},{10,11... | collective-permute-start | bytes 294920 | tf_op jit(solution)/shard_map/ppermute | solution.py:438
  5.4 9.5 %collective-permute-start.1 = (bf16[128,384]{1,0:T(8,128)(2,1)S(1)}, bf16[128,384]{1,0:T(8,128)(2,1)S(1)}, u32[]{:S(2)}, u32[]{:S(2)}) collective-permute-start(bf16[128,384]{1,0:T(8,128)(2,1)S(1)} %get-tuple-element.43), channel_id=1, source_target_pairs={{0,2},{1,3},{2,0},{3,1},{4,6},{5,7},{6,4},{7,5},{8,10},{9,11},{10,... | collective-permute-start | bytes 294920 | tf_op jit(solution)/shard_map/ppermute | solution.py:438
  7.0 10.5 %collective-permute-start.2 = (bf16[128,384]{1,0:T(8,128)(2,1)S(1)}, bf16[128,384]{1,0:T(8,128)(2,1)S(1)}, u32[]{:S(2)}, u32[]{:S(2)}) collective-permute-start(bf16[128,384]{1,0:T(8,128)(2,1)S(1)} %get-tuple-element.44), channel_id=1, source_target_pairs={{0,3},{1,2},{2,1},{3,0},{4,7},{5,6},{6,5},{7,4},{8,11},{9,10},{10,... | collective-permute-start | bytes 294920 | tf_op jit(solution)/shard_map/ppermute | solution.py:438
  7.0 10.5 %collective-permute-start.3 = (bf16[128,384]{1,0:T(8,128)(2,1)S(1)}, bf16[128,384]{1,0:T(8,128)(2,1)S(1)}, u32[]{:S(2)}, u32[]{:S(2)}) collective-permute-start(bf16[128,384]{1,0:T(8,128)(2,1)S(1)} %get-tuple-element.45), channel_id=1, source_target_pairs={{0,4},{1,5},{2,6},{3,7},{4,0},{5,1},{6,2},{7,3},{8,12},{9,13},{10,... | collective-permute-start | bytes 294920 | tf_op jit(solution)/shard_map/ppermute | solution.py:438
  9.9 15.2 %collective-permute-start.4 = (bf16[128,384]{1,0:T(8,128)(2,1)S(1)}, bf16[128,384]{1,0:T(8,128)(2,1)S(1)}, u32[]{:S(2)}, u32[]{:S(2)}) collective-permute-start(bf16[128,384]{1,0:T(8,128)(2,1)S(1)} %get-tuple-element.46), channel_id=1, source_target_pairs={{0,5},{1,4},{2,7},{3,6},{4,1},{5,0},{6,3},{7,2},{8,13},{9,12},{10,... | collective-permute-start | bytes 294920 | tf_op jit(solution)/shard_map/ppermute | solution.py:438
  11.2 13.9 %collective-permute-start.5 = (bf16[128,384]{1,0:T(8,128)(2,1)S(1)}, bf16[128,384]{1,0:T(8,128)(2,1)S(1)}, u32[]{:S(2)}, u32[]{:S(2)}) collective-permute-start(bf16[128,384]{1,0:T(8,128)(2,1)S(1)} %get-tuple-element.47), channel_id=1, source_target_pairs={{0,6},{1,7},{2,4},{3,5},{4,2},{5,3},{6,0},{7,1},{8,14},{9,15},{10,... | collective-permute-start | bytes 294920 | tf_op jit(solution)/shard_map/ppermute | solution.py:438
  14.8 10.3 %collective-permute-start.6 = (bf16[128,384]{1,0:T(8,128)(2,1)S(1)}, bf16[128,384]{1,0:T(8,128)(2,1)S(1)}, u32[]{:S(2)}, u32[]{:S(2)}) collective-permute-start(bf16[128,384]{1,0:T(8,128)(2,1)S(1)} %get-tuple-element.48), channel_id=1, source_target_pairs={{0,7},{1,6},{2,5},{3,4},{4,3},{5,2},{6,1},{7,0},{8,15},{9,14},{10,... | collective-permute-start | bytes 294920 | tf_op jit(solution)/shard_map/ppermute | solution.py:438
  25.7 26.2 %all-to-all-start = ((bf16[8,128,384]{2,1,0:T(8,128)(2,1)}), bf16[8,128,384]{2,1,0:T(8,128)(2,1)S(1)}, u32[]{:S(2)}, u32[]{:S(2)}) async-start(bf16[8,128,384]{2,1,0:T(8,128)(2,1)} %shard_map.97), calls=%async_computation | async-start | bytes 1572864 | tf_op jit(solution)/shard_map/all_to_all | solution.py:433
  32.3 1.9 %collective-permute-start.7 = (bf16[128,384]{1,0:T(8,128)(2,1)S(1)}, bf16[128,384]{1,0:T(8,128)(2,1)S(1)}, u32[]{:S(2)}, u32[]{:S(2)}) collective-permute-start(bf16[128,384]{1,0:T(8,128)(2,1)S(1)} %get-tuple-element.50), channel_id=1, source_target_pairs={{0,8},{1,9},{2,10},{3,11},{4,12},{5,13},{6,14},{7,15},{8,0},{9,1},... | collective-permute-start | bytes 294920 | tf_op jit(solution)/shard_map/ppermute | solution.py:438
  32.3 5.7 %collective-permute-start.8 = (bf16[128,384]{1,0:T(8,128)(2,1)S(1)}, bf16[128,384]{1,0:T(8,128)(2,1)S(1)}, u32[]{:S(2)}, u32[]{:S(2)}) collective-permute-start(bf16[128,384]{1,0:T(8,128)(2,1)S(1)} %get-tuple-element.51), channel_id=1, source_target_pairs={{0,16},{1,17},{2,18},{3,19},{4,20},{5,21},{6,22},{7,23},{8,24},{9,... | collective-permute-start | bytes 294920 | tf_op jit(solution)/shard_map/ppermute | solution.py:438
  33.9 5.3 %collective-permute-start.9 = (bf16[128,384]{1,0:T(8,128)(2,1)S(1)}, bf16[128,384]{1,0:T(8,128)(2,1)S(1)}, u32[]{:S(2)}, u32[]{:S(2)}) collective-permute-start(bf16[128,384]{1,0:T(8,128)(2,1)S(1)} %get-tuple-element.52), channel_id=1, source_target_pairs={{0,24},{1,25},{2,26},{3,27},{4,28},{5,29},{6,30},{7,31},{8,16},{9,... | collective-permute-start | bytes 294920 | tf_op jit(solution)/shard_map/ppermute | solution.py:438
  42.9 9.5 %collective-permute-start.10 = (bf16[128,384]{1,0:T(8,128)(2,1)S(1)}, bf16[128,384]{1,0:T(8,128)(2,1)S(1)}, u32[]{:S(2)}, u32[]{:S(2)}) collective-permute-start(bf16[128,384]{1,0:T(8,128)(2,1)S(1)} %get-tuple-element.54), channel_id=1, source_target_pairs={{0,8},{1,9},{2,10},{3,11},{4,12},{5,13},{6,14},{7,15},{8,0},{9,1},... | collective-permute-start | bytes 294920 | tf_op jit(solution)/shard_map/ppermute | solution.py:438
  43.5 8.9 %collective-permute-start.11 = (bf16[128,384]{1,0:T(8,128)(2,1)S(1)}, bf16[128,384]{1,0:T(8,128)(2,1)S(1)}, u32[]{:S(2)}, u32[]{:S(2)}) collective-permute-start(bf16[128,384]{1,0:T(8,128)(2,1)S(1)} %get-tuple-element.55), channel_id=1, source_target_pairs={{0,16},{1,17},{2,18},{3,19},{4,20},{5,21},{6,22},{7,23},{8,24},{9,... | collective-permute-start | bytes 294920 | tf_op jit(solution)/shard_map/ppermute | solution.py:438
  45.0 7.4 %collective-permute-start.12 = (bf16[128,384]{1,0:T(8,128)(2,1)S(1)}, bf16[128,384]{1,0:T(8,128)(2,1)S(1)}, u32[]{:S(2)}, u32[]{:S(2)}) collective-permute-start(bf16[128,384]{1,0:T(8,128)(2,1)S(1)} %get-tuple-element.56), channel_id=1, source_target_pairs={{0,24},{1,25},{2,26},{3,27},{4,28},{5,29},{6,30},{7,31},{8,16},{9,... | collective-permute-start | bytes 294920 | tf_op jit(solution)/shard_map/ppermute | solution.py:438
  53.7 33.1 %all-to-all-start.1 = ((bf16[8,128,384]{2,1,0:T(8,128)(2,1)}), bf16[8,128,384]{2,1,0:T(8,128)(2,1)S(1)}, u32[]{:S(2)}, u32[]{:S(2)}) async-start(bf16[8,128,384]{2,1,0:T(8,128)(2,1)} %shard_map.99), calls=%async_computation.1 | async-start | bytes 1572864 | tf_op jit(solution)/shard_map/all_to_all | solution.py:433
  57.3 1.9 %collective-permute-start.13 = (bf16[128,384]{1,0:T(8,128)(2,1)S(1)}, bf16[128,384]{1,0:T(8,128)(2,1)S(1)}, u32[]{:S(2)}, u32[]{:S(2)}) collective-permute-start(bf16[128,384]{1,0:T(8,128)(2,1)S(1)} %get-tuple-element.59), channel_id=1, source_target_pairs={{0,8},{1,9},{2,10},{3,11},{4,12},{5,13},{6,14},{7,15},{8,0},{9,1},... | collective-permute-start | bytes 294920 | tf_op jit(solution)/shard_map/ppermute | solution.py:438
  57.4 5.7 %collective-permute-start.14 = (bf16[128,384]{1,0:T(8,128)(2,1)S(1)}, bf16[128,384]{1,0:T(8,128)(2,1)S(1)}, u32[]{:S(2)}, u32[]{:S(2)}) collective-permute-start(bf16[128,384]{1,0:T(8,128)(2,1)S(1)} %get-tuple-element.60), channel_id=1, source_target_pairs={{0,16},{1,17},{2,18},{3,19},{4,20},{5,21},{6,22},{7,23},{8,24},{9,... | collective-permute-start | bytes 294920 | tf_op jit(solution)/shard_map/ppermute | solution.py:438
  58.9 5.4 %collective-permute-start.15 = (bf16[128,384]{1,0:T(8,128)(2,1)S(1)}, bf16[128,384]{1,0:T(8,128)(2,1)S(1)}, u32[]{:S(2)}, u32[]{:S(2)}) collective-permute-start(bf16[128,384]{1,0:T(8,128)(2,1)S(1)} %get-tuple-element.61), channel_id=1, source_target_pairs={{0,24},{1,25},{2,26},{3,27},{4,28},{5,29},{6,30},{7,31},{8,16},{9,... | collective-permute-start | bytes 294920 | tf_op jit(solution)/shard_map/ppermute | solution.py:438
  68.3 2.1 %collective-permute-start.16 = (bf16[96,96]{1,0:T(8,128)(2,1)S(1)}, bf16[96,96]{1,0:T(8,128)(2,1)S(1)}, u32[]{:S(2)}, u32[]{:S(2)}) collective-permute-start(bf16[96,96]{1,0:T(8,128)(2,1)S(1)} %get-tuple-element.64), channel_id=1, source_target_pairs={{0,8},{8,0},{16,24},{24,16},{1,9},{9,1},{17,25},{25,17},{2,10},{10... | collective-permute-start | bytes 55304 | tf_op jit(solution)/shard_map/ppermute | solution.py:438
  68.9 3.8 %collective-permute-start.17 = (bf16[96,96]{1,0:T(8,128)(2,1)S(1)}, bf16[96,96]{1,0:T(8,128)(2,1)S(1)}, u32[]{:S(2)}, u32[]{:S(2)}) collective-permute-start(bf16[96,96]{1,0:T(8,128)(2,1)S(1)} %get-tuple-element.65), channel_id=1, source_target_pairs={{0,16},{8,24},{16,0},{24,8},{1,17},{9,25},{17,1},{25,9},{2,18},{10... | collective-permute-start | bytes 55304 | tf_op jit(solution)/shard_map/ppermute | solution.py:438
  70.4 3.5 %collective-permute-start.18 = (bf16[96,96]{1,0:T(8,128)(2,1)S(1)}, bf16[96,96]{1,0:T(8,128)(2,1)S(1)}, u32[]{:S(2)}, u32[]{:S(2)}) collective-permute-start(bf16[96,96]{1,0:T(8,128)(2,1)S(1)} %get-tuple-element.66), channel_id=1, source_target_pairs={{0,24},{8,16},{16,8},{24,0},{1,25},{9,17},{17,9},{25,1},{2,26},{10... | collective-permute-start | bytes 55304 | tf_op jit(solution)/shard_map/ppermute | solution.py:438
  75.5 8.7 %collective-permute-start.21 = (bf16[128,384]{1,0:T(8,128)(2,1)S(1)}, bf16[128,384]{1,0:T(8,128)(2,1)S(1)}, u32[]{:S(2)}, u32[]{:S(2)}) collective-permute-start(bf16[128,384]{1,0:T(8,128)(2,1)S(1)} %get-tuple-element.70), channel_id=1, source_target_pairs={{0,8},{1,9},{2,10},{3,11},{4,12},{5,13},{6,14},{7,15},{8,0},{9,1},... | collective-permute-start | bytes 294920 | tf_op jit(solution)/shard_map/ppermute | solution.py:438
  75.6 8.6 %collective-permute-start.22 = (bf16[128,384]{1,0:T(8,128)(2,1)S(1)}, bf16[128,384]{1,0:T(8,128)(2,1)S(1)}, u32[]{:S(2)}, u32[]{:S(2)}) collective-permute-start(bf16[128,384]{1,0:T(8,128)(2,1)S(1)} %get-tuple-element.71), channel_id=1, source_target_pairs={{0,16},{1,17},{2,18},{3,19},{4,20},{5,21},{6,22},{7,23},{8,24},{9,... | collective-permute-start | bytes 294920 | tf_op jit(solution)/shard_map/ppermute | solution.py:438
  76.5 7.6 %collective-permute-start.23 = (bf16[128,384]{1,0:T(8,128)(2,1)S(1)}, bf16[128,384]{1,0:T(8,128)(2,1)S(1)}, u32[]{:S(2)}, u32[]{:S(2)}) collective-permute-start(bf16[128,384]{1,0:T(8,128)(2,1)S(1)} %get-tuple-element.72), channel_id=1, source_target_pairs={{0,24},{1,25},{2,26},{3,27},{4,28},{5,29},{6,30},{7,31},{8,16},{9,... | collective-permute-start | bytes 294920 | tf_op jit(solution)/shard_map/ppermute | solution.py:438
  77.4 3.8 %collective-permute-start.19 = (bf16[1,96,96]{2,1,0:T(8,128)(2,1)S(1)}, bf16[1,96,96]{2,1,0:T(8,128)(2,1)S(1)}, u32[]{:S(2)}, u32[]{:S(2)}) collective-permute-start(bf16[1,96,96]{2,1,0:T(8,128)(2,1)S(1)} %shard_map.102.first.rest_0_), channel_id=1, source_target_pairs={{0,2},{1,3},{2,0},{3,1},{4,6},{5,7},{6,4},{7,5},{8,10},{9,11},{10,... | collective-permute-start | bytes 55304 | tf_op jit(solution)/shard_map/ppermute | solution.py:578
  81.2 5.5 %collective-permute-start.20 = (bf16[2,96,96]{2,1,0:T(8,128)(2,1)S(1)}, bf16[2,96,96]{2,1,0:T(8,128)(2,1)S(1)}, u32[]{:S(2)}, u32[]{:S(2)}) collective-permute-start(bf16[2,96,96]{2,1,0:T(8,128)(2,1)S(1)} %shard_map.103.first), channel_id=1, source_target_pairs={{0,4},{1,5},{2,6},{3,7},{4,0},{5,1},{6,2},{7,3},{8,12},{9,13},{10,... | collective-permute-start | bytes 110600 | tf_op jit(solution)/shard_map/ppermute | solution.py:578
  86.8 24.9 %all-to-all-start.2 = ((bf16[8,128,384]{2,1,0:T(8,128)(2,1)}), bf16[8,128,384]{2,1,0:T(8,128)(2,1)S(1)}, u32[]{:S(2)}, u32[]{:S(2)}) async-start(bf16[8,128,384]{2,1,0:T(8,128)(2,1)} %get-tuple-element.73), calls=%async_computation.2 | async-start | bytes 1572864 | tf_op jit(solution)/shard_map/all_to_all | solution.py:433
  92.9 8.7 %collective-permute-start.24 = (bf16[4,96,96]{2,1,0:T(8,128)(2,1)S(1)}, bf16[4,96,96]{2,1,0:T(8,128)(2,1)S(1)}, u32[]{:S(2)}, u32[]{:S(2)}) collective-permute-start(bf16[4,96,96]{2,1,0:T(8,128)(2,1)S(1)} %get-tuple-element.74.near), channel_id=1, source_target_pairs={{0,1},{1,0},{2,3},{3,2},{4,5},{5,4},{6,7},{7,6},{8,9},{9,8},{10,11... | collective-permute-start | bytes 221192 | tf_op jit(solution)/shard_map/ppermute | solution.py:593
  96.1 15.6 %copy-start.2 = (bf16[32,16,768]{2,1,0:T(8,128)(2,1)S(1)}, bf16[32,16,768]{2,1,0:T(8,128)(2,1)}, u32[]{:S(2)}) copy-start(bf16[32,16,768]{2,1,0:T(8,128)(2,1)} %base.3) | copy-start | bytes 2359300
  102.8 5.7 %collective-permute-start.26 = (bf16[8,96,96]{2,1,0:T(8,128)(2,1)S(1)}, bf16[8,96,96]{2,1,0:T(8,128)(2,1)S(1)}, u32[]{:S(2)}, u32[]{:S(2)}) collective-permute-start(bf16[8,96,96]{2,1,0:T(8,128)(2,1)S(1)} %shard_map.107.rest_0_), channel_id=1, source_target_pairs={{0,16},{8,24},{16,0},{24,8},{1,17},{9,25},{17,1},{25,9},{2,18},{10... | collective-permute-start | bytes 442376 | tf_op jit(solution)/shard_map/ppermute | solution.py:601
  103.7 4.8 %collective-permute-start.25 = (bf16[8,96,96]{2,1,0:T(8,128)(2,1)S(1)}, bf16[8,96,96]{2,1,0:T(8,128)(2,1)S(1)}, u32[]{:S(2)}, u32[]{:S(2)}) collective-permute-start(bf16[8,96,96]{2,1,0:T(8,128)(2,1)S(1)} %shard_map.107.rest_0_), channel_id=1, source_target_pairs={{0,8},{8,0},{16,24},{24,16},{1,9},{9,1},{17,25},{25,17},{2,10},{10... | collective-permute-start | bytes 442376 | tf_op jit(solution)/shard_map/ppermute | solution.py:601
  108.6 3.1 %collective-permute-start.27 = (bf16[8,96,96]{2,1,0:T(8,128)(2,1)S(1)}, bf16[8,96,96]{2,1,0:T(8,128)(2,1)S(1)}, u32[]{:S(2)}, u32[]{:S(2)}) collective-permute-start(bf16[8,96,96]{2,1,0:T(8,128)(2,1)S(1)} %collective-permute-done.26.rest_2_), channel_id=1, source_target_pairs={{0,8},{8,0},{16,24},{24,16},{1,9},{9,1},{17,25},{25,17},{2,10},{10... | collective-permute-start | bytes 442376 | tf_op jit(solution)/shard_map/ppermute | solution.py:601
  (5 other events, 34.0 us)
